TPU v7x, 32 devices: a whole 2x2x4 slice. The times are simulated.
32 devices in a mesh: pipe: 4 (over y, core), win: 4 (over z), head: 2 (over x).
Axes of the slice: x: 2, y: 2, z: 4, core: 2. Of those that a mesh axis runs over, the one named last changes fastest.
Arguments:
- stream: bfloat16 [8, 128, 2048], P('head', 'win'), may hold values from -16 to 16
- score_scale: float32 [4, 2048], P('pipe'), may hold values from -12 to 12
- value_weight: bfloat16 [4, 2048, 2048], P('pipe', None, 'head'), may hold values from -0.125 to 0.125
- out_weight: bfloat16 [4, 2048, 2048], P('pipe', 'head'), may hold values from -0.25 to 0.25
Outputs:
- sections: bfloat16 [4, 8, 128, 2048], P('pipe', None, 'win', 'head')
All inputs are finite; a program needn't handle non-finite values.
Results may differ from a plain program's by a relative error of at most 0.03.
Values may be sent and summed in bfloat16 or wider, within the bound.
No kernel may reach another device: no remote copies, remote signals or barrier semaphores. Data moves between devices by JAX's collectives and lax.ppermute only.
A program may use at most 64 MiB of HBM per device.

v0:
```python
import math

import jax
import jax.numpy as jnp
from jax import lax
from jax.sharding import PartitionSpec as P

HEAD_DIM = 128
WIN = 32


EPSILON = 1e-06


def from_behind(value, axis, steps):
    count = lax.axis_size(axis)
    pairs = [(source, (source + steps) % count) for source in range(count)]
    return lax.ppermute(value, axis, pairs)


def from_behind_2(value, axis, steps):
    count = lax.axis_size(axis)
    leading, last = (max(0, -steps), min(count, count - steps))
    return lax.ppermute(value, axis, [(source, source + steps) for source in range(leading, last)])


def to_windows(tensor, window_count, heads_local):
    row_count = tensor.shape[0]
    shaped = tensor.reshape(row_count, window_count, WIN, heads_local, HEAD_DIM)
    shaped = shaped.transpose(1, 3, 0, 2, 4)
    return shaped.reshape(window_count * heads_local, row_count * WIN, HEAD_DIM)


def attend(framed, complete, query_scale, value_cols):
    row_count, col_count, channels = framed.shape
    heads_local = channels // HEAD_DIM
    window_count = col_count // WIN
    inv_root = 1.0 / math.sqrt(HEAD_DIM)
    queries = (framed.astype(jnp.float32) * query_scale).astype(jnp.bfloat16)
    values = jnp.dot(
        complete.reshape(row_count * col_count, complete.shape[2]),
        value_cols,
        preferred_element_type=jnp.float32,
    )
    values = values.astype(jnp.bfloat16).reshape(row_count, col_count, channels)
    windowed_queries = to_windows(queries, window_count, heads_local)
    windowed_keys = to_windows(framed, window_count, heads_local)
    windowed_values = to_windows(values, window_count, heads_local)
    scores = (
        jnp.einsum(
            "foa,fxa->fox", windowed_queries, windowed_keys, preferred_element_type=jnp.float32
        )
        * inv_root
    )
    score_maximum = jnp.max(scores, axis=2, keepdims=True)
    exp_scores = jnp.exp(scores - score_maximum)
    attention_probabilities = (exp_scores / jnp.sum(exp_scores, axis=2, keepdims=True)).astype(
        jnp.bfloat16
    )
    attended = jnp.einsum(
        "eom,eml->eol", attention_probabilities, windowed_values, preferred_element_type=jnp.float32
    ).astype(jnp.bfloat16)
    attended = attended.reshape(window_count, heads_local, row_count, WIN, HEAD_DIM)
    return attended.transpose(2, 0, 3, 1, 4).reshape(row_count, col_count, channels)


def per_device(stream, score_scale, value_weight, out_weight):
    gathered = lax.all_to_all(stream, "head", split_axis=2, concat_axis=0, tiled=True)
    row_count, col_count, channels = gathered.shape
    half_win = WIN // 2
    segment_id = lax.axis_index("pipe")
    sections = lax.axis_size("pipe")
    width_all = channels * lax.axis_size("head")
    first_chan = lax.axis_index("head") * channels
    query_scale = lax.dynamic_slice_in_dim(score_scale[0], first_chan, channels, 0)
    value_cols = value_weight[0]
    out_rows = out_weight[0]
    current = gathered
    recorded = jnp.zeros_like(gathered)
    for section in range(sections):
        active = segment_id == section
        shifted = section % 2 == 1
        current_f = current.astype(jnp.float32)
        partial_value = jnp.sum(current_f * current_f, axis=2)
        square_sums = lax.psum(partial_value, "head")
        inverse = lax.rsqrt(square_sums / width_all + EPSILON)
        normed = (current_f * inverse[:, :, None]).astype(jnp.bfloat16)
        framed = normed
        if shifted:
            next_section = from_behind(normed[:, :half_win], "win", -1)
            framed = jnp.concatenate([normed[:, half_win:], next_section], axis=1)
        complete = lax.all_gather(framed, "head", axis=2, tiled=True)
        attended = lax.cond(
            active,
            lambda pair: attend(pair[0], pair[1], query_scale, value_cols),
            lambda pair: jnp.zeros_like(pair[0]),
            (framed, complete),
        )
        if shifted:
            tail_cols = from_behind(attended[:, col_count - half_win :], "win", 1)
            attended = jnp.concatenate([tail_cols, attended[:, : col_count - half_win]], axis=1)
        term = lax.cond(
            active,
            lambda tensor: jnp.dot(
                tensor.reshape(row_count * col_count, channels),
                out_rows,
                preferred_element_type=jnp.float32,
            ).reshape(row_count, col_count, width_all),
            lambda tensor: jnp.zeros((row_count, col_count, width_all), jnp.float32),
            attended,
        )
        mixture = lax.psum_scatter(
            term.astype(jnp.bfloat16), "head", scatter_dimension=2, tiled=True
        ).astype(jnp.float32)
        updated = (current_f + mixture).astype(jnp.bfloat16)
        recorded = jnp.where(active, updated, recorded)
        if section + 1 < sections:
            current = from_behind_2(updated, "pipe", 1)
    return recorded[None]


def solution(mesh):
    placed = (
        P("head", "win", None),
        P("pipe", None),
        P("pipe", None, "head"),
        P("pipe", "head", None),
    )
    return jax.shard_map(
        per_device,
        mesh=mesh,
        in_specs=placed,
        out_specs=P("pipe", None, "win", "head"),
        check_vma=False,
    )
```

profile of v0, /device:TPU:5, one launch (start us, length us, event | category | flops | bytes accessed | tf_op | source)
XLA Modules:
  0.0 350.6 jit_solution(10476076642061034333)
XLA Ops:
  11.5 9.6 %all_to_all.4 = bf16[2,2,65536]{2,1,0:T(2,128)(2,1)S(1)} all-to-all(bf16[2,2,65536]{2,1,0:T(2,128)(2,1)S(1)} %reshape.154), channel_id=1, replica_groups=mesh['pipe'=4,'win'=4,'head'=2] {'head'}, dimensions={0} | all-to-all | bytes 1048576 | tf_op jit(solution)/shard_map/all_to_all | solution.py:68
  25.7 3.5 copy.70
  29.4 3.8 %psum.28 = f32[8,32]{1,0:T(8,128)S(1)} all-reduce(f32[8,32]{1,0:T(8,128)S(1)} %bitcast.230), channel_id=1, replica_groups=mesh['pipe'=4,'win'=4,'head'=2] {'head'}, use_global_device_ids=true, to_apply=%region_1.0 | all-reduce | flops 256 | bytes 2048 | tf_op jit(solution)/shard_map/psum | solution.py:85
  34.2 23.8 %all-gather.5.cloned.1.call-done = bf16[8,32,2048]{2,1,0:T(8,128)(2,1)} async-done(((bf16[8,32,1024]{2,1,0:T(8,128)(2,1)}), bf16[8,32,2048]{2,1,0:T(8,128)(2,1)}) %all-gather.5.cloned.1.call-update) | async-done | bytes 1048592 | tf_op jit(solution)/shard_map/all_gather | solution.py:92
  59.3 33.0 %reduce-scatter.5.cloned.1.call-done = bf16[8,32,1024]{2,1,0:T(8,128)(2,1)} async-done(((bf16[8,32,2048]{2,1,0:T(8,128)(2,1)}), bf16[8,32,1024]{2,1,0:T(8,128)(2,1)}) %reduce-scatter.5.cloned.1.call-update) | async-done | bytes 524304 | tf_op jit(solution)/shard_map/reduce_scatter | solution.py:112
  97.7 4.1 %psum.29 = f32[8,32]{1,0:T(8,128)S(1)} all-reduce(f32[8,32]{1,0:T(8,128)S(1)} %fusion.36), channel_id=1, replica_groups=mesh['pipe'=4,'win'=4,'head'=2] {'head'}, use_global_device_ids=true, to_apply=%region_10.11 | all-reduce | flops 256 | bytes 2048 | tf_op jit(solution)/shard_map/psum | solution.py:85
  102.0 3.1 collective-permute-start.1
  105.1 3.3 collective-permute-done.1
  109.3 30.6 %all-gather.7.cloned.1.call-done = bf16[8,32,2048]{2,1,0:T(8,128)(2,1)} async-done(((bf16[8,32,1024]{2,1,0:T(8,128)(2,1)}), bf16[8,32,2048]{2,1,0:T(8,128)(2,1)}) %all-gather.7.cloned.1.call-update) | async-done | bytes 1048592 | tf_op jit(solution)/shard_map/all_gather | solution.py:92
  141.5 7.8 %collective-permute-done.2 = bf16[8,16,1024]{2,1,0:T(8,128)(2,1)S(1)} collective-permute-done((bf16[8,16,1024]{2,1,0:T(8,128)(2,1)S(1)}, bf16[8,16,1024]{2,1,0:T(8,128)(2,1)S(1)}, u32[]{:S(2)}, u32[]{:S(2)}) %collective-permute-start.2) | collective-permute-done | bytes 262176 | tf_op jit(solution)/shard_map/ppermute | solution.py:18
  150.5 28.2 %reduce-scatter.7.cloned.1.call-done = bf16[8,32,1024]{2,1,0:T(8,128)(2,1)} async-done(((bf16[8,32,2048]{2,1,0:T(8,128)(2,1)}), bf16[8,32,1024]{2,1,0:T(8,128)(2,1)}) %reduce-scatter.7.cloned.1.call-update) | async-done | bytes 524304 | tf_op jit(solution)/shard_map/reduce_scatter | solution.py:112
  184.1 4.1 %psum.30 = f32[8,32]{1,0:T(8,128)S(1)} all-reduce(f32[8,32]{1,0:T(8,128)S(1)} %fusion.39), channel_id=1, replica_groups=mesh['pipe'=4,'win'=4,'head'=2] {'head'}, use_global_device_ids=true, to_apply=%region_19.20 | all-reduce | flops 256 | bytes 2048 | tf_op jit(solution)/shard_map/psum | solution.py:85
  189.2 28.8 %all-gather.9.cloned.1.call-done = bf16[8,32,2048]{2,1,0:T(8,128)(2,1)} async-done(((bf16[8,32,1024]{2,1,0:T(8,128)(2,1)}), bf16[8,32,2048]{2,1,0:T(8,128)(2,1)}) %all-gather.9.cloned.1.call-update) | async-done | bytes 1048592 | tf_op jit(solution)/shard_map/all_gather | solution.py:92
  219.3 33.9 %reduce-scatter.9.cloned.1.call-done = bf16[8,32,1024]{2,1,0:T(8,128)(2,1)} async-done(((bf16[8,32,2048]{2,1,0:T(8,128)(2,1)}), bf16[8,32,1024]{2,1,0:T(8,128)(2,1)}) %reduce-scatter.9.cloned.1.call-update) | async-done | bytes 524304 | tf_op jit(solution)/shard_map/reduce_scatter | solution.py:112
  258.5 4.1 %psum.31 = f32[8,32]{1,0:T(8,128)S(1)} all-reduce(f32[8,32]{1,0:T(8,128)S(1)} %fusion.42), channel_id=1, replica_groups=mesh['pipe'=4,'win'=4,'head'=2] {'head'}, use_global_device_ids=true, to_apply=%region_28.29 | all-reduce | flops 256 | bytes 2048 | tf_op jit(solution)/shard_map/psum | solution.py:85
  262.9 3.1 collective-permute-start.5
  266.0 3.3 collective-permute-done.5
  270.2 30.6 %all-gather.11.cloned.1.call-done = bf16[8,32,2048]{2,1,0:T(8,128)(2,1)} async-done(((bf16[8,32,1024]{2,1,0:T(8,128)(2,1)}), bf16[8,32,2048]{2,1,0:T(8,128)(2,1)}) %all-gather.11.cloned.1.call-update) | async-done | bytes 1048592 | tf_op jit(solution)/shard_map/all_gather | solution.py:92
  300.8 10.2 %conditional.14 = (bf16[8,32,1024]{2,1,0:T(8,128)(2,1)S(1)}) conditional(s32[]{:T(128)} %convert_element_type.173, () %tuple.66, (bf16[8,32,1024]{2,1,0:T(8,128)(2,1)}, f32[1024]{0:T(1024)S(1)}, bf16[8,32,2048]{2,1,0:T(8,128)(2,1)}, bf16[2048,1024]{1,0:T(8,128)(2,1)}) %tuple.116), branch_computations={%region_29.30_spmd, %region_30.33_spmd} | conditional | flops 1346109696 | bytes 32002112 | solution.py:93
  304.5 3.8 %fusion.29 = bf16[32,8,8,128]{3,1,2,0:T(8,128)(2,1)S(1)} fusion(bf16[256,2048]{1,0:T(8,128)(2,1)} %bitcast.240, bf16[2048,1024]{1,0:T(8,128)(2,1)} %get-tuple-element.98), kind=kOutput, calls=%fused_computation.49 | convolution fusion | flops 1074003968 | bytes 5767168 | tf_op jit(solution)/shard_map/cond/branch_1_fun/dot_general | solution.py:40
  312.2 5.8 %collective-permute-done.6 = bf16[8,16,1024]{2,1,0:T(8,128)(2,1)S(1)} collective-permute-done((bf16[8,16,1024]{2,1,0:T(8,128)(2,1)S(1)}, bf16[8,16,1024]{2,1,0:T(8,128)(2,1)S(1)}, u32[]{:S(2)}, u32[]{:S(2)}) %collective-permute-start.6) | collective-permute-done | bytes 262176 | tf_op jit(solution)/shard_map/ppermute | solution.py:18
  318.9 3.7 %conditional.15 = (bf16[8,32,2048]{2,1,0:T(8,128)(2,1)S(1)}) conditional(s32[]{:T(128)} %convert_element_type.173, () %tuple.65, (bf16[8,32,1024]{2,1,0:T(8,128)(2,1)}, bf16[1024,2048]{1,0:T(8,128)(2,1)}) %tuple.120), branch_computations={%region_33.34_spmd, %region_34.35_spmd} | conditional | flops 1073741824 | bytes 5767176 | solution.py:102
  318.9 3.7 %fusion.34 = bf16[8,32,2048]{2,1,0:T(8,128)(2,1)S(1)} fusion(bf16[8,32,1024]{2,1,0:T(8,128)(2,1)} %get-tuple-element.99, bf16[1024,2048]{1,0:T(8,128)(2,1)} %get-tuple-element.100), kind=kOutput, calls=%fused_computation.54 | convolution fusion | flops 1073741824 | bytes 5767168 | tf_op jit(solution)/shard_map/cond/branch_1_fun/dot_general | solution.py:104
  323.6 18.1 %reduce-scatter.11.cloned.1.call-done = bf16[8,32,1024]{2,1,0:T(8,128)(2,1)} async-done(((bf16[8,32,2048]{2,1,0:T(8,128)(2,1)}), bf16[8,32,1024]{2,1,0:T(8,128)(2,1)}) %reduce-scatter.11.cloned.1.call-update) | async-done | bytes 524304 | tf_op jit(solution)/shard_map/reduce_scatter | solution.py:112
  (98 shorter events, 47.2 us)
Async XLA Ops:
  6.5 27.6 %copy-start = (f32[1,2048]{1,0:T(1,128)S(1)}, f32[1,2048]{1,0:T(1,128)}, u32[]{:S(2)}) copy-start(f32[1,2048]{1,0:T(1,128)} %param.21) | copy-start | bytes 24580
  6.5 51.5 %all-gather.5.cloned.1.call-start = ((), (), s32[]{:S(2)}) async-start(), calls=%async_computation.5 | async-start | bytes 1572864 | tf_op jit(solution)/shard_map/all_gather | solution.py:92
  34.1 58.1 %reduce-scatter.5.cloned.1.call-start = ((), (), s32[]{:S(2)}) async-start(), calls=%async_computation.6 | async-start | bytes 1572864 | tf_op jit(solution)/shard_map/reduce_scatter | solution.py:112
  58.3 1.0 copy-start.6
  59.3 80.7 %all-gather.7.cloned.1.call-start = ((), (), s32[]{:S(2)}) async-start(), calls=%async_computation.7 | async-start | bytes 1572864 | tf_op jit(solution)/shard_map/all_gather | solution.py:92
  93.5 4.0 %copy-start.10 = (bf16[8,32,1024]{2,1,0:T(8,128)(2,1)}, bf16[8,32,1024]{2,1,0:T(8,128)(2,1)S(1)}, u32[]{:S(2)}) copy-start(bf16[8,32,1024]{2,1,0:T(8,128)(2,1)S(1)} %fusion.46) | copy-start | bytes 1572868
  93.5 4.0 %collective-permute-start = (bf16[8,32,1024]{2,1,0:T(8,128)(2,1)S(1)}, bf16[8,32,1024]{2,1,0:T(8,128)(2,1)S(1)}, u32[]{:S(2)}, u32[]{:S(2)}) collective-permute-start(bf16[8,32,1024]{2,1,0:T(8,128)(2,1)S(1)} %fusion.46), channel_id=1, source_target_pairs={{0,8},{8,16},{16,24},{1,9},{9,17},{17,25},{2,10},{10,18},{18,26},{... | collective-permute-start | bytes 1572872 | tf_op jit(solution)/shard_map/ppermute | solution.py:24
  102.0 6.4 %collective-permute-start.1 = (bf16[8,16,1024]{2,1,0:T(8,128)(2,1)S(1)}, bf16[8,16,1024]{2,1,0:T(8,128)(2,1)S(1)}, u32[]{:S(2)}, u32[]{:S(2)}) collective-permute-start(bf16[8,16,1024]{2,1,0:T(8,128)(2,1)S(1)} %get-tuple-element.116), channel_id=1, source_target_pairs={{0,6},{2,0},{4,2},{6,4},{1,7},{3,1},{5,3},{7,5},{8,14},{10,8},{12,... | collective-permute-start | bytes 786440 | tf_op jit(solution)/shard_map/ppermute | solution.py:18
  109.3 69.4 %reduce-scatter.7.cloned.1.call-start = ((), (), s32[]{:S(2)}) async-start(), calls=%async_computation.8 | async-start | bytes 1572864 | tf_op jit(solution)/shard_map/reduce_scatter | solution.py:112
  140.2 9.0 %collective-permute-start.2 = (bf16[8,16,1024]{2,1,0:T(8,128)(2,1)S(1)}, bf16[8,16,1024]{2,1,0:T(8,128)(2,1)S(1)}, u32[]{:S(2)}, u32[]{:S(2)}) collective-permute-start(bf16[8,16,1024]{2,1,0:T(8,128)(2,1)S(1)} %get-tuple-element.113), channel_id=1, source_target_pairs={{0,2},{2,4},{4,6},{6,0},{1,3},{3,5},{5,7},{7,1},{8,10},{10,12},{12... | collective-permute-start | bytes 786440 | tf_op jit(solution)/shard_map/ppermute | solution.py:18
  150.4 67.6 %all-gather.9.cloned.1.call-start = ((), (), s32[]{:S(2)}) async-start(), calls=%async_computation.9 | async-start | bytes 1572864 | tf_op jit(solution)/shard_map/all_gather | solution.py:92
  179.9 4.0 %collective-permute-start.3 = (bf16[8,32,1024]{2,1,0:T(8,128)(2,1)S(1)}, bf16[8,32,1024]{2,1,0:T(8,128)(2,1)S(1)}, u32[]{:S(2)}, u32[]{:S(2)}) collective-permute-start(bf16[8,32,1024]{2,1,0:T(8,128)(2,1)S(1)} %fusion.38), channel_id=1, source_target_pairs={{0,8},{8,16},{16,24},{1,9},{9,17},{17,25},{2,10},{10,18},{18,26},{... | collective-permute-start | bytes 1572872 | tf_op jit(solution)/shard_map/ppermute | solution.py:24
  189.1 64.0 %reduce-scatter.9.cloned.1.call-start = ((), (), s32[]{:S(2)}) async-start(), calls=%async_computation.10 | async-start | bytes 1572864 | tf_op jit(solution)/shard_map/reduce_scatter | solution.py:112
  218.2 1.0 copy-start.8
  219.2 81.6 %all-gather.11.cloned.1.call-start = ((), (), s32[]{:S(2)}) async-start(), calls=%async_computation.11 | async-start | bytes 1572864 | tf_op jit(solution)/shard_map/all_gather | solution.py:92
  254.4 4.0 %collective-permute-start.4 = (bf16[8,32,1024]{2,1,0:T(8,128)(2,1)S(1)}, bf16[8,32,1024]{2,1,0:T(8,128)(2,1)S(1)}, u32[]{:S(2)}, u32[]{:S(2)}) collective-permute-start(bf16[8,32,1024]{2,1,0:T(8,128)(2,1)S(1)} %fusion.41), channel_id=1, source_target_pairs={{0,8},{8,16},{16,24},{1,9},{9,17},{17,25},{2,10},{10,18},{18,26},{... | collective-permute-start | bytes 1572872 | tf_op jit(solution)/shard_map/ppermute | solution.py:24
  262.9 6.4 %collective-permute-start.5 = (bf16[8,16,1024]{2,1,0:T(8,128)(2,1)S(1)}, bf16[8,16,1024]{2,1,0:T(8,128)(2,1)S(1)}, u32[]{:S(2)}, u32[]{:S(2)}) collective-permute-start(bf16[8,16,1024]{2,1,0:T(8,128)(2,1)S(1)} %get-tuple-element.112), channel_id=1, source_target_pairs={{0,6},{2,0},{4,2},{6,4},{1,7},{3,1},{5,3},{7,5},{8,14},{10,8},{12,... | collective-permute-start | bytes 786440 | tf_op jit(solution)/shard_map/ppermute | solution.py:18
  270.1 71.6 %reduce-scatter.11.cloned.1.call-start = ((), (), s32[]{:S(2)}) async-start(), calls=%async_computation.12 | async-start | bytes 1572864 | tf_op jit(solution)/shard_map/reduce_scatter | solution.py:112
  300.8 1.4 copy-start.3
  308.3 1.6 copy-start.16
  311.0 7.1 %collective-permute-start.6 = (bf16[8,16,1024]{2,1,0:T(8,128)(2,1)S(1)}, bf16[8,16,1024]{2,1,0:T(8,128)(2,1)S(1)}, u32[]{:S(2)}, u32[]{:S(2)}) collective-permute-start(bf16[8,16,1024]{2,1,0:T(8,128)(2,1)S(1)} %get-tuple-element.109), channel_id=1, source_target_pairs={{0,2},{2,4},{4,6},{6,0},{1,3},{3,5},{5,7},{7,1},{8,10},{10,12},{12... | collective-permute-start | bytes 786440 | tf_op jit(solution)/shard_map/ppermute | solution.py:18
  318.9 22.8 %copy-start.11 = (bf16[8,32,1024]{2,1,0:T(8,128)(2,1)S(1)}, bf16[8,32,1024]{2,1,0:T(8,128)(2,1)}, u32[]{:S(2)}) copy-start(bf16[8,32,1024]{2,1,0:T(8,128)(2,1)} %copy-done.10) | copy-start | bytes 1572868
  322.6 1.0 copy-start.9
  322.6 21.2 %copy-start.1 = (f32[1,2048]{1,0:T(1,128)S(1)}, f32[1,2048]{1,0:T(1,128)}, u32[]{:S(2)}) copy-start(f32[1,2048]{1,0:T(1,128)} %param.21) | copy-start | bytes 24580
  (1 other events, 1.0 us)
Sparse Core Ops, SparseCore 0:
  34.2 23.7 all-gather.4
  60.3 31.9 reduce-scatter.4
  109.4 30.4 all-gather.6
  150.5 28.0 reduce-scatter.6
  189.3 28.6 all-gather.8
  220.1 32.9 reduce-scatter.8
  270.2 30.4 all-gather.10
  323.7 17.9 reduce-scatter.10
where the time goes:
time: 353 us; the launch traced here: 351 us
  waiting for transfers between devices  255 us (72%)
  blocking collectives  25.7 us (7%)
  local copies, waits for them, and re-layouts  16.6 us (5%)
  other arithmetic  15.8 us (4%)
  between operations  13.8 us (4%)
  starting transfers between devices  12.9 us (4%)
  matrix products  10 us (3%)
    all_gather x4, waiting for transfers between devices, per_device(): complete = lax.all_gather(framed, 'head', axis=2, tiled=True)  114 us
    reduce_scatter x4, waiting for transfers between devices, per_device(): lax.psum_scatter(term.astype(jnp.bfloat16), 'head', scatter_dimension=2,...  113 us
    ppermute x4, waiting for transfers between devices, from_behind(): return lax.ppermute(value, axis, pairs)  20.2 us
    psum x4, blocking collectives, per_device(): square_sums = lax.psum(partial_value, 'head')  16.1 us
    unnamed x20, local copies, waits for them, and re-layouts  9.94 us
    all_to_all x1, blocking collectives, per_device(): lax.all_to_all(stream, 'head', split_axis=2, concat_axis=0, tiled=True)  9.62 us
    ppermute x4, starting transfers between devices, from_behind(): return lax.ppermute(value, axis, pairs)  8.72 us
    ppermute x3, waiting for transfers between devices, from_behind_2(): lax.ppermute(value, axis, [(source, source + steps) for source in range(l...  8.05 us
  transfers between devices with their start and end apart: 15, of which 15 were waited for; matrix products, arithmetic and copies ran while one was open for 0% of the time, Pallas kernels for 0%

commit v1 on v0

v1 whole, which is shorter than its diff:
```python
import functools
import math

import jax
import jax.numpy as jnp
from jax import lax
from jax.experimental import pallas as pl
from jax.experimental.pallas import tpu as pltpu
from jax.sharding import PartitionSpec as P

HEAD_DIM = 128
WIN = 32
HALF = WIN // 2
EPSILON = 1e-06
AXES = ("pipe", "win", "head")
VMEM_LIMIT = 24 * 1024 * 1024

vmem = pl.BlockSpec(memory_space=pltpu.VMEM)
smem = pl.BlockSpec(memory_space=pltpu.SMEM)


def project_kernel(section, chunk_order, n_parts, meta, *refs):
    parts, refs = refs[:n_parts], refs[n_parts:]
    scale, weight, x_ref, q_ref, k_ref, v_ref, u_ref = refs
    channels = q_ref.shape[1]

    @pl.when(meta[0] == section)
    def _():
        first = pl.multiple_of(meta[1] * channels, channels)
        for source, target in enumerate(chunk_order):
            rows = pl.ds(source * HALF, HALF)
            put = pl.ds(target * HALF, HALF)
            total = parts[0][rows, :].astype(jnp.float32)
            for part in parts[1:]:
                total = total + part[rows, :].astype(jnp.float32)
            x = total.astype(x_ref.dtype)
            x_ref[put, :] = x
            wide = x.astype(jnp.float32)
            mean_square = jnp.mean(wide * wide, axis=1, keepdims=True)
            u_ref[put, :] = (wide * lax.rsqrt(mean_square + EPSILON)).astype(u_ref.dtype)
        key = u_ref[:, pl.ds(first, channels)]
        k_ref[...] = key
        q_ref[...] = (key.astype(jnp.float32) * scale[...]).astype(q_ref.dtype)
        v_ref[...] = jnp.dot(
            u_ref[...], weight[...], preferred_element_type=jnp.float32
        ).astype(v_ref.dtype)


def project(section, chunk_order, parts, meta, scale, weight):
    rows, width = parts[0].shape
    channels = weight.shape[1]
    bf16 = jnp.bfloat16
    return pl.pallas_call(
        functools.partial(project_kernel, section, chunk_order, len(parts)),
        out_shape=(
            jax.ShapeDtypeStruct((rows, width), bf16),
            jax.ShapeDtypeStruct((rows, channels), bf16),
            jax.ShapeDtypeStruct((rows, channels), bf16),
            jax.ShapeDtypeStruct((rows, channels), bf16),
        ),
        in_specs=[smem] + [vmem] * (len(parts) + 2),
        out_specs=(vmem,) * 4,
        scratch_shapes=[pltpu.VMEM((rows, width), bf16)],
        compiler_params=pltpu.CompilerParams(vmem_limit_bytes=VMEM_LIMIT),
        cost_estimate=pl.CostEstimate(
            flops=2 * rows * width * channels, bytes_accessed=2 * width * channels, transcendentals=0
        ),
        name="project",
    )(meta, *parts, scale, weight)


def attend_kernel(section, pieces, n_blocks, split, meta, *refs):
    blocks, refs = refs[: 4 * n_blocks], refs[4 * n_blocks :]
    xs, qs, ks, vs = (blocks[i * n_blocks : (i + 1) * n_blocks] for i in range(4))
    weight, refs = refs[0], refs[1:]
    outs, o_ref = refs[:-1], refs[-1]
    channels = qs[0].shape[1]
    width = xs[0].shape[1]
    inv_root = 1.0 / math.sqrt(HEAD_DIM)
    n_head = width // channels

    @pl.when(meta[0] == section)
    def _():
        for head in range(channels // HEAD_DIM):
            lanes = slice(head * HEAD_DIM, (head + 1) * HEAD_DIM)
            q = [qs[block][start : start + size, lanes] for block, start, size in pieces]
            q = jnp.concatenate(q, axis=0) if len(q) > 1 else q[0]
            scores = jnp.concatenate(
                [
                    lax.dot_general(
                        q, k[:, lanes], (((1,), (1,)), ((), ())), preferred_element_type=jnp.float32
                    )
                    for k in ks
                ],
                axis=1,
            )
            scores = scores * inv_root
            weights = jnp.exp(scores - jnp.max(scores, axis=1, keepdims=True))
            weights = (weights / jnp.sum(weights, axis=1, keepdims=True)).astype(jnp.bfloat16)
            attended, at = None, 0
            for v in vs:
                term = jnp.dot(
                    weights[:, at : at + v.shape[0]], v[:, lanes], preferred_element_type=jnp.float32
                )
                attended = term if attended is None else attended + term
                at += v.shape[0]
            o_ref[:, lanes] = attended.astype(o_ref.dtype)
        mine = jnp.where(meta[1] == 0, 1.0, 0.0)
        attended = o_ref[...]
        step = channels if split else min(512, width)
        for column in range(0, width, step):
            if split:
                out = outs[column // step]
                block = lax.rem(meta[1] + column // step, n_head)
                lanes = pl.ds(pl.multiple_of(block * step, step), step)
                put_lanes = slice(0, step)
            else:
                out = outs[0]
                lanes = put_lanes = slice(column, column + step)
            g = jnp.dot(attended, weight[:, lanes], preferred_element_type=jnp.float32)
            at = 0
            for turn, (block, start, size) in enumerate(pieces):
                residual = xs[block][start : start + size, lanes].astype(jnp.float32) * mine
                value = residual + g[at : at + size]
                if len(pieces) > 1:
                    place = lax.rem(meta[1] + len(pieces) - turn, len(pieces)) * size
                    rows = pl.ds(pl.multiple_of(place, size), size)
                else:
                    rows = slice(0, size)
                out[rows, put_lanes] = value.astype(out.dtype)
                at += size


def attend(section, pieces, blocks, meta, weight, split):
    rows = sum(size for _, _, size in pieces)
    channels, width = weight.shape
    keys = sum(block[2].shape[0] for block in blocks)
    n_head = width // channels
    if split:
        out_shape = tuple(jax.ShapeDtypeStruct((rows, channels), jnp.bfloat16) for _ in range(n_head))
    else:
        out_shape = (jax.ShapeDtypeStruct((rows, width), jnp.bfloat16),)
    arrays = [block[i] for i in range(4) for block in blocks]
    return pl.pallas_call(
        functools.partial(attend_kernel, section, pieces, len(blocks), split),
        out_shape=out_shape,
        in_specs=[smem] + [vmem] * (len(arrays) + 1),
        out_specs=(vmem,) * len(out_shape),
        scratch_shapes=[pltpu.VMEM((rows, channels), jnp.bfloat16)],
        compiler_params=pltpu.CompilerParams(vmem_limit_bytes=VMEM_LIMIT),
        cost_estimate=pl.CostEstimate(
            flops=2 * rows * channels * (width + 2 * keys),
            bytes_accessed=2 * width * channels,
            transcendentals=rows * keys * channels // HEAD_DIM,
        ),
        name="attend",
    )(meta, *arrays, weight)


def per_device(stream, score_scale, value_weight, out_weight):
    row_count, col_count, width = stream.shape
    assert col_count == WIN, "one window"
    sections, n_win, n_head = (lax.axis_size(axis) for axis in AXES)
    channels = value_weight.shape[2]
    stage, head = lax.axis_index("pipe"), lax.axis_index("head")
    meta = jnp.stack([stage, head]).astype(jnp.int32)
    scale = lax.dynamic_slice_in_dim(score_scale, head * channels, channels, 1)
    value_cols, out_rows = value_weight[0], out_weight[0]

    def send(value, pairs):
        at = lambda pipe, win, head: (pipe * n_win + win % n_win) * n_head + head % n_head
        return lax.ppermute(value, AXES, [(at(*source), at(*target)) for source, target in pairs])

    places = [(win, group) for win in range(n_win) for group in range(n_head)]

    piece = row_count * HALF
    natural = tuple(
        (chunk % 2) * row_count + chunk // 2 for chunk in range(row_count * col_count // HALF)
    )
    own = stream.reshape(row_count * col_count, width)
    arrived = [own]
    for turn in range(1, n_head):
        arrived.append(send(own, [((0, w, g), (0, w, g + turn)) for w, g in places]))
    blocks = [project(0, natural, [cells], meta, scale, value_cols) for cells in arrived]
    halves = [[(block, half * piece, piece) for block in range(n_head)] for half in range(2)]
    straight = tuple(range(row_count * n_head))
    recorded = [None, None]

    for section in range(sections):
        shift = section % 2
        last = section + 1 == sections
        cross = 0 if last else (1 if shift else -1)
        moved = []
        for half in range(2):
            part = attend(section, halves[half], blocks, meta, out_rows, last)
            if last:
                over = shift if half == 0 else 0
                terms = []
                for turn, block in enumerate(part):
                    if over or turn:
                        block = send(
                            block, [((section, w, g), (section, w + over, g + turn)) for w, g in places]
                        )
                    terms.append(block)
            else:
                over = cross if half == 0 else 0
                terms = [
                    send(part[0], [((section, w, g), (section + 1, w + over, g + turn)) for w, g in places])
                    for turn in range(n_head)
                ]
            moved.append(terms)
        if not last:
            blocks = [
                project(section + 1, straight, terms, meta, scale, value_cols) for terms in moved
            ]
            halves = [[(0, 0, piece * n_head)], [(1, 0, piece * n_head)]]
            for half in range(2):
                mine = lax.dynamic_slice_in_dim(blocks[half][0], head * channels, channels, 1)
                kept = recorded[half]
                recorded[half] = mine if kept is None else jnp.where(stage == section + 1, mine, kept)
    outputs = []
    for half in range(2):
        back = []
        for source in range(1, sections):
            over = source % 2 if half == 0 else 0
            back += [((source, w, g), (source - 1, w + over, g)) for w, g in places]
        earlier = send(recorded[half], back)
        total = sum(term.astype(jnp.float32) for term in moved[half]).astype(jnp.bfloat16)
        total = jnp.where(stage == sections - 1, total, earlier)
        outputs.append(total.reshape(row_count * n_head, HALF, channels))
    return jnp.concatenate(outputs, axis=1)[None]


def solution(mesh):
    placed = (
        P("head", "win", None),
        P("pipe", None),
        P("pipe", None, "head"),
        P("pipe", "head", None),
    )
    return jax.shard_map(
        per_device,
        mesh=mesh,
        in_specs=placed,
        out_specs=P("pipe", None, "win", "head"),
        check_vma=False,
    )
```

time: 353 us -> 125 us (0.35)
  waiting for transfers between devices: 255 us -> 68.6 us
  blocking collectives: 25.7 us -> 0 us
  Pallas kernels: 0 us -> 20.3 us
  other arithmetic: 15.8 us -> 1.43 us
  between operations: 13.8 us -> 0.41 us
  starting transfers between devices: 12.9 us -> 25.8 us
  matrix products: 10 us -> 0 us
  local copies, waits for them, and re-layouts: 16.6 us -> 7.77 us
    all_gather x4 -> x0, waiting for transfers between devices: 114 us -> none  [per_device(): complete = lax.all_gather(framed, 'head', axis=2, tiled=True)]
    reduce_scatter x4 -> x0, waiting for transfers between devices: 113 us -> none  [per_device(): lax.psum_scatter(term.astype(jnp.bfloat16), 'head', scatter_dimension=2,...]
    ppermute x7 -> x18, waiting for transfers between devices: 28.3 us -> 68.6 us  [send(): lax.ppermute(value, AXES, [(at(*source), at(*target)) for source, target...]
    pallas_call x0 -> x16, Pallas kernels: none -> 20.3 us  [the longest x8 12.9 us: attend(): pl.pallas_call(functools.partial(attend_kernel, section, pieces, len(bloc...]
    psum x4 -> x0, blocking collectives: 16.1 us -> none  [per_device(): square_sums = lax.psum(partial_value, 'head')]
    ppermute x7 -> x18, starting transfers between devices: 12.6 us -> 25.8 us  [send(): lax.ppermute(value, AXES, [(at(*source), at(*target)) for source, target...]
    all_to_all x1 -> x0, blocking collectives: 9.62 us -> none  [per_device(): lax.all_to_all(stream, 'head', split_axis=2, concat_axis=0, tiled=True)]
    convert_element_type x9 -> x0, other arithmetic: 9.32 us -> none  [the longest x3 3.71 us: per_device(): updated = (current_f + mixture).astype(jnp.bfloat16)]
  transfers between devices with their start and end apart: 15 -> 18, of which waited for: 15 -> 4; matrix products, arithmetic and copies ran while one was open for 0% -> 0% of each run, Pallas kernels for 0% -> 13%
where the time goes in v1:
time: 125 us; the launch traced here: 124 us
  waiting for transfers between devices  68.6 us (55%)
  starting transfers between devices  25.8 us (21%)
  Pallas kernels  20.3 us (16%)
  local copies, waits for them, and re-layouts  7.77 us (6%)
  other arithmetic  1.43 us (1%)
    ppermute x18, waiting for transfers between devices, send(): lax.ppermute(value, AXES, [(at(*source), at(*target)) for source, target...  68.6 us
    ppermute x18, starting transfers between devices, send(): lax.ppermute(value, AXES, [(at(*source), at(*target)) for source, target...  25.8 us
    pallas_call x8, Pallas kernels, attend(): pl.pallas_call(functools.partial(attend_kernel, section, pieces, len(bloc...  12.9 us
    unnamed x14, local copies, waits for them, and re-layouts  7.77 us
    pallas_call x8, Pallas kernels, project(): pl.pallas_call(functools.partial(project_kernel, section, chunk_order, le...  7.36 us
  transfers between devices with their start and end apart: 18, of which 4 were waited for; matrix products, arithmetic and copies ran while one was open for 0% of the time, Pallas kernels for 13%

profile of v1, /device:TPU:5, one launch (start us, length us, event | category | flops | bytes accessed | tf_op | source)
XLA Modules:
  0.0 124.4 jit_solution(17903056388987059331)
XLA Ops:
  0.9 2.2 %copy-done.1 = bf16[1,2048,1024]{2,1,0:T(8,128)(2,1)S(1)} copy-done((bf16[1,2048,1024]{2,1,0:T(8,128)(2,1)S(1)}, bf16[1,2048,1024]{2,1,0:T(8,128)(2,1)}, u32[]{:S(2)}) %copy-start.1) | copy-done | bytes 4194328
  3.1 1.0 copy-done.6
  4.7 1.6 %copy-done.2 = bf16[1,2048,1024]{2,1,0:T(8,128)(2,1)S(1)} copy-done((bf16[1,2048,1024]{2,1,0:T(8,128)(2,1)S(1)}, bf16[1,2048,1024]{2,1,0:T(8,128)(2,1)}, u32[]{:S(2)}) %copy-start.2) | copy-done | bytes 4194328
  18.0 1.3 %attend.13 = bf16[128,2048]{1,0:T(8,128)(2,1)} custom-call(s32[2]{0:T(128)S(1)} %pad_add_fusion.meta, bf16[128,2048]{1,0:T(8,128)(2,1)S(1)} %get-tuple-element.57.refs_0_, bf16[128,2048]{1,0:T(8,128)(2,1)S(1)} %get-tuple-element.58.refs_1_, bf16[128,1024]{1,0:T(8,128)(2,1)S(1)} %get-tuple-element.59.refs_2_, ...), custom_call_target="tpu_custom_call" | custom-call | flops 671088640 | bytes 4194304 | tf_op jit(solution)/shard_map/attend/pallas_call | solution.py:144
  19.3 1.3 %collective-permute-start.12 = (bf16[128,2048]{1,0:T(8,128)(2,1)}, bf16[128,2048]{1,0:T(8,128)(2,1)}, u32[]{:S(2)}, u32[]{:S(2)}) collective-permute-start(bf16[128,2048]{1,0:T(8,128)(2,1)} %attend.13), channel_id=1, source_target_pairs={{16,25},{17,24},{18,27},{19,26},{20,29},{21,28},{22,31},{23,30}} | collective-permute-start | bytes 1572872 | tf_op jit(solution)/shard_map/ppermute | solution.py:172
  20.6 1.3 %collective-permute-start.11 = (bf16[128,2048]{1,0:T(8,128)(2,1)}, bf16[128,2048]{1,0:T(8,128)(2,1)}, u32[]{:S(2)}, u32[]{:S(2)}) collective-permute-start(bf16[128,2048]{1,0:T(8,128)(2,1)} %attend.13), channel_id=1, source_target_pairs={{16,24},{17,25},{18,26},{19,27},{20,28},{21,29},{22,30},{23,31}} | collective-permute-start | bytes 1572872 | tf_op jit(solution)/shard_map/ppermute | solution.py:172
  21.9 1.4 %attend.12 = bf16[128,2048]{1,0:T(8,128)(2,1)} custom-call(s32[2]{0:T(128)S(1)} %pad_add_fusion.meta, bf16[128,2048]{1,0:T(8,128)(2,1)S(1)} %get-tuple-element.57.refs_0_, bf16[128,2048]{1,0:T(8,128)(2,1)S(1)} %get-tuple-element.58.refs_1_, bf16[128,1024]{1,0:T(8,128)(2,1)S(1)} %get-tuple-element.59.refs_2_, ...), custom_call_target="tpu_custom_call" | custom-call | flops 671088640 | bytes 4194304 | tf_op jit(solution)/shard_map/attend/pallas_call | solution.py:144
  23.2 1.3 %collective-permute-start.10 = (bf16[128,2048]{1,0:T(8,128)(2,1)}, bf16[128,2048]{1,0:T(8,128)(2,1)S(1)}, u32[]{:S(2)}, u32[]{:S(2)}) collective-permute-start(bf16[128,2048]{1,0:T(8,128)(2,1)} %attend.12), channel_id=1, source_target_pairs={{16,31},{17,30},{18,25},{19,24},{20,27},{21,26},{22,29},{23,28}} | collective-permute-start | bytes 1572872 | tf_op jit(solution)/shard_map/ppermute | solution.py:172
  24.5 1.3 %collective-permute-start.9 = (bf16[128,2048]{1,0:T(8,128)(2,1)}, bf16[128,2048]{1,0:T(8,128)(2,1)S(1)}, u32[]{:S(2)}, u32[]{:S(2)}) collective-permute-start(bf16[128,2048]{1,0:T(8,128)(2,1)} %attend.12), channel_id=1, source_target_pairs={{16,30},{17,31},{18,24},{19,25},{20,26},{21,27},{22,28},{23,29}} | collective-permute-start | bytes 1572872 | tf_op jit(solution)/shard_map/ppermute | solution.py:172
  25.8 58.1 %collective-permute-done.12.refs_1_ = bf16[128,2048]{1,0:T(8,128)(2,1)} collective-permute-done((bf16[128,2048]{1,0:T(8,128)(2,1)}, bf16[128,2048]{1,0:T(8,128)(2,1)}, u32[]{:S(2)}, u32[]{:S(2)}) %collective-permute-start.12) | collective-permute-done | bytes 524320 | tf_op jit(solution)/shard_map/ppermute | solution.py:172
  83.9 2.2 %copy-done.3 = bf16[1,2048,1024]{2,1,0:T(8,128)(2,1)S(1)} copy-done((bf16[1,2048,1024]{2,1,0:T(8,128)(2,1)S(1)}, bf16[1,2048,1024]{2,1,0:T(8,128)(2,1)}, u32[]{:S(2)}) %copy-start.3) | copy-done | bytes 4194328
  86.1 2.3 %project.15 = (bf16[128,2048]{1,0:T(8,128)(2,1)S(1)}, bf16[128,1024]{1,0:T(8,128)(2,1)S(1)}, bf16[128,1024]{1,0:T(8,128)(2,1)S(1)}, bf16[128,1024]{1,0:T(8,128)(2,1)S(1)}) custom-call(s32[2]{0:T(128)S(1)} %pad_add_fusion.meta, bf16[128,2048]{1,0:T(8,128)(2,1)} %collective-permute-done.11.refs_0_, bf16[128,2048]{1,0:T(8,128)(2,1)} %collective-permute-done.12.refs_1_, ...), custom_call_target="tpu_custom_call" | custom-call | flops 536870912 | bytes 4194304 | tf_op jit(solution)/shard_map/project/pallas_call | solution.py:53
  88.5 3.5 %collective-permute-start.17 = (bf16[128,1024]{1,0:T(8,128)(2,1)S(1)}, bf16[128,1024]{1,0:T(8,128)(2,1)S(1)}, u32[]{:S(2)}, u32[]{:S(2)}) collective-permute-start(bf16[128,1024]{1,0:T(8,128)(2,1)S(1)} %select_select_fusion), channel_id=1, source_target_pairs={{8,0},{9,1},{10,2},{11,3},{12,4},{13,5},{14,6},{15,7},{16,8},{17,9... | collective-permute-start | bytes 786440 | tf_op jit(solution)/shard_map/ppermute | solution.py:172
  92.1 4.9 %collective-permute-done.9.refs_0_ = bf16[128,2048]{1,0:T(8,128)(2,1)S(1)} collective-permute-done((bf16[128,2048]{1,0:T(8,128)(2,1)}, bf16[128,2048]{1,0:T(8,128)(2,1)S(1)}, u32[]{:S(2)}, u32[]{:S(2)}) %collective-permute-start.9) | collective-permute-done | bytes 524320 | tf_op jit(solution)/shard_map/ppermute | solution.py:172
  97.0 1.6 %project.14 = (bf16[128,2048]{1,0:T(8,128)(2,1)S(1)}, bf16[128,1024]{1,0:T(8,128)(2,1)S(1)}, bf16[128,1024]{1,0:T(8,128)(2,1)S(1)}, bf16[128,1024]{1,0:T(8,128)(2,1)S(1)}) custom-call(s32[2]{0:T(128)S(1)} %pad_add_fusion.meta, bf16[128,2048]{1,0:T(8,128)(2,1)S(1)} %collective-permute-done.9.refs_0_, bf16[128,2048]{1,0:T(8,128)(2,1)S(1)} %collective-permute-done.10.refs_1_, ...), custom_call_target="tpu_custom_call" | custom-call | flops 536870912 | bytes 4194304 | tf_op jit(solution)/shard_map/project/pallas_call | solution.py:53
  98.6 4.0 %attend.15 = (bf16[128,1024]{1,0:T(8,128)(2,1)S(1)}, bf16[128,1024]{1,0:T(8,128)(2,1)S(1)}) custom-call(s32[2]{0:T(128)S(1)} %pad_add_fusion.meta, bf16[128,2048]{1,0:T(8,128)(2,1)S(1)} %get-tuple-element.65.refs_0_, bf16[128,2048]{1,0:T(8,128)(2,1)S(1)} %get-tuple-element.66.refs_1_, bf16[128,1024]{1,0:T(8,128)(2,1)S(1)} %get-tuple-element.67.refs_2_, ...), custom_call_target="tpu_custom_call" | custom-call | flops 671088640 | bytes 4194304 | tf_op jit(solution)/shard_map/attend/pallas_call | solution.py:144
  102.6 2.2 %collective-permute-start.16 = (bf16[128,1024]{1,0:T(8,128)(2,1)S(1)}, bf16[128,1024]{1,0:T(8,128)(2,1)S(1)}, u32[]{:S(2)}, u32[]{:S(2)}) collective-permute-start(bf16[128,1024]{1,0:T(8,128)(2,1)S(1)} %get-tuple-element.76), channel_id=1, source_target_pairs={{24,25},{25,24},{26,27},{27,26},{28,29},{29,28},{30,31},{31,30}} | collective-permute-start | bytes 786440 | tf_op jit(solution)/shard_map/ppermute | solution.py:172
  105.0 1.3 %collective-permute-start.15 = (bf16[128,1024]{1,0:T(8,128)(2,1)S(1)}, bf16[128,1024]{1,0:T(8,128)(2,1)S(1)}, u32[]{:S(2)}, u32[]{:S(2)}) collective-permute-start(bf16[128,1024]{1,0:T(8,128)(2,1)S(1)} %select_select_fusion.1), channel_id=1, source_target_pairs={{8,2},{9,3},{10,4},{11,5},{12,6},{13,7},{14,0},{15,1},{16,8},{17,9... | collective-permute-start | bytes 786440 | tf_op jit(solution)/shard_map/ppermute | solution.py:172
  106.3 4.0 %attend.14 = (bf16[128,1024]{1,0:T(8,128)(2,1)S(1)}, bf16[128,1024]{1,0:T(8,128)(2,1)S(1)}) custom-call(s32[2]{0:T(128)S(1)} %pad_add_fusion.meta, bf16[128,2048]{1,0:T(8,128)(2,1)S(1)} %get-tuple-element.65.refs_0_, bf16[128,2048]{1,0:T(8,128)(2,1)S(1)} %get-tuple-element.66.refs_1_, bf16[128,1024]{1,0:T(8,128)(2,1)S(1)} %get-tuple-element.67.refs_2_, ...), custom_call_target="tpu_custom_call" | custom-call | flops 671088640 | bytes 4194304 | tf_op jit(solution)/shard_map/attend/pallas_call | solution.py:144
  110.3 3.2 %collective-permute-start.13 = (bf16[128,1024]{1,0:T(8,128)(2,1)S(1)}, bf16[128,1024]{1,0:T(8,128)(2,1)S(1)}, u32[]{:S(2)}, u32[]{:S(2)}) collective-permute-start(bf16[128,1024]{1,0:T(8,128)(2,1)S(1)} %get-tuple-element.73), channel_id=1, source_target_pairs={{24,26},{25,27},{26,28},{27,29},{28,30},{29,31},{30,24},{31,25}} | collective-permute-start | bytes 786440 | tf_op jit(solution)/shard_map/ppermute | solution.py:172
  113.5 4.1 %collective-permute-start.14 = (bf16[128,1024]{1,0:T(8,128)(2,1)S(1)}, bf16[128,1024]{1,0:T(8,128)(2,1)S(1)}, u32[]{:S(2)}, u32[]{:S(2)}) collective-permute-start(bf16[128,1024]{1,0:T(8,128)(2,1)S(1)} %get-tuple-element.74), channel_id=1, source_target_pairs={{24,27},{25,26},{26,29},{27,28},{28,31},{29,30},{30,25},{31,24}} | collective-permute-start | bytes 786440 | tf_op jit(solution)/shard_map/ppermute | solution.py:172
  117.8 2.6 %collective-permute-done.13 = bf16[128,1024]{1,0:T(8,128)(2,1)S(1)} collective-permute-done((bf16[128,1024]{1,0:T(8,128)(2,1)S(1)}, bf16[128,1024]{1,0:T(8,128)(2,1)S(1)}, u32[]{:S(2)}, u32[]{:S(2)}) %collective-permute-start.13) | collective-permute-done | bytes 262176 | tf_op jit(solution)/shard_map/ppermute | solution.py:172
  120.4 3.1 %collective-permute-done.14 = bf16[128,1024]{1,0:T(8,128)(2,1)S(1)} collective-permute-done((bf16[128,1024]{1,0:T(8,128)(2,1)S(1)}, bf16[128,1024]{1,0:T(8,128)(2,1)S(1)}, u32[]{:S(2)}, u32[]{:S(2)}) %collective-permute-start.14) | collective-permute-done | bytes 262176 | tf_op jit(solution)/shard_map/ppermute | solution.py:172
  123.6 0.8 maximum_bitcast_fusion
  (49 shorter events, 13.4 us)
Async XLA Ops:
  0.0 4.7 %collective-permute-start = (bf16[128,2048]{1,0:T(8,128)(2,1)}, bf16[128,2048]{1,0:T(8,128)(2,1)S(1)}, u32[]{:S(2)}, u32[]{:S(2)}) collective-permute-start(bf16[128,2048]{1,0:T(8,128)(2,1)} %bitcast.25), channel_id=1, source_target_pairs={{0,1},{1,0},{2,3},{3,2},{4,5},{5,4},{6,7},{7,6}} | collective-permute-start | bytes 1572872 | tf_op jit(solution)/shard_map/ppermute | solution.py:172
  0.9 2.2 %copy-start.1 = (bf16[1,2048,1024]{2,1,0:T(8,128)(2,1)S(1)}, bf16[1,2048,1024]{2,1,0:T(8,128)(2,1)}, u32[]{:S(2)}) copy-start(bf16[1,2048,1024]{2,1,0:T(8,128)(2,1)} %param.6) | copy-start | bytes 12582916
  3.1 1.0 copy-start.6
  4.1 2.2 %copy-start.2 = (bf16[1,2048,1024]{2,1,0:T(8,128)(2,1)S(1)}, bf16[1,2048,1024]{2,1,0:T(8,128)(2,1)}, u32[]{:S(2)}) copy-start(bf16[1,2048,1024]{2,1,0:T(8,128)(2,1)} %param.6) | copy-start | bytes 12582916
  4.1 3.5 %copy-start.4 = (bf16[1,1024,2048]{2,1,0:T(8,128)(2,1)S(1)}, bf16[1,1024,2048]{2,1,0:T(8,128)(2,1)}, u32[]{:S(2)}) copy-start(bf16[1,1024,2048]{2,1,0:T(8,128)(2,1)} %param.7) | copy-start | bytes 12582916
  8.2 3.4 %collective-permute-start.2 = (bf16[128,2048]{1,0:T(8,128)(2,1)S(1)}, bf16[128,2048]{1,0:T(8,128)(2,1)S(1)}, u32[]{:S(2)}, u32[]{:S(2)}) collective-permute-start(bf16[128,2048]{1,0:T(8,128)(2,1)S(1)} %attend.8), channel_id=1, source_target_pairs={{0,15},{1,14},{2,9},{3,8},{4,11},{5,10},{6,13},{7,12}} | collective-permute-start | bytes 1572872 | tf_op jit(solution)/shard_map/ppermute | solution.py:172
  8.9 2.7 %collective-permute-start.1 = (bf16[128,2048]{1,0:T(8,128)(2,1)S(1)}, bf16[128,2048]{1,0:T(8,128)(2,1)S(1)}, u32[]{:S(2)}, u32[]{:S(2)}) collective-permute-start(bf16[128,2048]{1,0:T(8,128)(2,1)S(1)} %attend.8), channel_id=1, source_target_pairs={{0,14},{1,15},{2,8},{3,9},{4,10},{5,11},{6,12},{7,13}} | collective-permute-start | bytes 1572872 | tf_op jit(solution)/shard_map/ppermute | solution.py:172
  10.1 2.0 %collective-permute-start.4 = (bf16[128,2048]{1,0:T(8,128)(2,1)S(1)}, bf16[128,2048]{1,0:T(8,128)(2,1)S(1)}, u32[]{:S(2)}, u32[]{:S(2)}) collective-permute-start(bf16[128,2048]{1,0:T(8,128)(2,1)S(1)} %attend.9), channel_id=1, source_target_pairs={{0,9},{1,8},{2,11},{3,10},{4,13},{5,12},{6,15},{7,14}} | collective-permute-start | bytes 1572872 | tf_op jit(solution)/shard_map/ppermute | solution.py:172
  10.8 1.3 %collective-permute-start.3 = (bf16[128,2048]{1,0:T(8,128)(2,1)S(1)}, bf16[128,2048]{1,0:T(8,128)(2,1)S(1)}, u32[]{:S(2)}, u32[]{:S(2)}) collective-permute-start(bf16[128,2048]{1,0:T(8,128)(2,1)S(1)} %attend.9), channel_id=1, source_target_pairs={{0,8},{1,9},{2,10},{3,11},{4,12},{5,13},{6,14},{7,15}} | collective-permute-start | bytes 1572872 | tf_op jit(solution)/shard_map/ppermute | solution.py:172
  13.3 3.4 %collective-permute-start.6 = (bf16[128,2048]{1,0:T(8,128)(2,1)S(1)}, bf16[128,2048]{1,0:T(8,128)(2,1)S(1)}, u32[]{:S(2)}, u32[]{:S(2)}) collective-permute-start(bf16[128,2048]{1,0:T(8,128)(2,1)S(1)} %attend.10), channel_id=1, source_target_pairs={{8,19},{9,18},{10,21},{11,20},{12,23},{13,22},{14,17},{15,16}} | collective-permute-start | bytes 1572872 | tf_op jit(solution)/shard_map/ppermute | solution.py:172
  14.0 2.7 %collective-permute-start.5 = (bf16[128,2048]{1,0:T(8,128)(2,1)S(1)}, bf16[128,2048]{1,0:T(8,128)(2,1)S(1)}, u32[]{:S(2)}, u32[]{:S(2)}) collective-permute-start(bf16[128,2048]{1,0:T(8,128)(2,1)S(1)} %attend.10), channel_id=1, source_target_pairs={{8,18},{9,19},{10,20},{11,21},{12,22},{13,23},{14,16},{15,17}} | collective-permute-start | bytes 1572872 | tf_op jit(solution)/shard_map/ppermute | solution.py:172
  15.2 2.2 %collective-permute-start.8 = (bf16[128,2048]{1,0:T(8,128)(2,1)S(1)}, bf16[128,2048]{1,0:T(8,128)(2,1)S(1)}, u32[]{:S(2)}, u32[]{:S(2)}) collective-permute-start(bf16[128,2048]{1,0:T(8,128)(2,1)S(1)} %attend.11), channel_id=1, source_target_pairs={{8,17},{9,16},{10,19},{11,18},{12,21},{13,20},{14,23},{15,22}} | collective-permute-start | bytes 1572872 | tf_op jit(solution)/shard_map/ppermute | solution.py:172
  15.9 1.5 %collective-permute-start.7 = (bf16[128,2048]{1,0:T(8,128)(2,1)S(1)}, bf16[128,2048]{1,0:T(8,128)(2,1)S(1)}, u32[]{:S(2)}, u32[]{:S(2)}) collective-permute-start(bf16[128,2048]{1,0:T(8,128)(2,1)S(1)} %attend.11), channel_id=1, source_target_pairs={{8,16},{9,17},{10,18},{11,19},{12,20},{13,21},{14,22},{15,23}} | collective-permute-start | bytes 1572872 | tf_op jit(solution)/shard_map/ppermute | solution.py:172
  19.3 64.6 %collective-permute-start.12 = (bf16[128,2048]{1,0:T(8,128)(2,1)}, bf16[128,2048]{1,0:T(8,128)(2,1)}, u32[]{:S(2)}, u32[]{:S(2)}) collective-permute-start(bf16[128,2048]{1,0:T(8,128)(2,1)} %attend.13), channel_id=1, source_target_pairs={{16,25},{17,24},{18,27},{19,26},{20,29},{21,28},{22,31},{23,30}} | collective-permute-start | bytes 1572872 | tf_op jit(solution)/shard_map/ppermute | solution.py:172
  20.6 63.3 %collective-permute-start.11 = (bf16[128,2048]{1,0:T(8,128)(2,1)}, bf16[128,2048]{1,0:T(8,128)(2,1)}, u32[]{:S(2)}, u32[]{:S(2)}) collective-permute-start(bf16[128,2048]{1,0:T(8,128)(2,1)} %attend.13), channel_id=1, source_target_pairs={{16,24},{17,25},{18,26},{19,27},{20,28},{21,29},{22,30},{23,31}} | collective-permute-start | bytes 1572872 | tf_op jit(solution)/shard_map/ppermute | solution.py:172
  23.2 68.8 %collective-permute-start.10 = (bf16[128,2048]{1,0:T(8,128)(2,1)}, bf16[128,2048]{1,0:T(8,128)(2,1)S(1)}, u32[]{:S(2)}, u32[]{:S(2)}) collective-permute-start(bf16[128,2048]{1,0:T(8,128)(2,1)} %attend.12), channel_id=1, source_target_pairs={{16,31},{17,30},{18,25},{19,24},{20,27},{21,26},{22,29},{23,28}} | collective-permute-start | bytes 1572872 | tf_op jit(solution)/shard_map/ppermute | solution.py:172
  24.5 72.5 %collective-permute-start.9 = (bf16[128,2048]{1,0:T(8,128)(2,1)}, bf16[128,2048]{1,0:T(8,128)(2,1)S(1)}, u32[]{:S(2)}, u32[]{:S(2)}) collective-permute-start(bf16[128,2048]{1,0:T(8,128)(2,1)} %attend.12), channel_id=1, source_target_pairs={{16,30},{17,31},{18,24},{19,25},{20,26},{21,27},{22,28},{23,29}} | collective-permute-start | bytes 1572872 | tf_op jit(solution)/shard_map/ppermute | solution.py:172
  83.9 2.2 %copy-start.3 = (bf16[1,2048,1024]{2,1,0:T(8,128)(2,1)S(1)}, bf16[1,2048,1024]{2,1,0:T(8,128)(2,1)}, u32[]{:S(2)}) copy-start(bf16[1,2048,1024]{2,1,0:T(8,128)(2,1)} %param.6) | copy-start | bytes 12582916
  88.4 10.2 %copy-start.5 = (bf16[1,1024,2048]{2,1,0:T(8,128)(2,1)S(1)}, bf16[1,1024,2048]{2,1,0:T(8,128)(2,1)}, u32[]{:S(2)}) copy-start(bf16[1,1024,2048]{2,1,0:T(8,128)(2,1)} %param.7) | copy-start | bytes 12582916
  88.5 29.1 %collective-permute-start.17 = (bf16[128,1024]{1,0:T(8,128)(2,1)S(1)}, bf16[128,1024]{1,0:T(8,128)(2,1)S(1)}, u32[]{:S(2)}, u32[]{:S(2)}) collective-permute-start(bf16[128,1024]{1,0:T(8,128)(2,1)S(1)} %select_select_fusion), channel_id=1, source_target_pairs={{8,0},{9,1},{10,2},{11,3},{12,4},{13,5},{14,6},{15,7},{16,8},{17,9... | collective-permute-start | bytes 786440 | tf_op jit(solution)/shard_map/ppermute | solution.py:172
  102.6 15.0 %collective-permute-start.16 = (bf16[128,1024]{1,0:T(8,128)(2,1)S(1)}, bf16[128,1024]{1,0:T(8,128)(2,1)S(1)}, u32[]{:S(2)}, u32[]{:S(2)}) collective-permute-start(bf16[128,1024]{1,0:T(8,128)(2,1)S(1)} %get-tuple-element.76), channel_id=1, source_target_pairs={{24,25},{25,24},{26,27},{27,26},{28,29},{29,28},{30,31},{31,30}} | collective-permute-start | bytes 786440 | tf_op jit(solution)/shard_map/ppermute | solution.py:172
  105.0 12.8 %collective-permute-start.15 = (bf16[128,1024]{1,0:T(8,128)(2,1)S(1)}, bf16[128,1024]{1,0:T(8,128)(2,1)S(1)}, u32[]{:S(2)}, u32[]{:S(2)}) collective-permute-start(bf16[128,1024]{1,0:T(8,128)(2,1)S(1)} %select_select_fusion.1), channel_id=1, source_target_pairs={{8,2},{9,3},{10,4},{11,5},{12,6},{13,7},{14,0},{15,1},{16,8},{17,9... | collective-permute-start | bytes 786440 | tf_op jit(solution)/shard_map/ppermute | solution.py:172
  110.3 10.1 %collective-permute-start.13 = (bf16[128,1024]{1,0:T(8,128)(2,1)S(1)}, bf16[128,1024]{1,0:T(8,128)(2,1)S(1)}, u32[]{:S(2)}, u32[]{:S(2)}) collective-permute-start(bf16[128,1024]{1,0:T(8,128)(2,1)S(1)} %get-tuple-element.73), channel_id=1, source_target_pairs={{24,26},{25,27},{26,28},{27,29},{28,30},{29,31},{30,24},{31,25}} | collective-permute-start | bytes 786440 | tf_op jit(solution)/shard_map/ppermute | solution.py:172
  113.5 9.9 %collective-permute-start.14 = (bf16[128,1024]{1,0:T(8,128)(2,1)S(1)}, bf16[128,1024]{1,0:T(8,128)(2,1)S(1)}, u32[]{:S(2)}, u32[]{:S(2)}) collective-permute-start(bf16[128,1024]{1,0:T(8,128)(2,1)S(1)} %get-tuple-element.74), channel_id=1, source_target_pairs={{24,27},{25,26},{26,29},{27,28},{28,31},{29,30},{30,25},{31,24}} | collective-permute-start | bytes 786440 | tf_op jit(solution)/shard_map/ppermute | solution.py:172
  (1 other events, 0.9 us)

commit v2 on v1

v2 whole, which is shorter than its diff:
```python
import functools
import math

import jax
import jax.numpy as jnp
from jax import lax
from jax.experimental import pallas as pl
from jax.experimental.pallas import tpu as pltpu
from jax.sharding import PartitionSpec as P

HEAD_DIM = 128
WIN = 32
HALF = WIN // 2
EPSILON = 1e-06
AXES = ("pipe", "win", "head")
VMEM_LIMIT = 14 * 1024 * 1024

vmem = pl.BlockSpec(memory_space=pltpu.VMEM)
anywhere = pl.BlockSpec(memory_space=pl.ANY)
MARK = jax.ShapeDtypeStruct((8, 128), jnp.float32)


def project_kernel(section, chunk_order, n_parts, keep, mark, *refs):
    parts, refs = refs[:n_parts], refs[n_parts:]
    scale, weight, refs = refs[0], refs[1], refs[2:]
    before, refs = (refs[0], refs[1:]) if keep == "hand on" else (None, refs)
    x_ref, q_ref, k_ref, v_ref, refs = *refs[:4], refs[4:]
    kept = refs[0] if keep else None
    u_ref = refs[-1]
    channels = q_ref.shape[1]

    @pl.when(lax.axis_index("pipe") == section)
    def _():
        mine = pl.ds(pl.multiple_of(lax.axis_index("head") * channels, channels), channels)
        for source, target in enumerate(chunk_order):
            rows = pl.ds(source * HALF, HALF)
            put = pl.ds(target * HALF, HALF)
            total = parts[0][rows, :].astype(jnp.float32)
            for part in parts[1:]:
                total = total + part[rows, :].astype(jnp.float32)
            x = total.astype(x_ref.dtype)
            x_ref[put, :] = x
            wide = x.astype(jnp.float32)
            mean_square = jnp.mean(wide * wide, axis=1, keepdims=True)
            u_ref[put, :] = (wide * lax.rsqrt(mean_square + EPSILON)).astype(u_ref.dtype)
        key = u_ref[:, mine]
        k_ref[...] = key
        q_ref[...] = (key.astype(jnp.float32) * scale[:, mine]).astype(q_ref.dtype)
        v_ref[...] = jnp.dot(
            u_ref[...], weight[...], preferred_element_type=jnp.float32
        ).astype(v_ref.dtype)
        if keep:
            kept[...] = x_ref[:, mine]

    if keep == "hand on":

        @pl.when(lax.axis_index("pipe") != section)
        def _():
            kept[...] = before[...]


def project(section, chunk_order, parts, mark, scale, weight, before):
    rows, width = parts[0].shape
    channels = weight.shape[1]
    keep = "" if section == 0 else "start" if before is None else "hand on"
    shapes = [(rows, width)] + [(rows, channels)] * (4 if keep else 3)
    arrays = [*parts, scale, weight] + ([before] if keep == "hand on" else [])
    return pl.pallas_call(
        functools.partial(project_kernel, section, chunk_order, len(parts), keep),
        out_shape=tuple(jax.ShapeDtypeStruct(shape, jnp.bfloat16) for shape in shapes) + (MARK,),
        in_specs=[anywhere] + [vmem] * len(arrays),
        out_specs=(vmem,) * len(shapes) + (anywhere,),
        scratch_shapes=[pltpu.VMEM((rows, width), jnp.bfloat16)],
        compiler_params=pltpu.CompilerParams(vmem_limit_bytes=VMEM_LIMIT),
        cost_estimate=pl.CostEstimate(
            flops=2 * rows * width * channels, bytes_accessed=2 * width * channels, transcendentals=0
        ),
        name="project",
    )(mark, *arrays)


def join(values, axis):
    return jnp.concatenate(values, axis=axis) if len(values) > 1 else values[0]


def attend_kernel(section, pieces, n_blocks, split, mark, *refs):
    blocks, refs = refs[: 4 * n_blocks], refs[4 * n_blocks :]
    xs, qs, ks, vs = (blocks[i * n_blocks : (i + 1) * n_blocks] for i in range(4))
    weight, refs = refs[0], refs[1:]
    outs, o_ref = refs[:-2], refs[-1]
    channels = qs[0].shape[1]
    width = xs[0].shape[1]
    inv_root = 1.0 / math.sqrt(HEAD_DIM)
    n_head = width // channels

    @pl.when(lax.axis_index("pipe") == section)
    def _():
        heads = [slice(at, at + HEAD_DIM) for at in range(0, channels, HEAD_DIM)]
        keys = sum(k.shape[0] for k in ks)
        ones = jnp.ones((keys, HEAD_DIM), jnp.bfloat16)
        weights = []
        for lanes in heads:
            q = join([qs[block][start : start + size, lanes] for block, start, size in pieces], 0)
            scores = join(
                [
                    lax.dot_general(
                        q, k[:, lanes], (((1,), (1,)), ((), ())), preferred_element_type=jnp.float32
                    )
                    for k in ks
                ],
                1,
            )
            highest = jnp.max(scores, axis=1, keepdims=True)
            weights.append(jnp.exp((scores - highest) * inv_root).astype(jnp.bfloat16))
        for lanes, weight_of_head in zip(heads, weights):
            v = jnp.concatenate([join([v[:, lanes] for v in vs], 0), ones], axis=1)
            attended = jnp.dot(weight_of_head, v, preferred_element_type=jnp.float32)
            o_ref[:, lanes] = (attended[:, :HEAD_DIM] / attended[:, HEAD_DIM:]).astype(o_ref.dtype)
        mine = jnp.where(lax.axis_index("head") == 0, 1.0, 0.0)
        attended = o_ref[...]
        step = channels if split else min(512, width)
        for column in range(0, width, step):
            if split:
                out = outs[column // step]
                block = lax.rem(lax.axis_index("head") + column // step, n_head)
                lanes = pl.ds(pl.multiple_of(block * step, step), step)
                put_lanes = slice(0, step)
            else:
                out = outs[0]
                lanes = put_lanes = slice(column, column + step)
            g = jnp.dot(attended, weight[:, lanes], preferred_element_type=jnp.float32)
            at = 0
            for turn, (block, start, size) in enumerate(pieces):
                residual = xs[block][start : start + size, lanes].astype(jnp.float32) * mine
                value = residual + g[at : at + size]
                if len(pieces) > 1:
                    place = lax.rem(lax.axis_index("head") + len(pieces) - turn, len(pieces)) * size
                    rows = pl.ds(pl.multiple_of(place, size), size)
                else:
                    rows = slice(0, size)
                out[rows, put_lanes] = value.astype(out.dtype)
                at += size


def attend(section, pieces, blocks, mark, weight, split):
    rows = sum(size for _, _, size in pieces)
    channels, width = weight.shape
    keys = sum(block[2].shape[0] for block in blocks)
    n_head = width // channels
    if split:
        out_shape = tuple(jax.ShapeDtypeStruct((rows, channels), jnp.bfloat16) for _ in range(n_head))
    else:
        out_shape = (jax.ShapeDtypeStruct((rows, width), jnp.bfloat16),)
    arrays = [block[i] for i in range(4) for block in blocks]
    return pl.pallas_call(
        functools.partial(attend_kernel, section, pieces, len(blocks), split),
        out_shape=out_shape + (MARK,),
        in_specs=[anywhere] + [vmem] * (len(arrays) + 1),
        out_specs=(vmem,) * len(out_shape) + (anywhere,),
        scratch_shapes=[pltpu.VMEM((rows, channels), jnp.bfloat16)],
        compiler_params=pltpu.CompilerParams(vmem_limit_bytes=VMEM_LIMIT),
        cost_estimate=pl.CostEstimate(
            flops=2 * rows * channels * (width + 2 * keys),
            bytes_accessed=2 * width * channels,
            transcendentals=rows * keys * channels // HEAD_DIM,
        ),
        name="attend",
    )(mark, *arrays, weight)


def add_kernel(section, mark, *refs):
    @pl.when(lax.axis_index("pipe") == section)
    def _():
        total = refs[0][...].astype(jnp.float32)
        for term in refs[1:-2]:
            total = total + term[...].astype(jnp.float32)
        refs[-2][...] = total.astype(refs[-2].dtype)


def add(section, terms, mark):
    return pl.pallas_call(
        functools.partial(add_kernel, section),
        out_shape=(jax.ShapeDtypeStruct(terms[0].shape, terms[0].dtype), MARK),
        in_specs=[anywhere] + [vmem] * len(terms),
        out_specs=(vmem, anywhere),
        compiler_params=pltpu.CompilerParams(vmem_limit_bytes=VMEM_LIMIT),
        name="add",
    )(mark, *terms)


def finish_kernel(section, *refs):
    sums, backs, out = refs[:2], refs[2:4], refs[4]
    shape = (out.shape[0], HALF, out.shape[2])
    for choice, halves in ((lax.axis_index("pipe") == section, sums), (lax.axis_index("pipe") != section, backs)):

        @pl.when(choice)
        def _():
            for half in range(2):
                out[:, half * HALF : (half + 1) * HALF, :] = halves[half][...].reshape(shape)


def finish(section, row_count, mark, moved, backs):
    channels = backs[0].shape[1]
    sums = []
    for terms in moved:
        total, mark = add(section, terms, mark)
        sums.append(total)
    return pl.pallas_call(
        functools.partial(finish_kernel, section),
        out_shape=jax.ShapeDtypeStruct((row_count, WIN, channels), jnp.bfloat16),
        in_specs=[vmem] * 4,
        out_specs=vmem,
        compiler_params=pltpu.CompilerParams(vmem_limit_bytes=VMEM_LIMIT),
        name="finish",
    )(*sums, *backs)


def after(arrays, mark):
    shapes = tuple(jax.ShapeDtypeStruct(array.shape, array.dtype) for array in arrays)
    return pl.pallas_call(
        lambda *refs: None,
        out_shape=shapes,
        in_specs=[anywhere] * (len(arrays) + 1),
        out_specs=(anywhere,) * len(arrays),
        input_output_aliases={place: place for place in range(len(arrays))},
        compiler_params=pltpu.CompilerParams(vmem_limit_bytes=1024 * 1024),
        name="after",
    )(*arrays, mark)


def per_device(stream, score_scale, value_weight, out_weight):
    row_count, col_count, width = stream.shape
    assert col_count == WIN, "one window"
    sections, n_win, n_head = (lax.axis_size(axis) for axis in AXES)
    value_cols, out_rows = value_weight[0], out_weight[0]
    places = [(win, group) for win in range(n_win) for group in range(n_head)]

    def send(value, start, stop, over=0, turn=0):
        return send_all(value, [(start, stop)], [over], turn)

    def send_all(value, hops, overs, turn=0):
        at = lambda pipe, win, group: (pipe * n_win + win % n_win) * n_head + group % n_head
        pairs = [
            (at(start, win, group), at(stop, win + over, group + turn))
            for (start, stop), over in zip(hops, overs)
            for win, group in places
        ]
        return lax.ppermute(value, AXES, pairs)

    piece = row_count * HALF
    natural = tuple(
        (chunk % 2) * row_count + chunk // 2 for chunk in range(row_count * col_count // HALF)
    )
    own = stream.reshape(row_count * col_count, width)
    arrived = [own] + [send(own, 0, 0, 0, turn) for turn in range(1, n_head)]
    mark = jnp.zeros(MARK.shape, MARK.dtype)
    blocks = []
    for cells in arrived:
        *block, mark = project(0, natural, [cells], mark, score_scale, value_cols, None)
        blocks.append(block)
    halves = [[(block, half * piece, piece) for block in range(n_head)] for half in range(2)]
    straight = tuple(range(row_count * n_head))
    kept = [None, None]

    for section in range(sections):
        shift = section % 2
        last = section + 1 == sections
        moved = []
        for half in range(2):
            *part, mark = attend(section, halves[half], blocks, mark, out_rows, last)
            cross = 0 if half else shift if last else 1 if shift else -1
            if last:
                terms = [
                    send(block, section, section, cross, turn) if cross or turn else block
                    for turn, block in enumerate(part)
                ]
            elif shift and not half:
                terms = [send(part[0], section, section + 1, cross)]
            else:
                terms = [send(part[0], section, section + 1, cross, turn) for turn in range(n_head)]
            moved.append(terms)
        if shift and not last:
            (one,) = after(moved[0], mark)
            moved[0] = [one] + [
                send(one, section + 1, section + 1, 0, turn) for turn in range(1, n_head)
            ]
        if not last:
            blocks = [None, None]
            for half in (1, 0) if shift else (0, 1):
                *blocks[half], kept[half], mark = project(
                    section + 1, straight, moved[half], mark, score_scale, value_cols, kept[half]
                )
            halves = [[(0, 0, piece * n_head)], [(1, 0, piece * n_head)]]
    hops = [(source, source - 1) for source in range(1, sections)]
    kept = after(kept, mark)
    backs = [
        send_all(kept[half], hops, [0 if half else source % 2 for source, _ in hops])
        for half in range(2)
    ]
    return finish(sections - 1, row_count * n_head, mark, moved, backs)[None]


def solution(mesh):
    placed = (
        P("head", "win", None),
        P("pipe", None),
        P("pipe", None, "head"),
        P("pipe", "head", None),
    )
    return jax.shard_map(
        per_device,
        mesh=mesh,
        in_specs=placed,
        out_specs=P("pipe", None, "win", "head"),
        check_vma=False,
    )
```

time: 125 us -> 98.5 us (0.79)
  the two profiles are of different devices: /device:TPU:5 before, /device:TPU:4 now
where the time goes in v2:
time: 98.5 us; the launch traced here: 98 us
  waiting for transfers between devices  61 us (62%)
  starting transfers between devices  23.1 us (23%)
  local copies, waits for them, and re-layouts  7.38 us (7%)
  Pallas kernels  6.12 us (6%)
    ppermute x18, waiting for transfers between devices, send_all(): return lax.ppermute(value, AXES, pairs)  61 us
    ppermute x18, starting transfers between devices, send_all(): return lax.ppermute(value, AXES, pairs)  23.1 us
    unnamed x12, local copies, waits for them, and re-layouts  7.38 us
    pallas_call x8, Pallas kernels, attend(): pl.pallas_call(functools.partial(attend_kernel, section, pieces, len(bloc...  3.08 us
    pallas_call x8, Pallas kernels, project(): pl.pallas_call(functools.partial(project_kernel, section, chunk_order, le...  2.18 us
  transfers between devices with their start and end apart: 18, of which 6 were waited for; matrix products, arithmetic and copies ran while one was open for 0% of the time, Pallas kernels for 3%

profile of v2, /device:TPU:4, one launch (start us, length us, event | category | flops | bytes accessed | tf_op | source)
XLA Modules:
  0.0 98.0 jit_solution(7907110294857157858)
XLA Ops:
  0.7 2.2 %copy-done = bf16[1,2048,1024]{2,1,0:T(8,128)(2,1)S(1)} copy-done((bf16[1,2048,1024]{2,1,0:T(8,128)(2,1)S(1)}, bf16[1,2048,1024]{2,1,0:T(8,128)(2,1)}, u32[]{:S(2)}) %copy-start) | copy-done | bytes 4194328
  3.6 1.0 %copy-done.5 = bf16[4,32,2048]{2,1,0:T(8,128)(2,1)S(1)} copy-done((bf16[4,32,2048]{2,1,0:T(8,128)(2,1)S(1)}, bf16[4,32,2048]{2,1,0:T(8,128)(2,1)}, u32[]{:S(2)}) %copy-start.5) | copy-done | bytes 524312
  4.6 2.2 %copy-done.1 = bf16[1,2048,1024]{2,1,0:T(8,128)(2,1)S(1)} copy-done((bf16[1,2048,1024]{2,1,0:T(8,128)(2,1)S(1)}, bf16[1,2048,1024]{2,1,0:T(8,128)(2,1)}, u32[]{:S(2)}) %copy-start.1) | copy-done | bytes 4194328
  6.8 1.3 %copy-done.2 = bf16[1,1024,2048]{2,1,0:T(8,128)(2,1)S(1)} copy-done((bf16[1,1024,2048]{2,1,0:T(8,128)(2,1)S(1)}, bf16[1,1024,2048]{2,1,0:T(8,128)(2,1)}, u32[]{:S(2)}) %copy-start.2) | copy-done | bytes 4194328
  11.2 1.3 %collective-permute-start.7 = (bf16[128,2048]{1,0:T(8,128)(2,1)S(1)}, bf16[128,2048]{1,0:T(8,128)(2,1)S(1)}, u32[]{:S(2)}, u32[]{:S(2)}) collective-permute-start(bf16[128,2048]{1,0:T(8,128)(2,1)S(1)} %get-tuple-element.103), channel_id=1, source_target_pairs={{8,18},{9,19},{10,20},{11,21},{12,22},{13,23},{14,16},{15,17}} | collective-permute-start | bytes 1572872 | tf_op jit(solution)/shard_map/ppermute | solution.py:248
  12.5 1.3 %collective-permute-start.6 = (bf16[128,2048]{1,0:T(8,128)(2,1)S(1)}, bf16[128,2048]{1,0:T(8,128)(2,1)S(1)}, u32[]{:S(2)}, u32[]{:S(2)}) collective-permute-start(bf16[128,2048]{1,0:T(8,128)(2,1)S(1)} %get-tuple-element.100), channel_id=1, source_target_pairs={{8,17},{9,16},{10,19},{11,18},{12,21},{13,20},{14,23},{15,22}} | collective-permute-start | bytes 1572872 | tf_op jit(solution)/shard_map/ppermute | solution.py:248
  13.8 1.3 %collective-permute-start.5 = (bf16[128,2048]{1,0:T(8,128)(2,1)S(1)}, bf16[128,2048]{1,0:T(8,128)(2,1)S(1)}, u32[]{:S(2)}, u32[]{:S(2)}) collective-permute-start(bf16[128,2048]{1,0:T(8,128)(2,1)S(1)} %get-tuple-element.100), channel_id=1, source_target_pairs={{8,16},{9,17},{10,18},{11,19},{12,20},{13,21},{14,22},{15,23}} | collective-permute-start | bytes 1572872 | tf_op jit(solution)/shard_map/ppermute | solution.py:248
  15.1 30.1 %collective-permute-done.7.refs_0_ = bf16[128,2048]{1,0:T(8,128)(2,1)S(1)} collective-permute-done((bf16[128,2048]{1,0:T(8,128)(2,1)S(1)}, bf16[128,2048]{1,0:T(8,128)(2,1)S(1)}, u32[]{:S(2)}, u32[]{:S(2)}) %collective-permute-start.7) | collective-permute-done | bytes 524320 | tf_op jit(solution)/shard_map/ppermute | solution.py:248
  45.2 4.5 %collective-permute-start.8 = (bf16[128,2048]{1,0:T(8,128)(2,1)S(1)}, bf16[128,2048]{1,0:T(8,128)(2,1)S(1)}, u32[]{:S(2)}, u32[]{:S(2)}) collective-permute-start(bf16[128,2048]{1,0:T(8,128)(2,1)S(1)} %after.2.refs_0_), channel_id=1, source_target_pairs={{16,17},{17,16},{18,19},{19,18},{20,21},{21,20},{22,23},{23,22}} | collective-permute-start | bytes 1572872 | tf_op jit(solution)/shard_map/ppermute | solution.py:248
  49.7 4.0 %collective-permute-done.5.refs_0_ = bf16[128,2048]{1,0:T(8,128)(2,1)S(1)} collective-permute-done((bf16[128,2048]{1,0:T(8,128)(2,1)S(1)}, bf16[128,2048]{1,0:T(8,128)(2,1)S(1)}, u32[]{:S(2)}, u32[]{:S(2)}) %collective-permute-start.5) | collective-permute-done | bytes 524320 | tf_op jit(solution)/shard_map/ppermute | solution.py:248
  53.7 1.0 %project.12 = (bf16[128,2048]{1,0:T(8,128)(2,1)S(1)}, bf16[128,1024]{1,0:T(8,128)(2,1)S(1)}, bf16[128,1024]{1,0:T(8,128)(2,1)S(1)}, bf16[128,1024]{1,0:T(8,128)(...) custom-call(f32[8,128]{1,0:T(8,128)S(1)} %get-tuple-element.99.mark.refs_1_, ...), custom_call_target="tpu_custom_call" | custom-call | flops 536870912 | bytes 4194304 | tf_op jit(solution)/shard_map/project/pallas_call | solution.py:68
  54.8 2.1 %collective-permute-done.8.refs_1_ = bf16[128,2048]{1,0:T(8,128)(2,1)S(1)} collective-permute-done((bf16[128,2048]{1,0:T(8,128)(2,1)S(1)}, bf16[128,2048]{1,0:T(8,128)(2,1)S(1)}, u32[]{:S(2)}, u32[]{:S(2)}) %collective-permute-start.8) | collective-permute-done | bytes 524320 | tf_op jit(solution)/shard_map/ppermute | solution.py:248
  56.9 1.0 %project.13 = (bf16[128,2048]{1,0:T(8,128)(2,1)S(1)}, bf16[128,1024]{1,0:T(8,128)(2,1)S(1)}, bf16[128,1024]{1,0:T(8,128)(2,1)S(1)}, bf16[128,1024]{1,0:T(8,128)(...) custom-call(f32[8,128]{1,0:T(8,128)S(1)} %get-tuple-element.102.mark, bf16[128,2048]{1,0:T(8,128)(2,1)S(1)} %after.2.refs_0_, ...), custom_call_target="tpu_custom_call" | custom-call | flops 536870912 | bytes 4194304 | tf_op jit(solution)/shard_map/project/pallas_call | solution.py:68
  57.9 1.6 %attend.12 = (bf16[128,2048]{1,0:T(8,128)(2,1)S(1)}, f32[8,128]{1,0:T(8,128)S(1)}) custom-call(f32[8,128]{1,0:T(8,128)S(1)} %get-tuple-element.105.mark, bf16[128,2048]{1,0:T(8,128)(2,1)S(1)} %get-tuple-element.106.refs_0_, bf16[128,2048]{1,0:T(8,128)(2,1)S(1)} %get-tuple-element.107.refs_1_, bf16[128,1024]{1,0:T(8,128)(2,1)S(1)} %get-tuple-element.108.refs_2_, ...), custom_call_target="tpu_custom_call" | custom-call | flops 671088640 | bytes 4194304 | tf_op jit(solution)/shard_map/attend/pallas_call | solution.py:155
  59.5 1.3 %collective-permute-start.10 = (bf16[128,2048]{1,0:T(8,128)(2,1)S(1)}, bf16[128,2048]{1,0:T(8,128)(2,1)S(1)}, u32[]{:S(2)}, u32[]{:S(2)}) collective-permute-start(bf16[128,2048]{1,0:T(8,128)(2,1)S(1)} %get-tuple-element.116), channel_id=1, source_target_pairs={{16,31},{17,30},{18,25},{19,24},{20,27},{21,26},{22,29},{23,28}} | collective-permute-start | bytes 1572872 | tf_op jit(solution)/shard_map/ppermute | solution.py:248
  60.8 1.3 %collective-permute-start.9 = (bf16[128,2048]{1,0:T(8,128)(2,1)S(1)}, bf16[128,2048]{1,0:T(8,128)(2,1)S(1)}, u32[]{:S(2)}, u32[]{:S(2)}) collective-permute-start(bf16[128,2048]{1,0:T(8,128)(2,1)S(1)} %get-tuple-element.116), channel_id=1, source_target_pairs={{16,30},{17,31},{18,24},{19,25},{20,26},{21,27},{22,28},{23,29}} | collective-permute-start | bytes 1572872 | tf_op jit(solution)/shard_map/ppermute | solution.py:248
  62.2 1.4 %attend.13 = (bf16[128,2048]{1,0:T(8,128)(2,1)S(1)}, f32[8,128]{1,0:T(8,128)S(1)}) custom-call(f32[8,128]{1,0:T(8,128)S(1)} %get-tuple-element.114.mark, bf16[128,2048]{1,0:T(8,128)(2,1)S(1)} %get-tuple-element.106.refs_0_, bf16[128,2048]{1,0:T(8,128)(2,1)S(1)} %get-tuple-element.107.refs_1_, bf16[128,1024]{1,0:T(8,128)(2,1)S(1)} %get-tuple-element.108.refs_2_, ...), custom_call_target="tpu_custom_call" | custom-call | flops 671088640 | bytes 4194304 | tf_op jit(solution)/shard_map/attend/pallas_call | solution.py:155
  63.6 1.3 %collective-permute-start.12 = (bf16[128,2048]{1,0:T(8,128)(2,1)S(1)}, bf16[128,2048]{1,0:T(8,128)(2,1)S(1)}, u32[]{:S(2)}, u32[]{:S(2)}) collective-permute-start(bf16[128,2048]{1,0:T(8,128)(2,1)S(1)} %get-tuple-element.119), channel_id=1, source_target_pairs={{16,25},{17,24},{18,27},{19,26},{20,29},{21,28},{22,31},{23,30}} | collective-permute-start | bytes 1572872 | tf_op jit(solution)/shard_map/ppermute | solution.py:248
  64.9 1.3 %collective-permute-start.11 = (bf16[128,2048]{1,0:T(8,128)(2,1)S(1)}, bf16[128,2048]{1,0:T(8,128)(2,1)S(1)}, u32[]{:S(2)}, u32[]{:S(2)}) collective-permute-start(bf16[128,2048]{1,0:T(8,128)(2,1)S(1)} %get-tuple-element.119), channel_id=1, source_target_pairs={{16,24},{17,25},{18,26},{19,27},{20,28},{21,29},{22,30},{23,31}} | collective-permute-start | bytes 1572872 | tf_op jit(solution)/shard_map/ppermute | solution.py:248
  66.2 1.2 %collective-permute-done.10.refs_1_ = bf16[128,2048]{1,0:T(8,128)(2,1)S(1)} collective-permute-done((bf16[128,2048]{1,0:T(8,128)(2,1)S(1)}, bf16[128,2048]{1,0:T(8,128)(2,1)S(1)}, u32[]{:S(2)}, u32[]{:S(2)}) %collective-permute-start.10) | collective-permute-done | bytes 524320 | tf_op jit(solution)/shard_map/ppermute | solution.py:248
  67.5 5.6 %collective-permute-done.9.refs_0_ = bf16[128,2048]{1,0:T(8,128)(2,1)S(1)} collective-permute-done((bf16[128,2048]{1,0:T(8,128)(2,1)S(1)}, bf16[128,2048]{1,0:T(8,128)(2,1)S(1)}, u32[]{:S(2)}, u32[]{:S(2)}) %collective-permute-start.9) | collective-permute-done | bytes 524320 | tf_op jit(solution)/shard_map/ppermute | solution.py:248
  75.3 1.9 %collective-permute-start.16 = (bf16[128,1024]{1,0:T(8,128)(2,1)S(1)}, bf16[128,1024]{1,0:T(8,128)(2,1)S(1)}, u32[]{:S(2)}, u32[]{:S(2)}) collective-permute-start(bf16[128,1024]{1,0:T(8,128)(2,1)S(1)} %get-tuple-element.141), channel_id=1, source_target_pairs={{8,2},{9,3},{10,4},{11,5},{12,6},{13,7},{14,0},{15,1},{16,8},{17,9... | collective-permute-start | bytes 786440 | tf_op jit(solution)/shard_map/ppermute | solution.py:248
  77.2 1.9 %collective-permute-start.17 = (bf16[128,1024]{1,0:T(8,128)(2,1)S(1)}, bf16[128,1024]{1,0:T(8,128)(2,1)S(1)}, u32[]{:S(2)}, u32[]{:S(2)}) collective-permute-start(bf16[128,1024]{1,0:T(8,128)(2,1)S(1)} %get-tuple-element.142), channel_id=1, source_target_pairs={{8,0},{9,1},{10,2},{11,3},{12,4},{13,5},{14,6},{15,7},{16,8},{17,9... | collective-permute-start | bytes 786440 | tf_op jit(solution)/shard_map/ppermute | solution.py:248
  79.3 17.9 %collective-permute-done.16.refs_2_ = bf16[128,1024]{1,0:T(8,128)(2,1)S(1)} collective-permute-done((bf16[128,1024]{1,0:T(8,128)(2,1)S(1)}, bf16[128,1024]{1,0:T(8,128)(2,1)S(1)}, u32[]{:S(2)}, u32[]{:S(2)}) %collective-permute-start.16) | collective-permute-done | bytes 262176 | tf_op jit(solution)/shard_map/ppermute | solution.py:248
  (46 shorter events, 7.4 us)
Async XLA Ops:
  0.0 4.6 %collective-permute-start = (bf16[128,2048]{1,0:T(8,128)(2,1)}, bf16[128,2048]{1,0:T(8,128)(2,1)S(1)}, u32[]{:S(2)}, u32[]{:S(2)}) collective-permute-start(bf16[128,2048]{1,0:T(8,128)(2,1)} %bitcast.20), channel_id=1, source_target_pairs={{0,1},{1,0},{2,3},{3,2},{4,5},{5,4},{6,7},{7,6}} | collective-permute-start | bytes 1572872 | tf_op jit(solution)/shard_map/ppermute | solution.py:248
  0.7 2.2 %copy-start = (bf16[1,2048,1024]{2,1,0:T(8,128)(2,1)S(1)}, bf16[1,2048,1024]{2,1,0:T(8,128)(2,1)}, u32[]{:S(2)}) copy-start(bf16[1,2048,1024]{2,1,0:T(8,128)(2,1)} %param.6) | copy-start | bytes 12582916
  2.9 0.7 copy-start.3
  3.6 1.0 %copy-start.5 = (bf16[4,32,2048]{2,1,0:T(8,128)(2,1)S(1)}, bf16[4,32,2048]{2,1,0:T(8,128)(2,1)}, u32[]{:S(2)}) copy-start(bf16[4,32,2048]{2,1,0:T(8,128)(2,1)} %param.4) | copy-start | bytes 1572868
  4.6 2.2 %copy-start.1 = (bf16[1,2048,1024]{2,1,0:T(8,128)(2,1)S(1)}, bf16[1,2048,1024]{2,1,0:T(8,128)(2,1)}, u32[]{:S(2)}) copy-start(bf16[1,2048,1024]{2,1,0:T(8,128)(2,1)} %param.6) | copy-start | bytes 12582916
  4.6 3.5 %copy-start.2 = (bf16[1,1024,2048]{2,1,0:T(8,128)(2,1)S(1)}, bf16[1,1024,2048]{2,1,0:T(8,128)(2,1)}, u32[]{:S(2)}) copy-start(bf16[1,1024,2048]{2,1,0:T(8,128)(2,1)} %param.7) | copy-start | bytes 12582916
  8.1 3.0 %copy-start.4 = (f32[1,2048]{1,0:T(1,128)S(1)}, f32[1,2048]{1,0:T(1,128)}, u32[]{:S(2)}) copy-start(f32[1,2048]{1,0:T(1,128)} %refs_2_.11) | copy-start | bytes 24580
  8.1 3.0 %collective-permute-start.2 = (bf16[128,2048]{1,0:T(8,128)(2,1)S(1)}, bf16[128,2048]{1,0:T(8,128)(2,1)S(1)}, u32[]{:S(2)}, u32[]{:S(2)}) collective-permute-start(bf16[128,2048]{1,0:T(8,128)(2,1)S(1)} %get-tuple-element.86), channel_id=1, source_target_pairs={{0,15},{1,14},{2,9},{3,8},{4,11},{5,10},{6,13},{7,12}} | collective-permute-start | bytes 1572872 | tf_op jit(solution)/shard_map/ppermute | solution.py:248
  8.9 2.1 %collective-permute-start.1 = (bf16[128,2048]{1,0:T(8,128)(2,1)S(1)}, bf16[128,2048]{1,0:T(8,128)(2,1)S(1)}, u32[]{:S(2)}, u32[]{:S(2)}) collective-permute-start(bf16[128,2048]{1,0:T(8,128)(2,1)S(1)} %get-tuple-element.86), channel_id=1, source_target_pairs={{0,14},{1,15},{2,8},{3,9},{4,10},{5,11},{6,12},{7,13}} | collective-permute-start | bytes 1572872 | tf_op jit(solution)/shard_map/ppermute | solution.py:248
  9.7 1.5 %collective-permute-start.4 = (bf16[128,2048]{1,0:T(8,128)(2,1)S(1)}, bf16[128,2048]{1,0:T(8,128)(2,1)S(1)}, u32[]{:S(2)}, u32[]{:S(2)}) collective-permute-start(bf16[128,2048]{1,0:T(8,128)(2,1)S(1)} %get-tuple-element.88), channel_id=1, source_target_pairs={{0,9},{1,8},{2,11},{3,10},{4,13},{5,12},{6,15},{7,14}} | collective-permute-start | bytes 1572872 | tf_op jit(solution)/shard_map/ppermute | solution.py:248
  10.4 0.8 collective-permute-start.3
  11.2 34.0 %collective-permute-start.7 = (bf16[128,2048]{1,0:T(8,128)(2,1)S(1)}, bf16[128,2048]{1,0:T(8,128)(2,1)S(1)}, u32[]{:S(2)}, u32[]{:S(2)}) collective-permute-start(bf16[128,2048]{1,0:T(8,128)(2,1)S(1)} %get-tuple-element.103), channel_id=1, source_target_pairs={{8,18},{9,19},{10,20},{11,21},{12,22},{13,23},{14,16},{15,17}} | collective-permute-start | bytes 1572872 | tf_op jit(solution)/shard_map/ppermute | solution.py:248
  12.5 37.2 %collective-permute-start.6 = (bf16[128,2048]{1,0:T(8,128)(2,1)S(1)}, bf16[128,2048]{1,0:T(8,128)(2,1)S(1)}, u32[]{:S(2)}, u32[]{:S(2)}) collective-permute-start(bf16[128,2048]{1,0:T(8,128)(2,1)S(1)} %get-tuple-element.100), channel_id=1, source_target_pairs={{8,17},{9,16},{10,19},{11,18},{12,21},{13,20},{14,23},{15,22}} | collective-permute-start | bytes 1572872 | tf_op jit(solution)/shard_map/ppermute | solution.py:248
  13.8 39.9 %collective-permute-start.5 = (bf16[128,2048]{1,0:T(8,128)(2,1)S(1)}, bf16[128,2048]{1,0:T(8,128)(2,1)S(1)}, u32[]{:S(2)}, u32[]{:S(2)}) collective-permute-start(bf16[128,2048]{1,0:T(8,128)(2,1)S(1)} %get-tuple-element.100), channel_id=1, source_target_pairs={{8,16},{9,17},{10,18},{11,19},{12,20},{13,21},{14,22},{15,23}} | collective-permute-start | bytes 1572872 | tf_op jit(solution)/shard_map/ppermute | solution.py:248
  45.2 11.7 %collective-permute-start.8 = (bf16[128,2048]{1,0:T(8,128)(2,1)S(1)}, bf16[128,2048]{1,0:T(8,128)(2,1)S(1)}, u32[]{:S(2)}, u32[]{:S(2)}) collective-permute-start(bf16[128,2048]{1,0:T(8,128)(2,1)S(1)} %after.2.refs_0_), channel_id=1, source_target_pairs={{16,17},{17,16},{18,19},{19,18},{20,21},{21,20},{22,23},{23,22}} | collective-permute-start | bytes 1572872 | tf_op jit(solution)/shard_map/ppermute | solution.py:248
  59.5 8.0 %collective-permute-start.10 = (bf16[128,2048]{1,0:T(8,128)(2,1)S(1)}, bf16[128,2048]{1,0:T(8,128)(2,1)S(1)}, u32[]{:S(2)}, u32[]{:S(2)}) collective-permute-start(bf16[128,2048]{1,0:T(8,128)(2,1)S(1)} %get-tuple-element.116), channel_id=1, source_target_pairs={{16,31},{17,30},{18,25},{19,24},{20,27},{21,26},{22,29},{23,28}} | collective-permute-start | bytes 1572872 | tf_op jit(solution)/shard_map/ppermute | solution.py:248
  60.8 12.3 %collective-permute-start.9 = (bf16[128,2048]{1,0:T(8,128)(2,1)S(1)}, bf16[128,2048]{1,0:T(8,128)(2,1)S(1)}, u32[]{:S(2)}, u32[]{:S(2)}) collective-permute-start(bf16[128,2048]{1,0:T(8,128)(2,1)S(1)} %get-tuple-element.116), channel_id=1, source_target_pairs={{16,30},{17,31},{18,24},{19,25},{20,26},{21,27},{22,28},{23,29}} | collective-permute-start | bytes 1572872 | tf_op jit(solution)/shard_map/ppermute | solution.py:248
  63.6 9.6 %collective-permute-start.12 = (bf16[128,2048]{1,0:T(8,128)(2,1)S(1)}, bf16[128,2048]{1,0:T(8,128)(2,1)S(1)}, u32[]{:S(2)}, u32[]{:S(2)}) collective-permute-start(bf16[128,2048]{1,0:T(8,128)(2,1)S(1)} %get-tuple-element.119), channel_id=1, source_target_pairs={{16,25},{17,24},{18,27},{19,26},{20,29},{21,28},{22,31},{23,30}} | collective-permute-start | bytes 1572872 | tf_op jit(solution)/shard_map/ppermute | solution.py:248
  64.9 8.2 %collective-permute-start.11 = (bf16[128,2048]{1,0:T(8,128)(2,1)S(1)}, bf16[128,2048]{1,0:T(8,128)(2,1)S(1)}, u32[]{:S(2)}, u32[]{:S(2)}) collective-permute-start(bf16[128,2048]{1,0:T(8,128)(2,1)S(1)} %get-tuple-element.119), channel_id=1, source_target_pairs={{16,24},{17,25},{18,26},{19,27},{20,28},{21,29},{22,30},{23,31}} | collective-permute-start | bytes 1572872 | tf_op jit(solution)/shard_map/ppermute | solution.py:248
  73.3 6.0 %collective-permute-start.15 = (bf16[128,1024]{1,0:T(8,128)(2,1)S(1)}, bf16[128,1024]{1,0:T(8,128)(2,1)S(1)}, u32[]{:S(2)}, u32[]{:S(2)}) collective-permute-start(bf16[128,1024]{1,0:T(8,128)(2,1)S(1)} %get-tuple-element.137), channel_id=1, source_target_pairs={{24,25},{25,24},{26,27},{27,26},{28,29},{29,28},{30,31},{31,30}} | collective-permute-start | bytes 786440 | tf_op jit(solution)/shard_map/ppermute | solution.py:248
  73.9 5.2 %collective-permute-start.13 = (bf16[128,1024]{1,0:T(8,128)(2,1)S(1)}, bf16[128,1024]{1,0:T(8,128)(2,1)S(1)}, u32[]{:S(2)}, u32[]{:S(2)}) collective-permute-start(bf16[128,1024]{1,0:T(8,128)(2,1)S(1)} %get-tuple-element.132), channel_id=1, source_target_pairs={{24,26},{25,27},{26,28},{27,29},{28,30},{29,31},{30,24},{31,25}} | collective-permute-start | bytes 786440 | tf_op jit(solution)/shard_map/ppermute | solution.py:248
  74.6 4.6 %collective-permute-start.14 = (bf16[128,1024]{1,0:T(8,128)(2,1)S(1)}, bf16[128,1024]{1,0:T(8,128)(2,1)S(1)}, u32[]{:S(2)}, u32[]{:S(2)}) collective-permute-start(bf16[128,1024]{1,0:T(8,128)(2,1)S(1)} %get-tuple-element.133), channel_id=1, source_target_pairs={{24,27},{25,26},{26,29},{27,28},{28,31},{29,30},{30,25},{31,24}} | collective-permute-start | bytes 786440 | tf_op jit(solution)/shard_map/ppermute | solution.py:248
  75.3 21.9 %collective-permute-start.16 = (bf16[128,1024]{1,0:T(8,128)(2,1)S(1)}, bf16[128,1024]{1,0:T(8,128)(2,1)S(1)}, u32[]{:S(2)}, u32[]{:S(2)}) collective-permute-start(bf16[128,1024]{1,0:T(8,128)(2,1)S(1)} %get-tuple-element.141), channel_id=1, source_target_pairs={{8,2},{9,3},{10,4},{11,5},{12,6},{13,7},{14,0},{15,1},{16,8},{17,9... | collective-permute-start | bytes 786440 | tf_op jit(solution)/shard_map/ppermute | solution.py:248
  77.2 20.0 %collective-permute-start.17 = (bf16[128,1024]{1,0:T(8,128)(2,1)S(1)}, bf16[128,1024]{1,0:T(8,128)(2,1)S(1)}, u32[]{:S(2)}, u32[]{:S(2)}) collective-permute-start(bf16[128,1024]{1,0:T(8,128)(2,1)S(1)} %get-tuple-element.142), channel_id=1, source_target_pairs={{8,0},{9,1},{10,2},{11,3},{12,4},{13,5},{14,6},{15,7},{16,8},{17,9... | collective-permute-start | bytes 786440 | tf_op jit(solution)/shard_map/ppermute | solution.py:248

commit v3 on v2

--- a/solution.py
+++ b/solution.py
@@ -59,12 +59,11 @@
             kept[...] = before[...]
 
 
-def project(section, chunk_order, parts, mark, scale, weight, before):
+def project(section, chunk_order, parts, mark, scale, weight, keep="", before=()):
     rows, width = parts[0].shape
     channels = weight.shape[1]
-    keep = "" if section == 0 else "start" if before is None else "hand on"
     shapes = [(rows, width)] + [(rows, channels)] * (4 if keep else 3)
-    arrays = [*parts, scale, weight] + ([before] if keep == "hand on" else [])
+    arrays = [*parts, scale, weight, *before]
     return pl.pallas_call(
         functools.partial(project_kernel, section, chunk_order, len(parts), keep),
         out_shape=tuple(jax.ShapeDtypeStruct(shape, jnp.bfloat16) for shape in shapes) + (MARK,),
@@ -83,10 +82,11 @@
     return jnp.concatenate(values, axis=axis) if len(values) > 1 else values[0]
 
 
-def attend_kernel(section, pieces, n_blocks, split, mark, *refs):
+def attend_kernel(section, pieces, n_blocks, split, carry, copies, mark, *refs):
     blocks, refs = refs[: 4 * n_blocks], refs[4 * n_blocks :]
     xs, qs, ks, vs = (blocks[i * n_blocks : (i + 1) * n_blocks] for i in range(4))
     weight, refs = refs[0], refs[1:]
+    kept, refs = refs[:carry], refs[carry:]
     outs, o_ref = refs[:-2], refs[-1]
     channels = qs[0].shape[1]
     width = xs[0].shape[1]
@@ -140,22 +140,44 @@
                     rows = slice(0, size)
                 out[rows, put_lanes] = value.astype(out.dtype)
                 at += size
-
-
-def attend(section, pieces, blocks, mark, weight, split):
+        for turn in range(1, copies):
+            block = lax.rem(lax.axis_index("head") + turn, n_head)
+            lanes = pl.ds(pl.multiple_of(block * channels, channels), channels)
+            outs[turn][...] = outs[0][:, lanes]
+
+    if copies:
+
+        @pl.when(lax.axis_index("pipe") != section)
+        def _():
+            outs[1][...] = kept[0][...]
+
+    elif carry:
+        rows = o_ref.shape[0]
+        outs[0][rows:, :] = kept[1][...]
+
+        @pl.when(lax.axis_index("pipe") != section)
+        def _():
+            outs[0][:rows, :] = kept[0][...]
+
+
+def attend(section, pieces, blocks, mark, weight, split, kept=(), share=False):
     rows = sum(size for _, _, size in pieces)
     channels, width = weight.shape
     keys = sum(block[2].shape[0] for block in blocks)
     n_head = width // channels
     if split:
-        out_shape = tuple(jax.ShapeDtypeStruct((rows, channels), jnp.bfloat16) for _ in range(n_head))
+        out_shape = tuple(
+            jax.ShapeDtypeStruct((rows * (2 if kept and turn == 0 else 1), channels), jnp.bfloat16)
+            for turn in range(n_head)
+        )
     else:
         out_shape = (jax.ShapeDtypeStruct((rows, width), jnp.bfloat16),)
-    arrays = [block[i] for i in range(4) for block in blocks]
-    return pl.pallas_call(
-        functools.partial(attend_kernel, section, pieces, len(blocks), split),
+        out_shape += (jax.ShapeDtypeStruct((rows, channels), jnp.bfloat16),) * (n_head - 1 if share else 0)
+    arrays = [block[i] for i in range(4) for block in blocks] + [weight, *kept]
+    return pl.pallas_call(
+        functools.partial(attend_kernel, section, pieces, len(blocks), split, len(kept), n_head if share else 0),
         out_shape=out_shape + (MARK,),
-        in_specs=[anywhere] + [vmem] * (len(arrays) + 1),
+        in_specs=[anywhere] + [vmem] * len(arrays),
         out_specs=(vmem,) * len(out_shape) + (anywhere,),
         scratch_shapes=[pltpu.VMEM((rows, channels), jnp.bfloat16)],
         compiler_params=pltpu.CompilerParams(vmem_limit_bytes=VMEM_LIMIT),
@@ -165,84 +187,110 @@
             transcendentals=rows * keys * channels // HEAD_DIM,
         ),
         name="attend",
-    )(mark, *arrays, weight)
-
-
-def add_kernel(section, mark, *refs):
+    )(mark, *arrays)
+
+
+def add_kernel(section, n_before, mark, *refs):
     @pl.when(lax.axis_index("pipe") == section)
     def _():
-        total = refs[0][...].astype(jnp.float32)
-        for term in refs[1:-2]:
-            total = total + term[...].astype(jnp.float32)
-        refs[-2][...] = total.astype(refs[-2].dtype)
-
-
-def add(section, terms, mark):
-    return pl.pallas_call(
-        functools.partial(add_kernel, section),
-        out_shape=(jax.ShapeDtypeStruct(terms[0].shape, terms[0].dtype), MARK),
-        in_specs=[anywhere] + [vmem] * len(terms),
+        before, terms, out = refs[:n_before], refs[n_before:-2], refs[-2]
+        rows = out.shape[0] - sum(block.shape[0] for block in before)
+        total = terms[0][:rows, :].astype(jnp.float32)
+        for term in terms[1:]:
+            total = total + term[:rows, :].astype(jnp.float32)
+        for block in before:
+            out[: block.shape[0], :] = block[...]
+        out[out.shape[0] - rows :, :] = total.astype(out.dtype)
+
+
+def add(section, terms, mark, flops=0, before=()):
+    rows, width = min(term.shape for term in terms)
+    rows += sum(block.shape[0] for block in before)
+    return pl.pallas_call(
+        functools.partial(add_kernel, section, len(before)),
+        out_shape=(jax.ShapeDtypeStruct((rows, width), terms[0].dtype), MARK),
+        in_specs=[anywhere] + [vmem] * (len(before) + len(terms)),
         out_specs=(vmem, anywhere),
         compiler_params=pltpu.CompilerParams(vmem_limit_bytes=VMEM_LIMIT),
+        cost_estimate=pl.CostEstimate(flops=flops, bytes_accessed=flops // 100, transcendentals=0),
         name="add",
-    )(mark, *terms)
-
-
-def finish_kernel(section, *refs):
-    sums, backs, out = refs[:2], refs[2:4], refs[4]
+    )(mark, *before, *terms)
+
+
+def finish_kernel(last, total, second, share, *refs):
+    shared, out = refs[:-1], refs[-1]
     shape = (out.shape[0], HALF, out.shape[2])
-    for choice, halves in ((lax.axis_index("pipe") == section, sums), (lax.axis_index("pipe") != section, backs)):
-
-        @pl.when(choice)
-        def _():
-            for half in range(2):
-                out[:, half * HALF : (half + 1) * HALF, :] = halves[half][...].reshape(shape)
-
-
-def finish(section, row_count, mark, moved, backs):
-    channels = backs[0].shape[1]
-    sums = []
-    for terms in moved:
-        total, mark = add(section, terms, mark)
-        sums.append(total)
-    return pl.pallas_call(
-        functools.partial(finish_kernel, section),
-        out_shape=jax.ShapeDtypeStruct((row_count, WIN, channels), jnp.bfloat16),
-        in_specs=[vmem] * 4,
+    rows, channels = shared[0].shape
+    stage = lax.axis_index("pipe")
+    first_half, second_half = (slice(half * HALF, (half + 1) * HALF) for half in range(2))
+
+    @pl.when(stage == last)
+    def _():
+        out[:, first_half, :] = total[:rows, :].reshape(shape)
+        out[:, second_half, :] = total[rows:, :].reshape(shape)
+
+    @pl.when(stage != last)
+    def _():
+        out[:, second_half, :] = second[rows:, :].reshape(shape)
+
+    @pl.when((stage < last - 1) & (stage % 2 == 0))
+    def _():
+        out[:, first_half, :] = shared[0][...].reshape(shape)
+
+    @pl.when((stage < last - 1) & (stage % 2 == 1))
+    def _():
+        out[:, first_half, :] = second[:rows, :].reshape(shape)
+
+    @pl.when(stage == last - 1)
+    def _():
+        mine = pl.ds(pl.multiple_of(lax.axis_index("head") * channels, channels), channels)
+        value = share[:, mine].astype(jnp.float32)
+        for term in shared:
+            value = value + term[...].astype(jnp.float32)
+        out[:, first_half, :] = value.astype(out.dtype).reshape(shape)
+
+
+def finish(last, row_count, total, second, share, shared):
+    arrays = [total, second, share, *shared]
+    return pl.pallas_call(
+        functools.partial(finish_kernel, last),
+        out_shape=jax.ShapeDtypeStruct((row_count, WIN, total.shape[1]), jnp.bfloat16),
+        in_specs=[vmem] * len(arrays),
         out_specs=vmem,
         compiler_params=pltpu.CompilerParams(vmem_limit_bytes=VMEM_LIMIT),
         name="finish",
-    )(*sums, *backs)
-
-
-def after(arrays, mark):
+    )(*arrays)
+
+
+def after(arrays, *marks):
     shapes = tuple(jax.ShapeDtypeStruct(array.shape, array.dtype) for array in arrays)
     return pl.pallas_call(
         lambda *refs: None,
         out_shape=shapes,
-        in_specs=[anywhere] * (len(arrays) + 1),
+        in_specs=[anywhere] * (len(arrays) + len(marks)),
         out_specs=(anywhere,) * len(arrays),
         input_output_aliases={place: place for place in range(len(arrays))},
         compiler_params=pltpu.CompilerParams(vmem_limit_bytes=1024 * 1024),
         name="after",
-    )(*arrays, mark)
+    )(*arrays, *marks)
 
 
 def per_device(stream, score_scale, value_weight, out_weight):
     row_count, col_count, width = stream.shape
     assert col_count == WIN, "one window"
     sections, n_win, n_head = (lax.axis_size(axis) for axis in AXES)
+    assert sections % 2 == 0, "section pairs"
     value_cols, out_rows = value_weight[0], out_weight[0]
     places = [(win, group) for win in range(n_win) for group in range(n_head)]
 
     def send(value, start, stop, over=0, turn=0):
-        return send_all(value, [(start, stop)], [over], turn)
-
-    def send_all(value, hops, overs, turn=0):
+        return send_all(value, [(start, stop, over, turn)])
+
+    def send_all(value, hops):
         at = lambda pipe, win, group: (pipe * n_win + win % n_win) * n_head + group % n_head
         pairs = [
             (at(start, win, group), at(stop, win + over, group + turn))
-            for (start, stop), over in zip(hops, overs)
+            for start, stop, over, turn in hops
             for win, group in places
         ]
         return lax.ppermute(value, AXES, pairs)
@@ -256,48 +304,66 @@
     mark = jnp.zeros(MARK.shape, MARK.dtype)
     blocks = []
     for cells in arrived:
-        *block, mark = project(0, natural, [cells], mark, score_scale, value_cols, None)
+        *block, mark = project(0, natural, [cells], mark, score_scale, value_cols)
         blocks.append(block)
     halves = [[(block, half * piece, piece) for block in range(n_head)] for half in range(2)]
     straight = tuple(range(row_count * n_head))
     kept = [None, None]
+    back = [(source, source - 1, 0, 0) for source in range(1, sections)]
 
     for section in range(sections):
         shift = section % 2
         last = section + 1 == sections
+        idle = (section + 2) % sections
         moved = []
         for half in range(2):
-            *part, mark = attend(section, halves[half], blocks, mark, out_rows, last)
+            share = section + 2 == sections and not half
+            carried = kept[:1] if share else kept if last and half else []
+            if last and half:
+                (mark,) = after([mark], *early)
+            *part, mark = attend(section, halves[half], blocks, mark, out_rows, last, carried, share)
+            if share:
+                own_share, *shared = part
             cross = 0 if half else shift if last else 1 if shift else -1
-            if last:
-                terms = [
-                    send(block, section, section, cross, turn) if cross or turn else block
-                    for turn, block in enumerate(part)
-                ]
+            if last and half:
+                terms = [send(part[turn], section, section - 1, 0, turn) for turn in range(1, n_head)]
+                terms += [send_all(part[0], back)]
+            elif last:
+                terms = [send(part[turn], section, section - 1, cross, turn) for turn in range(n_head)]
             elif shift and not half:
-                terms = [send(part[0], section, section + 1, cross)]
+                terms = [send(part[0], section, idle, cross)]
+            elif shift:
+                terms = [send(part[0], section, section - 1, 0, turn) for turn in range(n_head)]
             else:
                 terms = [send(part[0], section, section + 1, cross, turn) for turn in range(n_head)]
             moved.append(terms)
         if shift and not last:
             (one,) = after(moved[0], mark)
-            moved[0] = [one] + [
-                send(one, section + 1, section + 1, 0, turn) for turn in range(1, n_head)
+            moved[0] = [send(one, idle, section + 1, 0, turn) for turn in range(n_head)]
+            total, mark = add(section - 1, moved[1], mark)
+            moved[1] = [send(total, section - 1, section + 1)]
+        if section + 2 == sections:
+            across = [(source, source - 1, 1, 0) for source in range(1, section, 2)]
+            early = [
+                send_all(block, ([] if turn else across) + [(section, section, 0, turn + 1)])
+                for turn, block in enumerate(after(shared, mark))
             ]
         if not last:
             blocks = [None, None]
-            for half in (1, 0) if shift else (0, 1):
-                *blocks[half], kept[half], mark = project(
-                    section + 1, straight, moved[half], mark, score_scale, value_cols, kept[half]
+            for half in range(2):
+                keep = "" if section + 2 == sections and not half else "hand on" if section else "start"
+                before = [kept[half]] if keep == "hand on" else []
+                *blocks[half], mark = project(
+                    section + 1, straight, moved[half], mark, score_scale, value_cols, keep, before
                 )
+                if keep:
+                    *blocks[half], kept[half] = blocks[half]
             halves = [[(0, 0, piece * n_head)], [(1, 0, piece * n_head)]]
-    hops = [(source, source - 1) for source in range(1, sections)]
-    kept = after(kept, mark)
-    backs = [
-        send_all(kept[half], hops, [0 if half else source % 2 for source, _ in hops])
-        for half in range(2)
-    ]
-    return finish(sections - 1, row_count * n_head, mark, moved, backs)[None]
+    first, mark = add(sections - 2, moved[0], mark, 4 * 10**9)
+    second, mark = add(sections - 2, moved[1][:-1], mark, 4 * 10**9)
+    total, mark = add(sections - 2, [second, moved[1][-1]], mark, 0, (first,))
+    total = send(total, sections - 2, sections - 1)
+    return finish(sections - 1, row_count * n_head, total, moved[1][-1], own_share, early)[None]
 
 
 def solution(mesh):

time: 98.5 us -> 93.1 us (0.945)
  the two profiles are of different devices: /device:TPU:4 before, /device:TPU:5 now
where the time goes in v3:
time: 93.1 us; the launch traced here: 92.2 us
  waiting for transfers between devices  56.3 us (60%)
  starting transfers between devices  22 us (24%)
  local copies, waits for them, and re-layouts  7.38 us (8%)
  Pallas kernels  6.13 us (7%)
    ppermute x21, waiting for transfers between devices, send_all(): return lax.ppermute(value, AXES, pairs)  56.3 us
    ppermute x21, starting transfers between devices, send_all(): return lax.ppermute(value, AXES, pairs)  22 us
    unnamed x12, local copies, waits for them, and re-layouts  7.38 us
    pallas_call x8, Pallas kernels, attend(): pl.pallas_call(functools.partial(attend_kernel, section, pieces, len(bloc...  3.09 us
    pallas_call x8, Pallas kernels, project(): pl.pallas_call(functools.partial(project_kernel, section, chunk_order, le...  2.17 us
  transfers between devices with their start and end apart: 21, of which 7 were waited for; matrix products, arithmetic and copies ran while one was open for 0% of the time, Pallas kernels for 5%

profile of v3, /device:TPU:5, one launch (start us, length us, event | category | flops | bytes accessed | tf_op | source)
XLA Modules:
  0.0 92.2 jit_solution(14960413410805897265)
XLA Ops:
  0.7 2.2 %copy-done = bf16[1,2048,1024]{2,1,0:T(8,128)(2,1)S(1)} copy-done((bf16[1,2048,1024]{2,1,0:T(8,128)(2,1)S(1)}, bf16[1,2048,1024]{2,1,0:T(8,128)(2,1)}, u32[]{:S(2)}) %copy-start) | copy-done | bytes 4194328
  4.6 2.2 %copy-done.1 = bf16[1,2048,1024]{2,1,0:T(8,128)(2,1)S(1)} copy-done((bf16[1,2048,1024]{2,1,0:T(8,128)(2,1)S(1)}, bf16[1,2048,1024]{2,1,0:T(8,128)(2,1)}, u32[]{:S(2)}) %copy-start.1) | copy-done | bytes 4194328
  6.8 1.3 %copy-done.2 = bf16[1,1024,2048]{2,1,0:T(8,128)(2,1)S(1)} copy-done((bf16[1,1024,2048]{2,1,0:T(8,128)(2,1)S(1)}, bf16[1,1024,2048]{2,1,0:T(8,128)(2,1)}, u32[]{:S(2)}) %copy-start.2) | copy-done | bytes 4194328
  11.2 1.3 %collective-permute-start.7 = (bf16[128,2048]{1,0:T(8,128)(2,1)S(1)}, bf16[128,2048]{1,0:T(8,128)(2,1)S(1)}, u32[]{:S(2)}, u32[]{:S(2)}) collective-permute-start(bf16[128,2048]{1,0:T(8,128)(2,1)S(1)} %get-tuple-element.104), channel_id=1, source_target_pairs={{8,26},{9,27},{10,28},{11,29},{12,30},{13,31},{14,24},{15,25}} | collective-permute-start | bytes 1572872 | tf_op jit(solution)/shard_map/ppermute | solution.py:296
  13.9 28.5 %collective-permute-done.7.refs_0_ = bf16[128,2048]{1,0:T(8,128)(2,1)S(1)} collective-permute-done((bf16[128,2048]{1,0:T(8,128)(2,1)S(1)}, bf16[128,2048]{1,0:T(8,128)(2,1)S(1)}, u32[]{:S(2)}, u32[]{:S(2)}) %collective-permute-start.7) | collective-permute-done | bytes 524320 | tf_op jit(solution)/shard_map/ppermute | solution.py:296
  42.4 1.3 %collective-permute-start.9 = (bf16[128,2048]{1,0:T(8,128)(2,1)S(1)}, bf16[128,2048]{1,0:T(8,128)(2,1)S(1)}, u32[]{:S(2)}, u32[]{:S(2)}) collective-permute-start(bf16[128,2048]{1,0:T(8,128)(2,1)S(1)} %after.3), channel_id=1, source_target_pairs={{24,17},{25,16},{26,19},{27,18},{28,21},{29,20},{30,23},{31,22}} | collective-permute-start | bytes 1572872 | tf_op jit(solution)/shard_map/ppermute | solution.py:296
  43.8 1.3 %collective-permute-start.8 = (bf16[128,2048]{1,0:T(8,128)(2,1)S(1)}, bf16[128,2048]{1,0:T(8,128)(2,1)S(1)}, u32[]{:S(2)}, u32[]{:S(2)}) collective-permute-start(bf16[128,2048]{1,0:T(8,128)(2,1)S(1)} %after.3), channel_id=1, source_target_pairs={{24,16},{25,17},{26,18},{27,19},{28,20},{29,21},{30,22},{31,23}} | collective-permute-start | bytes 1572872 | tf_op jit(solution)/shard_map/ppermute | solution.py:296
  45.8 4.0 %collective-permute-done.9.refs_1_ = bf16[128,2048]{1,0:T(8,128)(2,1)S(1)} collective-permute-done((bf16[128,2048]{1,0:T(8,128)(2,1)S(1)}, bf16[128,2048]{1,0:T(8,128)(2,1)S(1)}, u32[]{:S(2)}, u32[]{:S(2)}) %collective-permute-start.9) | collective-permute-done | bytes 524320 | tf_op jit(solution)/shard_map/ppermute | solution.py:296
  50.1 1.3 %collective-permute-start.12 = (bf16[128,2048]{1,0:T(8,128)(2,1)S(1)}, bf16[128,2048]{1,0:T(8,128)(2,1)S(1)}, u32[]{:S(2)}, u32[]{:S(2)}) collective-permute-start(bf16[128,2048]{1,0:T(8,128)(2,1)S(1)} %get-tuple-element.121.share), channel_id=1, source_target_pairs={{16,31},{17,30},{18,25},{19,24},{20,27},{21,26},{22,29},{23,28}} | collective-permute-start | bytes 1572872 | tf_op jit(solution)/shard_map/ppermute | solution.py:296
  51.4 1.3 %collective-permute-start.11 = (bf16[128,2048]{1,0:T(8,128)(2,1)S(1)}, bf16[128,2048]{1,0:T(8,128)(2,1)S(1)}, u32[]{:S(2)}, u32[]{:S(2)}) collective-permute-start(bf16[128,2048]{1,0:T(8,128)(2,1)S(1)} %get-tuple-element.121.share), channel_id=1, source_target_pairs={{16,30},{17,31},{18,24},{19,25},{20,26},{21,27},{22,28},{23,29}} | collective-permute-start | bytes 1572872 | tf_op jit(solution)/shard_map/ppermute | solution.py:296
  52.8 1.3 %collective-permute-start.14 = (bf16[128,2048]{1,0:T(8,128)(2,1)S(1)}, bf16[128,2048]{1,0:T(8,128)(2,1)S(1)}, u32[]{:S(2)}, u32[]{:S(2)}) collective-permute-start(bf16[128,2048]{1,0:T(8,128)(2,1)S(1)} %get-tuple-element.123), channel_id=1, source_target_pairs={{16,25},{17,24},{18,27},{19,26},{20,29},{21,28},{22,31},{23,30}} | collective-permute-start | bytes 1572872 | tf_op jit(solution)/shard_map/ppermute | solution.py:296
  54.1 1.3 %collective-permute-start.13 = (bf16[128,2048]{1,0:T(8,128)(2,1)S(1)}, bf16[128,2048]{1,0:T(8,128)(2,1)S(1)}, u32[]{:S(2)}, u32[]{:S(2)}) collective-permute-start(bf16[128,2048]{1,0:T(8,128)(2,1)S(1)} %get-tuple-element.123), channel_id=1, source_target_pairs={{16,24},{17,25},{18,26},{19,27},{20,28},{21,29},{22,30},{23,31}} | collective-permute-start | bytes 1572872 | tf_op jit(solution)/shard_map/ppermute | solution.py:296
  56.1 10.5 %collective-permute-done.12.refs_1_ = bf16[128,2048]{1,0:T(8,128)(2,1)S(1)} collective-permute-done((bf16[128,2048]{1,0:T(8,128)(2,1)S(1)}, bf16[128,2048]{1,0:T(8,128)(2,1)S(1)}, u32[]{:S(2)}, u32[]{:S(2)}) %collective-permute-start.12) | collective-permute-done | bytes 524320 | tf_op jit(solution)/shard_map/ppermute | solution.py:296
  66.5 6.0 %collective-permute-done.11.refs_0_ = bf16[128,2048]{1,0:T(8,128)(2,1)S(1)} collective-permute-done((bf16[128,2048]{1,0:T(8,128)(2,1)S(1)}, bf16[128,2048]{1,0:T(8,128)(2,1)S(1)}, u32[]{:S(2)}, u32[]{:S(2)}) %collective-permute-start.11) | collective-permute-done | bytes 524320 | tf_op jit(solution)/shard_map/ppermute | solution.py:296
  73.6 1.1 %project.15 = (bf16[128,2048]{1,0:T(8,128)(2,1)S(1)}, bf16[128,1024]{1,0:T(8,128)(2,1)S(1)}, bf16[128,1024]{1,0:T(8,128)(2,1)S(1)}, bf16[128,1024]{1,0:T(8,128)(...) custom-call(f32[8,128]{1,0:T(8,128)S(1)} %get-tuple-element.122.mark, ...), custom_call_target="tpu_custom_call" | custom-call | flops 536870912 | bytes 4194304 | tf_op jit(solution)/shard_map/project/pallas_call | solution.py:67
  74.6 1.4 %attend.14 = (bf16[128,1024]{1,0:T(8,128)(2,1)S(1)}, bf16[128,1024]{1,0:T(8,128)(2,1)S(1)}, f32[8,128]{1,0:T(8,128)S(1)}) custom-call(f32[8,128]{1,0:T(8,128)S(1)} %get-tuple-element.125.mark, bf16[128,2048]{1,0:T(8,128)(2,1)S(1)} %get-tuple-element.126.refs_0_, bf16[128,2048]{1,0:T(8,128)(2,1)S(1)} %get-tuple-element.127.refs_1_, ...), custom_call_target="tpu_custom_call" | custom-call | flops 671088640 | bytes 4194304 | tf_op jit(solution)/shard_map/attend/pallas_call | solution.py:177
  76.0 1.3 %collective-permute-start.16 = (bf16[128,1024]{1,0:T(8,128)(2,1)S(1)}, bf16[128,1024]{1,0:T(8,128)(2,1)S(1)}, u32[]{:S(2)}, u32[]{:S(2)}) collective-permute-start(bf16[128,1024]{1,0:T(8,128)(2,1)S(1)} %get-tuple-element.138), channel_id=1, source_target_pairs={{24,18},{25,19},{26,20},{27,21},{28,22},{29,23},{30,16},{31,17}} | collective-permute-start | bytes 786440 | tf_op jit(solution)/shard_map/ppermute | solution.py:296
  77.3 1.3 %collective-permute-start.17 = (bf16[128,1024]{1,0:T(8,128)(2,1)S(1)}, bf16[128,1024]{1,0:T(8,128)(2,1)S(1)}, u32[]{:S(2)}, u32[]{:S(2)}) collective-permute-start(bf16[128,1024]{1,0:T(8,128)(2,1)S(1)} %get-tuple-element.139), channel_id=1, source_target_pairs={{24,19},{25,18},{26,21},{27,20},{28,23},{29,22},{30,17},{31,16}} | collective-permute-start | bytes 786440 | tf_op jit(solution)/shard_map/ppermute | solution.py:296
  78.7 1.4 %attend.15 = (bf16[256,1024]{1,0:T(8,128)(2,1)S(1)}, bf16[128,1024]{1,0:T(8,128)(2,1)S(1)}, f32[8,128]{1,0:T(8,128)S(1)}) custom-call(f32[8,128]{1,0:T(8,128)S(1)} %after.5.mark, bf16[128,2048]{1,0:T(8,128)(2,1)S(1)} %get-tuple-element.126.refs_0_, bf16[128,2048]{1,0:T(8,128)(2,1)S(1)} %get-tuple-element.127.refs_1_, ...), custom_call_target="tpu_custom_call" | custom-call | flops 671088640 | bytes 4194304 | tf_op jit(solution)/shard_map/attend/pallas_call | solution.py:177
  80.1 1.3 %collective-permute-start.18 = (bf16[128,1024]{1,0:T(8,128)(2,1)S(1)}, bf16[128,1024]{1,0:T(8,128)(2,1)S(1)}, u32[]{:S(2)}, u32[]{:S(2)}) collective-permute-start(bf16[128,1024]{1,0:T(8,128)(2,1)S(1)} %get-tuple-element.141), channel_id=1, source_target_pairs={{24,17},{25,16},{26,19},{27,18},{28,21},{29,20},{30,23},{31,22}} | collective-permute-start | bytes 786440 | tf_op jit(solution)/shard_map/ppermute | solution.py:296
  81.4 1.3 %collective-permute-start.19 = (bf16[256,1024]{1,0:T(8,128)(2,1)S(1)}, bf16[256,1024]{1,0:T(8,128)(2,1)S(1)}, u32[]{:S(2)}, u32[]{:S(2)}) collective-permute-start(bf16[256,1024]{1,0:T(8,128)(2,1)S(1)} %get-tuple-element.145), channel_id=1, source_target_pairs={{8,0},{9,1},{10,2},{11,3},{12,4},{13,5},{14,6},{15,7},{16,8},{17,9... | collective-permute-start | bytes 1572872 | tf_op jit(solution)/shard_map/ppermute | solution.py:296
  83.4 4.1 %collective-permute-done.18.refs_0_ = bf16[128,1024]{1,0:T(8,128)(2,1)S(1)} collective-permute-done((bf16[128,1024]{1,0:T(8,128)(2,1)S(1)}, bf16[128,1024]{1,0:T(8,128)(2,1)S(1)}, u32[]{:S(2)}, u32[]{:S(2)}) %collective-permute-start.18) | collective-permute-done | bytes 262176 | tf_op jit(solution)/shard_map/ppermute | solution.py:296
  87.5 1.3 %collective-permute-start.20 = (bf16[256,1024]{1,0:T(8,128)(2,1)S(1)}, bf16[256,1024]{1,0:T(8,128)(2,1)S(1)}, u32[]{:S(2)}, u32[]{:S(2)}) collective-permute-start(bf16[256,1024]{1,0:T(8,128)(2,1)S(1)} %get-tuple-element.146), channel_id=1, source_target_pairs={{16,24},{17,25},{18,26},{19,27},{20,28},{21,29},{22,30},{23,31}} | collective-permute-start | bytes 1572872 | tf_op jit(solution)/shard_map/ppermute | solution.py:296
  88.8 2.6 %collective-permute-done.20.total = bf16[256,1024]{1,0:T(8,128)(2,1)S(1)} collective-permute-done((bf16[256,1024]{1,0:T(8,128)(2,1)S(1)}, bf16[256,1024]{1,0:T(8,128)(2,1)S(1)}, u32[]{:S(2)}, u32[]{:S(2)}) %collective-permute-start.20) | collective-permute-done | bytes 524320 | tf_op jit(solution)/shard_map/ppermute | solution.py:296
  (55 shorter events, 11.1 us)
Async XLA Ops:
  0.0 4.6 %collective-permute-start = (bf16[128,2048]{1,0:T(8,128)(2,1)}, bf16[128,2048]{1,0:T(8,128)(2,1)S(1)}, u32[]{:S(2)}, u32[]{:S(2)}) collective-permute-start(bf16[128,2048]{1,0:T(8,128)(2,1)} %bitcast.20), channel_id=1, source_target_pairs={{0,1},{1,0},{2,3},{3,2},{4,5},{5,4},{6,7},{7,6}} | collective-permute-start | bytes 1572872 | tf_op jit(solution)/shard_map/ppermute | solution.py:296
  0.7 2.2 %copy-start = (bf16[1,2048,1024]{2,1,0:T(8,128)(2,1)S(1)}, bf16[1,2048,1024]{2,1,0:T(8,128)(2,1)}, u32[]{:S(2)}) copy-start(bf16[1,2048,1024]{2,1,0:T(8,128)(2,1)} %param.6) | copy-start | bytes 12582916
  4.6 3.5 %copy-start.2 = (bf16[1,1024,2048]{2,1,0:T(8,128)(2,1)S(1)}, bf16[1,1024,2048]{2,1,0:T(8,128)(2,1)}, u32[]{:S(2)}) copy-start(bf16[1,1024,2048]{2,1,0:T(8,128)(2,1)} %param.7) | copy-start | bytes 12582916
  8.1 3.0 %copy-start.4 = (f32[1,2048]{1,0:T(1,128)S(1)}, f32[1,2048]{1,0:T(1,128)}, u32[]{:S(2)}) copy-start(f32[1,2048]{1,0:T(1,128)} %refs_2_.9) | copy-start | bytes 24580
  8.1 3.0 %collective-permute-start.2 = (bf16[128,2048]{1,0:T(8,128)(2,1)S(1)}, bf16[128,2048]{1,0:T(8,128)(2,1)S(1)}, u32[]{:S(2)}, u32[]{:S(2)}) collective-permute-start(bf16[128,2048]{1,0:T(8,128)(2,1)S(1)} %get-tuple-element.88), channel_id=1, source_target_pairs={{0,15},{1,14},{2,9},{3,8},{4,11},{5,10},{6,13},{7,12}} | collective-permute-start | bytes 1572872 | tf_op jit(solution)/shard_map/ppermute | solution.py:296
  8.9 2.1 %collective-permute-start.1 = (bf16[128,2048]{1,0:T(8,128)(2,1)S(1)}, bf16[128,2048]{1,0:T(8,128)(2,1)S(1)}, u32[]{:S(2)}, u32[]{:S(2)}) collective-permute-start(bf16[128,2048]{1,0:T(8,128)(2,1)S(1)} %get-tuple-element.88), channel_id=1, source_target_pairs={{0,14},{1,15},{2,8},{3,9},{4,10},{5,11},{6,12},{7,13}} | collective-permute-start | bytes 1572872 | tf_op jit(solution)/shard_map/ppermute | solution.py:296
  9.7 1.5 %collective-permute-start.4 = (bf16[128,2048]{1,0:T(8,128)(2,1)S(1)}, bf16[128,2048]{1,0:T(8,128)(2,1)S(1)}, u32[]{:S(2)}, u32[]{:S(2)}) collective-permute-start(bf16[128,2048]{1,0:T(8,128)(2,1)S(1)} %get-tuple-element.90), channel_id=1, source_target_pairs={{0,9},{1,8},{2,11},{3,10},{4,13},{5,12},{6,15},{7,14}} | collective-permute-start | bytes 1572872 | tf_op jit(solution)/shard_map/ppermute | solution.py:296
  10.4 0.8 collective-permute-start.3
  11.2 31.3 %collective-permute-start.7 = (bf16[128,2048]{1,0:T(8,128)(2,1)S(1)}, bf16[128,2048]{1,0:T(8,128)(2,1)S(1)}, u32[]{:S(2)}, u32[]{:S(2)}) collective-permute-start(bf16[128,2048]{1,0:T(8,128)(2,1)S(1)} %get-tuple-element.104), channel_id=1, source_target_pairs={{8,26},{9,27},{10,28},{11,29},{12,30},{13,31},{14,24},{15,25}} | collective-permute-start | bytes 1572872 | tf_op jit(solution)/shard_map/ppermute | solution.py:296
  12.5 32.6 %collective-permute-start.6 = (bf16[128,2048]{1,0:T(8,128)(2,1)S(1)}, bf16[128,2048]{1,0:T(8,128)(2,1)S(1)}, u32[]{:S(2)}, u32[]{:S(2)}) collective-permute-start(bf16[128,2048]{1,0:T(8,128)(2,1)S(1)} %get-tuple-element.102), channel_id=1, source_target_pairs={{8,1},{9,0},{10,3},{11,2},{12,5},{13,4},{14,7},{15,6}} | collective-permute-start | bytes 1572872 | tf_op jit(solution)/shard_map/ppermute | solution.py:296
  13.2 31.9 %collective-permute-start.5 = (bf16[128,2048]{1,0:T(8,128)(2,1)S(1)}, bf16[128,2048]{1,0:T(8,128)(2,1)S(1)}, u32[]{:S(2)}, u32[]{:S(2)}) collective-permute-start(bf16[128,2048]{1,0:T(8,128)(2,1)S(1)} %get-tuple-element.102), channel_id=1, source_target_pairs={{8,0},{9,1},{10,2},{11,3},{12,4},{13,5},{14,6},{15,7}} | collective-permute-start | bytes 1572872 | tf_op jit(solution)/shard_map/ppermute | solution.py:296
  42.4 7.4 %collective-permute-start.9 = (bf16[128,2048]{1,0:T(8,128)(2,1)S(1)}, bf16[128,2048]{1,0:T(8,128)(2,1)S(1)}, u32[]{:S(2)}, u32[]{:S(2)}) collective-permute-start(bf16[128,2048]{1,0:T(8,128)(2,1)S(1)} %after.3), channel_id=1, source_target_pairs={{24,17},{25,16},{26,19},{27,18},{28,21},{29,20},{30,23},{31,22}} | collective-permute-start | bytes 1572872 | tf_op jit(solution)/shard_map/ppermute | solution.py:296
  43.8 6.1 %collective-permute-start.8 = (bf16[128,2048]{1,0:T(8,128)(2,1)S(1)}, bf16[128,2048]{1,0:T(8,128)(2,1)S(1)}, u32[]{:S(2)}, u32[]{:S(2)}) collective-permute-start(bf16[128,2048]{1,0:T(8,128)(2,1)S(1)} %after.3), channel_id=1, source_target_pairs={{24,16},{25,17},{26,18},{27,19},{28,20},{29,21},{30,22},{31,23}} | collective-permute-start | bytes 1572872 | tf_op jit(solution)/shard_map/ppermute | solution.py:296
  45.1 4.7 %collective-permute-start.10 = (bf16[128,2048]{1,0:T(8,128)(2,1)S(1)}, bf16[128,2048]{1,0:T(8,128)(2,1)S(1)}, u32[]{:S(2)}, u32[]{:S(2)}) collective-permute-start(bf16[128,2048]{1,0:T(8,128)(2,1)S(1)} %get-tuple-element.107), channel_id=1, source_target_pairs={{0,16},{1,17},{2,18},{3,19},{4,20},{5,21},{6,22},{7,23}} | collective-permute-start | bytes 1572872 | tf_op jit(solution)/shard_map/ppermute | solution.py:296
  50.1 16.4 %collective-permute-start.12 = (bf16[128,2048]{1,0:T(8,128)(2,1)S(1)}, bf16[128,2048]{1,0:T(8,128)(2,1)S(1)}, u32[]{:S(2)}, u32[]{:S(2)}) collective-permute-start(bf16[128,2048]{1,0:T(8,128)(2,1)S(1)} %get-tuple-element.121.share), channel_id=1, source_target_pairs={{16,31},{17,30},{18,25},{19,24},{20,27},{21,26},{22,29},{23,28}} | collective-permute-start | bytes 1572872 | tf_op jit(solution)/shard_map/ppermute | solution.py:296
  51.4 21.1 %collective-permute-start.11 = (bf16[128,2048]{1,0:T(8,128)(2,1)S(1)}, bf16[128,2048]{1,0:T(8,128)(2,1)S(1)}, u32[]{:S(2)}, u32[]{:S(2)}) collective-permute-start(bf16[128,2048]{1,0:T(8,128)(2,1)S(1)} %get-tuple-element.121.share), channel_id=1, source_target_pairs={{16,30},{17,31},{18,24},{19,25},{20,26},{21,27},{22,28},{23,29}} | collective-permute-start | bytes 1572872 | tf_op jit(solution)/shard_map/ppermute | solution.py:296
  52.8 20.8 %collective-permute-start.14 = (bf16[128,2048]{1,0:T(8,128)(2,1)S(1)}, bf16[128,2048]{1,0:T(8,128)(2,1)S(1)}, u32[]{:S(2)}, u32[]{:S(2)}) collective-permute-start(bf16[128,2048]{1,0:T(8,128)(2,1)S(1)} %get-tuple-element.123), channel_id=1, source_target_pairs={{16,25},{17,24},{18,27},{19,26},{20,29},{21,28},{22,31},{23,30}} | collective-permute-start | bytes 1572872 | tf_op jit(solution)/shard_map/ppermute | solution.py:296
  54.1 19.5 %collective-permute-start.13 = (bf16[128,2048]{1,0:T(8,128)(2,1)S(1)}, bf16[128,2048]{1,0:T(8,128)(2,1)S(1)}, u32[]{:S(2)}, u32[]{:S(2)}) collective-permute-start(bf16[128,2048]{1,0:T(8,128)(2,1)S(1)} %get-tuple-element.123), channel_id=1, source_target_pairs={{16,24},{17,25},{18,26},{19,27},{20,28},{21,29},{22,30},{23,31}} | collective-permute-start | bytes 1572872 | tf_op jit(solution)/shard_map/ppermute | solution.py:296
  55.4 23.3 %collective-permute-start.15 = (bf16[128,1024]{1,0:T(8,128)(2,1)S(1)}, bf16[128,1024]{1,0:T(8,128)(2,1)S(1)}, u32[]{:S(2)}, u32[]{:S(2)}) collective-permute-start(bf16[128,1024]{1,0:T(8,128)(2,1)S(1)} %after.4), channel_id=1, source_target_pairs={{8,2},{9,3},{10,4},{11,5},{12,6},{13,7},{14,0},{15,1},{16,17},{17,... | collective-permute-start | bytes 786440 | tf_op jit(solution)/shard_map/ppermute | solution.py:296
  76.0 6.7 %collective-permute-start.16 = (bf16[128,1024]{1,0:T(8,128)(2,1)S(1)}, bf16[128,1024]{1,0:T(8,128)(2,1)S(1)}, u32[]{:S(2)}, u32[]{:S(2)}) collective-permute-start(bf16[128,1024]{1,0:T(8,128)(2,1)S(1)} %get-tuple-element.138), channel_id=1, source_target_pairs={{24,18},{25,19},{26,20},{27,21},{28,22},{29,23},{30,16},{31,17}} | collective-permute-start | bytes 786440 | tf_op jit(solution)/shard_map/ppermute | solution.py:296
  77.3 6.1 %collective-permute-start.17 = (bf16[128,1024]{1,0:T(8,128)(2,1)S(1)}, bf16[128,1024]{1,0:T(8,128)(2,1)S(1)}, u32[]{:S(2)}, u32[]{:S(2)}) collective-permute-start(bf16[128,1024]{1,0:T(8,128)(2,1)S(1)} %get-tuple-element.139), channel_id=1, source_target_pairs={{24,19},{25,18},{26,21},{27,20},{28,23},{29,22},{30,17},{31,16}} | collective-permute-start | bytes 786440 | tf_op jit(solution)/shard_map/ppermute | solution.py:296
  80.1 7.4 %collective-permute-start.18 = (bf16[128,1024]{1,0:T(8,128)(2,1)S(1)}, bf16[128,1024]{1,0:T(8,128)(2,1)S(1)}, u32[]{:S(2)}, u32[]{:S(2)}) collective-permute-start(bf16[128,1024]{1,0:T(8,128)(2,1)S(1)} %get-tuple-element.141), channel_id=1, source_target_pairs={{24,17},{25,16},{26,19},{27,18},{28,21},{29,20},{30,23},{31,22}} | collective-permute-start | bytes 786440 | tf_op jit(solution)/shard_map/ppermute | solution.py:296
  81.4 6.1 %collective-permute-start.19 = (bf16[256,1024]{1,0:T(8,128)(2,1)S(1)}, bf16[256,1024]{1,0:T(8,128)(2,1)S(1)}, u32[]{:S(2)}, u32[]{:S(2)}) collective-permute-start(bf16[256,1024]{1,0:T(8,128)(2,1)S(1)} %get-tuple-element.145), channel_id=1, source_target_pairs={{8,0},{9,1},{10,2},{11,3},{12,4},{13,5},{14,6},{15,7},{16,8},{17,9... | collective-permute-start | bytes 1572872 | tf_op jit(solution)/shard_map/ppermute | solution.py:296
  87.5 3.8 %collective-permute-start.20 = (bf16[256,1024]{1,0:T(8,128)(2,1)S(1)}, bf16[256,1024]{1,0:T(8,128)(2,1)S(1)}, u32[]{:S(2)}, u32[]{:S(2)}) collective-permute-start(bf16[256,1024]{1,0:T(8,128)(2,1)S(1)} %get-tuple-element.146), channel_id=1, source_target_pairs={{16,24},{17,25},{18,26},{19,27},{20,28},{21,29},{22,30},{23,31}} | collective-permute-start | bytes 1572872 | tf_op jit(solution)/shard_map/ppermute | solution.py:296
  (3 other events, 3.9 us)

commit v4 on v3

--- a/solution.py
+++ b/solution.py
@@ -20,9 +20,9 @@
 MARK = jax.ShapeDtypeStruct((8, 128), jnp.float32)
 
 
-def project_kernel(section, chunk_order, n_parts, keep, mark, *refs):
+def project_kernel(section, chunk_order, n_parts, keep, first_row, mark, *refs):
     parts, refs = refs[:n_parts], refs[n_parts:]
-    scale, weight, refs = refs[0], refs[1], refs[2:]
+    scale, weight, refs = refs[0], refs[1], refs[2 + 2 * (first_row > 0) :]
     before, refs = (refs[0], refs[1:]) if keep == "hand on" else (None, refs)
     x_ref, q_ref, k_ref, v_ref, refs = *refs[:4], refs[4:]
     kept = refs[0] if keep else None
@@ -44,9 +44,10 @@
             mean_square = jnp.mean(wide * wide, axis=1, keepdims=True)
             u_ref[put, :] = (wide * lax.rsqrt(mean_square + EPSILON)).astype(u_ref.dtype)
         key = u_ref[:, mine]
-        k_ref[...] = key
+        here = slice(first_row, first_row + u_ref.shape[0])
+        k_ref[here, :] = key
         q_ref[...] = (key.astype(jnp.float32) * scale[:, mine]).astype(q_ref.dtype)
-        v_ref[...] = jnp.dot(
+        v_ref[here, :] = jnp.dot(
             u_ref[...], weight[...], preferred_element_type=jnp.float32
         ).astype(v_ref.dtype)
         if keep:
@@ -59,16 +60,19 @@
             kept[...] = before[...]
 
 
-def project(section, chunk_order, parts, mark, scale, weight, keep="", before=()):
+def project(section, chunk_order, parts, mark, scale, weight, first_row, total_rows, filled, keep="", before=()):
     rows, width = parts[0].shape
     channels = weight.shape[1]
-    shapes = [(rows, width)] + [(rows, channels)] * (4 if keep else 3)
-    arrays = [*parts, scale, weight, *before]
-    return pl.pallas_call(
-        functools.partial(project_kernel, section, chunk_order, len(parts), keep),
+    shapes = [(rows, width), (rows, channels)] + [(total_rows, channels)] * 2
+    shapes += [(rows, channels)] * (1 if keep else 0)
+    arrays = [*parts, scale, weight, *filled, *before]
+    at = 1 + len(parts) + 2
+    return pl.pallas_call(
+        functools.partial(project_kernel, section, chunk_order, len(parts), keep, first_row),
         out_shape=tuple(jax.ShapeDtypeStruct(shape, jnp.bfloat16) for shape in shapes) + (MARK,),
         in_specs=[anywhere] + [vmem] * len(arrays),
         out_specs=(vmem,) * len(shapes) + (anywhere,),
+        input_output_aliases={at: 2, at + 1: 3} if filled else {},
         scratch_shapes=[pltpu.VMEM((rows, width), jnp.bfloat16)],
         compiler_params=pltpu.CompilerParams(vmem_limit_bytes=VMEM_LIMIT),
         cost_estimate=pl.CostEstimate(
@@ -82,9 +86,8 @@
     return jnp.concatenate(values, axis=axis) if len(values) > 1 else values[0]
 
 
-def attend_kernel(section, pieces, n_blocks, split, carry, copies, mark, *refs):
-    blocks, refs = refs[: 4 * n_blocks], refs[4 * n_blocks :]
-    xs, qs, ks, vs = (blocks[i * n_blocks : (i + 1) * n_blocks] for i in range(4))
+def attend_kernel(section, pieces, n_blocks, split, carry, copies, mark, k, v, *refs):
+    xs, qs, refs = refs[:n_blocks], refs[n_blocks : 2 * n_blocks], refs[2 * n_blocks :]
     weight, refs = refs[0], refs[1:]
     kept, refs = refs[:carry], refs[carry:]
     outs, o_ref = refs[:-2], refs[-1]
@@ -96,25 +99,18 @@
     @pl.when(lax.axis_index("pipe") == section)
     def _():
         heads = [slice(at, at + HEAD_DIM) for at in range(0, channels, HEAD_DIM)]
-        keys = sum(k.shape[0] for k in ks)
-        ones = jnp.ones((keys, HEAD_DIM), jnp.bfloat16)
+        ones = jnp.ones((v.shape[0], HEAD_DIM), jnp.bfloat16)
         weights = []
         for lanes in heads:
             q = join([qs[block][start : start + size, lanes] for block, start, size in pieces], 0)
-            scores = join(
-                [
-                    lax.dot_general(
-                        q, k[:, lanes], (((1,), (1,)), ((), ())), preferred_element_type=jnp.float32
-                    )
-                    for k in ks
-                ],
-                1,
+            scores = lax.dot_general(
+                q, k[:, lanes], (((1,), (1,)), ((), ())), preferred_element_type=jnp.float32
             )
             highest = jnp.max(scores, axis=1, keepdims=True)
             weights.append(jnp.exp((scores - highest) * inv_root).astype(jnp.bfloat16))
         for lanes, weight_of_head in zip(heads, weights):
-            v = jnp.concatenate([join([v[:, lanes] for v in vs], 0), ones], axis=1)
-            attended = jnp.dot(weight_of_head, v, preferred_element_type=jnp.float32)
+            values = jnp.concatenate([v[:, lanes], ones], axis=1)
+            attended = jnp.dot(weight_of_head, values, preferred_element_type=jnp.float32)
             o_ref[:, lanes] = (attended[:, :HEAD_DIM] / attended[:, HEAD_DIM:]).astype(o_ref.dtype)
         mine = jnp.where(lax.axis_index("head") == 0, 1.0, 0.0)
         attended = o_ref[...]
@@ -163,7 +159,7 @@
 def attend(section, pieces, blocks, mark, weight, split, kept=(), share=False):
     rows = sum(size for _, _, size in pieces)
     channels, width = weight.shape
-    keys = sum(block[2].shape[0] for block in blocks)
+    keys, values = blocks[-1][2:]
     n_head = width // channels
     if split:
         out_shape = tuple(
@@ -173,7 +169,7 @@
     else:
         out_shape = (jax.ShapeDtypeStruct((rows, width), jnp.bfloat16),)
         out_shape += (jax.ShapeDtypeStruct((rows, channels), jnp.bfloat16),) * (n_head - 1 if share else 0)
-    arrays = [block[i] for i in range(4) for block in blocks] + [weight, *kept]
+    arrays = [keys, values] + [block[i] for i in range(2) for block in blocks] + [weight, *kept]
     return pl.pallas_call(
         functools.partial(attend_kernel, section, pieces, len(blocks), split, len(kept), n_head if share else 0),
         out_shape=out_shape + (MARK,),
@@ -182,9 +178,9 @@
         scratch_shapes=[pltpu.VMEM((rows, channels), jnp.bfloat16)],
         compiler_params=pltpu.CompilerParams(vmem_limit_bytes=VMEM_LIMIT),
         cost_estimate=pl.CostEstimate(
-            flops=2 * rows * channels * (width + 2 * keys),
+            flops=2 * rows * channels * (width + 2 * keys.shape[0]),
             bytes_accessed=2 * width * channels,
-            transcendentals=rows * keys * channels // HEAD_DIM,
+            transcendentals=rows * keys.shape[0] * channels // HEAD_DIM,
         ),
         name="attend",
     )(mark, *arrays)
@@ -262,6 +258,16 @@
     )(*arrays)
 
 
+def new_mark():
+    return pl.pallas_call(
+        lambda ref: None,
+        out_shape=MARK,
+        out_specs=anywhere,
+        compiler_params=pltpu.CompilerParams(vmem_limit_bytes=1024 * 1024),
+        name="new_mark",
+    )()
+
+
 def after(arrays, *marks):
     shapes = tuple(jax.ShapeDtypeStruct(array.shape, array.dtype) for array in arrays)
     return pl.pallas_call(
@@ -301,11 +307,14 @@
     )
     own = stream.reshape(row_count * col_count, width)
     arrived = [own] + [send(own, 0, 0, 0, turn) for turn in range(1, n_head)]
-    mark = jnp.zeros(MARK.shape, MARK.dtype)
-    blocks = []
-    for cells in arrived:
-        *block, mark = project(0, natural, [cells], mark, score_scale, value_cols)
+    mark = new_mark()
+    blocks, filled = [], ()
+    for turn, cells in enumerate(arrived):
+        *block, mark = project(
+            0, natural, [cells], mark, score_scale, value_cols, turn * own.shape[0], n_head * own.shape[0], filled
+        )
         blocks.append(block)
+        filled = block[2:]
     halves = [[(block, half * piece, piece) for block in range(n_head)] for half in range(2)]
     straight = tuple(range(row_count * n_head))
     kept = [None, None]
@@ -349,18 +358,31 @@
                 for turn, block in enumerate(after(shared, mark))
             ]
         if not last:
-            blocks = [None, None]
+            blocks, filled, rows = [], (), piece * n_head
             for half in range(2):
                 keep = "" if section + 2 == sections and not half else "hand on" if section else "start"
                 before = [kept[half]] if keep == "hand on" else []
-                *blocks[half], mark = project(
-                    section + 1, straight, moved[half], mark, score_scale, value_cols, keep, before
+                *block, mark = project(
+                    section + 1,
+                    straight,
+                    moved[half],
+                    mark,
+                    score_scale,
+                    value_cols,
+                    half * rows,
+                    2 * rows,
+                    filled,
+                    keep,
+                    before,
                 )
                 if keep:
-                    *blocks[half], kept[half] = blocks[half]
+                    *block, kept[half] = block
+                blocks.append(block)
+                filled = block[2:]
             halves = [[(0, 0, piece * n_head)], [(1, 0, piece * n_head)]]
-    first, mark = add(sections - 2, moved[0], mark, 4 * 10**9)
+    *across, mark = after([*moved[0][1:], mark])
     second, mark = add(sections - 2, moved[1][:-1], mark, 4 * 10**9)
+    first, mark = add(sections - 2, [moved[0][0], *across], mark, 4 * 10**9)
     total, mark = add(sections - 2, [second, moved[1][-1]], mark, 0, (first,))
     total = send(total, sections - 2, sections - 1)
     return finish(sections - 1, row_count * n_head, total, moved[1][-1], own_share, early)[None]

time: 93.1 us -> 90.4 us (0.971)
  waiting for transfers between devices: 56.3 us -> 54.3 us
    ppermute x21, waiting for transfers between devices: 56.3 us -> 54.3 us  [send_all(): return lax.ppermute(value, AXES, pairs)]
  transfers between devices with their start and end apart: 21 -> 21, of which waited for: 7 -> 6; matrix products, arithmetic and copies ran while one was open for 0% -> 0% of each run, Pallas kernels for 5% -> 5%
where the time goes in v4:
time: 90.4 us; the launch traced here: 89.9 us
  waiting for transfers between devices  54.3 us (60%)
  starting transfers between devices  22 us (24%)
  local copies, waits for them, and re-layouts  7.38 us (8%)
  Pallas kernels  5.74 us (6%)
    ppermute x21, waiting for transfers between devices, send_all(): return lax.ppermute(value, AXES, pairs)  54.3 us
    ppermute x21, starting transfers between devices, send_all(): return lax.ppermute(value, AXES, pairs)  22 us
    unnamed x12, local copies, waits for them, and re-layouts  7.38 us
    pallas_call x8, Pallas kernels, attend(): pl.pallas_call(functools.partial(attend_kernel, section, pieces, len(bloc...  2.68 us
    pallas_call x8, Pallas kernels, project(): pl.pallas_call(functools.partial(project_kernel, section, chunk_order, le...  2.17 us
  transfers between devices with their start and end apart: 21, of which 6 were waited for; matrix products, arithmetic and copies ran while one was open for 0% of the time, Pallas kernels for 5%

profile of v4, /device:TPU:5, one launch (start us, length us, event | category | flops | bytes accessed | tf_op | source)
XLA Modules:
  0.0 89.9 jit_solution(14634245237744612821)
XLA Ops:
  0.7 2.2 %copy-done = bf16[1,2048,1024]{2,1,0:T(8,128)(2,1)S(1)} copy-done((bf16[1,2048,1024]{2,1,0:T(8,128)(2,1)S(1)}, bf16[1,2048,1024]{2,1,0:T(8,128)(2,1)}, u32[]{:S(2)}) %copy-start) | copy-done | bytes 4194328
  4.6 2.2 %copy-done.1 = bf16[1,2048,1024]{2,1,0:T(8,128)(2,1)S(1)} copy-done((bf16[1,2048,1024]{2,1,0:T(8,128)(2,1)S(1)}, bf16[1,2048,1024]{2,1,0:T(8,128)(2,1)}, u32[]{:S(2)}) %copy-start.1) | copy-done | bytes 4194328
  6.8 1.3 %copy-done.2 = bf16[1,1024,2048]{2,1,0:T(8,128)(2,1)S(1)} copy-done((bf16[1,1024,2048]{2,1,0:T(8,128)(2,1)S(1)}, bf16[1,1024,2048]{2,1,0:T(8,128)(2,1)}, u32[]{:S(2)}) %copy-start.2) | copy-done | bytes 4194328
  11.2 1.3 %collective-permute-start.7 = (bf16[128,2048]{1,0:T(8,128)(2,1)S(1)}, bf16[128,2048]{1,0:T(8,128)(2,1)S(1)}, u32[]{:S(2)}, u32[]{:S(2)}) collective-permute-start(bf16[128,2048]{1,0:T(8,128)(2,1)S(1)} %get-tuple-element.106), channel_id=1, source_target_pairs={{8,26},{9,27},{10,28},{11,29},{12,30},{13,31},{14,24},{15,25}} | collective-permute-start | bytes 1572872 | tf_op jit(solution)/shard_map/ppermute | solution.py:302
  13.9 28.1 %collective-permute-done.7.refs_0_ = bf16[128,2048]{1,0:T(8,128)(2,1)S(1)} collective-permute-done((bf16[128,2048]{1,0:T(8,128)(2,1)S(1)}, bf16[128,2048]{1,0:T(8,128)(2,1)S(1)}, u32[]{:S(2)}, u32[]{:S(2)}) %collective-permute-start.7) | collective-permute-done | bytes 524320 | tf_op jit(solution)/shard_map/ppermute | solution.py:302
  42.0 1.3 %collective-permute-start.9 = (bf16[128,2048]{1,0:T(8,128)(2,1)S(1)}, bf16[128,2048]{1,0:T(8,128)(2,1)S(1)}, u32[]{:S(2)}, u32[]{:S(2)}) collective-permute-start(bf16[128,2048]{1,0:T(8,128)(2,1)S(1)} %after.4), channel_id=1, source_target_pairs={{24,17},{25,16},{26,19},{27,18},{28,21},{29,20},{30,23},{31,22}} | collective-permute-start | bytes 1572872 | tf_op jit(solution)/shard_map/ppermute | solution.py:302
  43.4 1.3 %collective-permute-start.8 = (bf16[128,2048]{1,0:T(8,128)(2,1)S(1)}, bf16[128,2048]{1,0:T(8,128)(2,1)S(1)}, u32[]{:S(2)}, u32[]{:S(2)}) collective-permute-start(bf16[128,2048]{1,0:T(8,128)(2,1)S(1)} %after.4), channel_id=1, source_target_pairs={{24,16},{25,17},{26,18},{27,19},{28,20},{29,21},{30,22},{31,23}} | collective-permute-start | bytes 1572872 | tf_op jit(solution)/shard_map/ppermute | solution.py:302
  45.4 4.0 %collective-permute-done.9.refs_1_ = bf16[128,2048]{1,0:T(8,128)(2,1)S(1)} collective-permute-done((bf16[128,2048]{1,0:T(8,128)(2,1)S(1)}, bf16[128,2048]{1,0:T(8,128)(2,1)S(1)}, u32[]{:S(2)}, u32[]{:S(2)}) %collective-permute-start.9) | collective-permute-done | bytes 524320 | tf_op jit(solution)/shard_map/ppermute | solution.py:302
  49.7 1.3 %collective-permute-start.12 = (bf16[128,2048]{1,0:T(8,128)(2,1)S(1)}, bf16[128,2048]{1,0:T(8,128)(2,1)S(1)}, u32[]{:S(2)}, u32[]{:S(2)}) collective-permute-start(bf16[128,2048]{1,0:T(8,128)(2,1)S(1)} %get-tuple-element.123.share), channel_id=1, source_target_pairs={{16,31},{17,30},{18,25},{19,24},{20,27},{21,26},{22,29},{23,28}} | collective-permute-start | bytes 1572872 | tf_op jit(solution)/shard_map/ppermute | solution.py:302
  51.0 1.3 %collective-permute-start.11 = (bf16[128,2048]{1,0:T(8,128)(2,1)S(1)}, bf16[128,2048]{1,0:T(8,128)(2,1)S(1)}, u32[]{:S(2)}, u32[]{:S(2)}) collective-permute-start(bf16[128,2048]{1,0:T(8,128)(2,1)S(1)} %get-tuple-element.123.share), channel_id=1, source_target_pairs={{16,30},{17,31},{18,24},{19,25},{20,26},{21,27},{22,28},{23,29}} | collective-permute-start | bytes 1572872 | tf_op jit(solution)/shard_map/ppermute | solution.py:302
  52.4 1.3 %collective-permute-start.14 = (bf16[128,2048]{1,0:T(8,128)(2,1)S(1)}, bf16[128,2048]{1,0:T(8,128)(2,1)S(1)}, u32[]{:S(2)}, u32[]{:S(2)}) collective-permute-start(bf16[128,2048]{1,0:T(8,128)(2,1)S(1)} %get-tuple-element.125), channel_id=1, source_target_pairs={{16,25},{17,24},{18,27},{19,26},{20,29},{21,28},{22,31},{23,30}} | collective-permute-start | bytes 1572872 | tf_op jit(solution)/shard_map/ppermute | solution.py:302
  53.7 1.3 %collective-permute-start.13 = (bf16[128,2048]{1,0:T(8,128)(2,1)S(1)}, bf16[128,2048]{1,0:T(8,128)(2,1)S(1)}, u32[]{:S(2)}, u32[]{:S(2)}) collective-permute-start(bf16[128,2048]{1,0:T(8,128)(2,1)S(1)} %get-tuple-element.125), channel_id=1, source_target_pairs={{16,24},{17,25},{18,26},{19,27},{20,28},{21,29},{22,30},{23,31}} | collective-permute-start | bytes 1572872 | tf_op jit(solution)/shard_map/ppermute | solution.py:302
  55.7 10.0 %collective-permute-done.12.refs_1_ = bf16[128,2048]{1,0:T(8,128)(2,1)S(1)} collective-permute-done((bf16[128,2048]{1,0:T(8,128)(2,1)S(1)}, bf16[128,2048]{1,0:T(8,128)(2,1)S(1)}, u32[]{:S(2)}, u32[]{:S(2)}) %collective-permute-start.12) | collective-permute-done | bytes 524320 | tf_op jit(solution)/shard_map/ppermute | solution.py:302
  65.7 6.0 %collective-permute-done.11.refs_0_ = bf16[128,2048]{1,0:T(8,128)(2,1)S(1)} collective-permute-done((bf16[128,2048]{1,0:T(8,128)(2,1)S(1)}, bf16[128,2048]{1,0:T(8,128)(2,1)S(1)}, u32[]{:S(2)}, u32[]{:S(2)}) %collective-permute-start.11) | collective-permute-done | bytes 524320 | tf_op jit(solution)/shard_map/ppermute | solution.py:302
  72.7 1.1 %project.15 = (bf16[128,2048]{1,0:T(8,128)(2,1)S(1)}, bf16[128,1024]{1,0:T(8,128)(2,1)S(1)}, bf16[256,1024]{1,0:T(8,128)(2,1)S(1)}, bf16[256,1024]{1,0:T(8,128)(...) custom-call(f32[8,128]{1,0:T(8,128)S(1)} %get-tuple-element.124.mark,, ...), custom_call_target="tpu_custom_call", output_to_operand_aliasing={{2}: (5, {}), {3}: (6, {})} | custom-call | flops 536870912 | bytes 4194304 | tf_op jit(solution)/shard_map/project/pallas_call | solution.py:70
  73.7 1.2 %attend.14 = (bf16[128,1024]{1,0:T(8,128)(2,1)S(1)}, bf16[128,1024]{1,0:T(8,128)(2,1)S(1)}, f32[8,128]{1,0:T(8,128)S(1)}) custom-call(f32[8,128]{1,0:T(8,128)S(1)} %get-tuple-element.129.mark, bf16[256,1024]{1,0:T(8,128)(2,1)S(1)} %get-tuple-element.130.k, bf16[256,1024]{1,0:T(8,128)(2,1)S(1)} %get-tuple-element.131.v, ...), custom_call_target="tpu_custom_call" | custom-call | flops 671088640 | bytes 4194304 | tf_op jit(solution)/shard_map/attend/pallas_call | solution.py:173
  74.9 1.3 %collective-permute-start.15 = (bf16[128,1024]{1,0:T(8,128)(2,1)S(1)}, bf16[128,1024]{1,0:T(8,128)(2,1)S(1)}, u32[]{:S(2)}, u32[]{:S(2)}) collective-permute-start(bf16[128,1024]{1,0:T(8,128)(2,1)S(1)} %get-tuple-element.136), channel_id=1, source_target_pairs={{24,19},{25,18},{26,21},{27,20},{28,23},{29,22},{30,17},{31,16}} | collective-permute-start | bytes 786440 | tf_op jit(solution)/shard_map/ppermute | solution.py:302
  76.3 1.2 %attend.15 = (bf16[256,1024]{1,0:T(8,128)(2,1)S(1)}, bf16[128,1024]{1,0:T(8,128)(2,1)S(1)}, f32[8,128]{1,0:T(8,128)S(1)}) custom-call(f32[8,128]{1,0:T(8,128)S(1)} %after.6.mark, bf16[256,1024]{1,0:T(8,128)(2,1)S(1)} %get-tuple-element.130.k, bf16[256,1024]{1,0:T(8,128)(2,1)S(1)} %get-tuple-element.131.v, bf16[128,2048]{1,0:T(8,128)(2,1)S(1)} %get-tuple-element.132.refs_0_, ...), custom_call_target="tpu_custom_call" | custom-call | flops 671088640 | bytes 4194304 | tf_op jit(solution)/shard_map/attend/pallas_call | solution.py:173
  77.5 1.3 %collective-permute-start.17 = (bf16[128,1024]{1,0:T(8,128)(2,1)S(1)}, bf16[128,1024]{1,0:T(8,128)(2,1)S(1)}, u32[]{:S(2)}, u32[]{:S(2)}) collective-permute-start(bf16[128,1024]{1,0:T(8,128)(2,1)S(1)} %get-tuple-element.142), channel_id=1, source_target_pairs={{24,17},{25,16},{26,19},{27,18},{28,21},{29,20},{30,23},{31,22}} | collective-permute-start | bytes 786440 | tf_op jit(solution)/shard_map/ppermute | solution.py:302
  78.8 1.3 %collective-permute-start.18 = (bf16[128,1024]{1,0:T(8,128)(2,1)S(1)}, bf16[128,1024]{1,0:T(8,128)(2,1)S(1)}, u32[]{:S(2)}, u32[]{:S(2)}) collective-permute-start(bf16[128,1024]{1,0:T(8,128)(2,1)S(1)} %get-tuple-element.144), channel_id=1, source_target_pairs={{24,18},{25,19},{26,20},{27,21},{28,22},{29,23},{30,16},{31,17}} | collective-permute-start | bytes 786440 | tf_op jit(solution)/shard_map/ppermute | solution.py:302
  80.1 1.3 %collective-permute-start.19 = (bf16[256,1024]{1,0:T(8,128)(2,1)S(1)}, bf16[256,1024]{1,0:T(8,128)(2,1)S(1)}, u32[]{:S(2)}, u32[]{:S(2)}) collective-permute-start(bf16[256,1024]{1,0:T(8,128)(2,1)S(1)} %get-tuple-element.149), channel_id=1, source_target_pairs={{8,0},{9,1},{10,2},{11,3},{12,4},{13,5},{14,6},{15,7},{16,8},{17,9... | collective-permute-start | bytes 1572872 | tf_op jit(solution)/shard_map/ppermute | solution.py:302
  81.4 2.3 %collective-permute-done.17.refs_0_ = bf16[128,1024]{1,0:T(8,128)(2,1)S(1)} collective-permute-done((bf16[128,1024]{1,0:T(8,128)(2,1)S(1)}, bf16[128,1024]{1,0:T(8,128)(2,1)S(1)}, u32[]{:S(2)}, u32[]{:S(2)}) %collective-permute-start.17) | collective-permute-done | bytes 262176 | tf_op jit(solution)/shard_map/ppermute | solution.py:302
  83.7 1.3 %collective-permute-start.20 = (bf16[256,1024]{1,0:T(8,128)(2,1)S(1)}, bf16[256,1024]{1,0:T(8,128)(2,1)S(1)}, u32[]{:S(2)}, u32[]{:S(2)}) collective-permute-start(bf16[256,1024]{1,0:T(8,128)(2,1)S(1)} %get-tuple-element.150), channel_id=1, source_target_pairs={{16,24},{17,25},{18,26},{19,27},{20,28},{21,29},{22,30},{23,31}} | collective-permute-start | bytes 1572872 | tf_op jit(solution)/shard_map/ppermute | solution.py:302
  85.0 4.0 %collective-permute-done.20.total = bf16[256,1024]{1,0:T(8,128)(2,1)S(1)} collective-permute-done((bf16[256,1024]{1,0:T(8,128)(2,1)S(1)}, bf16[256,1024]{1,0:T(8,128)(2,1)S(1)}, u32[]{:S(2)}, u32[]{:S(2)}) %collective-permute-start.20) | collective-permute-done | bytes 524320 | tf_op jit(solution)/shard_map/ppermute | solution.py:302
  (56 shorter events, 10.4 us)
Async XLA Ops:
  0.0 4.6 %collective-permute-start = (bf16[128,2048]{1,0:T(8,128)(2,1)}, bf16[128,2048]{1,0:T(8,128)(2,1)S(1)}, u32[]{:S(2)}, u32[]{:S(2)}) collective-permute-start(bf16[128,2048]{1,0:T(8,128)(2,1)} %bitcast.20), channel_id=1, source_target_pairs={{0,1},{1,0},{2,3},{3,2},{4,5},{5,4},{6,7},{7,6}} | collective-permute-start | bytes 1572872 | tf_op jit(solution)/shard_map/ppermute | solution.py:302
  0.7 2.2 %copy-start = (bf16[1,2048,1024]{2,1,0:T(8,128)(2,1)S(1)}, bf16[1,2048,1024]{2,1,0:T(8,128)(2,1)}, u32[]{:S(2)}) copy-start(bf16[1,2048,1024]{2,1,0:T(8,128)(2,1)} %param.6) | copy-start | bytes 12582916
  4.6 3.5 %copy-start.2 = (bf16[1,1024,2048]{2,1,0:T(8,128)(2,1)S(1)}, bf16[1,1024,2048]{2,1,0:T(8,128)(2,1)}, u32[]{:S(2)}) copy-start(bf16[1,1024,2048]{2,1,0:T(8,128)(2,1)} %param.7) | copy-start | bytes 12582916
  8.1 3.0 %copy-start.4 = (f32[1,2048]{1,0:T(1,128)S(1)}, f32[1,2048]{1,0:T(1,128)}, u32[]{:S(2)}) copy-start(f32[1,2048]{1,0:T(1,128)} %refs_2_.9) | copy-start | bytes 24580
  8.1 3.0 %collective-permute-start.2 = (bf16[128,2048]{1,0:T(8,128)(2,1)S(1)}, bf16[128,2048]{1,0:T(8,128)(2,1)S(1)}, u32[]{:S(2)}, u32[]{:S(2)}) collective-permute-start(bf16[128,2048]{1,0:T(8,128)(2,1)S(1)} %get-tuple-element.90), channel_id=1, source_target_pairs={{0,15},{1,14},{2,9},{3,8},{4,11},{5,10},{6,13},{7,12}} | collective-permute-start | bytes 1572872 | tf_op jit(solution)/shard_map/ppermute | solution.py:302
  8.9 2.1 %collective-permute-start.1 = (bf16[128,2048]{1,0:T(8,128)(2,1)S(1)}, bf16[128,2048]{1,0:T(8,128)(2,1)S(1)}, u32[]{:S(2)}, u32[]{:S(2)}) collective-permute-start(bf16[128,2048]{1,0:T(8,128)(2,1)S(1)} %get-tuple-element.90), channel_id=1, source_target_pairs={{0,14},{1,15},{2,8},{3,9},{4,10},{5,11},{6,12},{7,13}} | collective-permute-start | bytes 1572872 | tf_op jit(solution)/shard_map/ppermute | solution.py:302
  9.7 1.5 %collective-permute-start.4 = (bf16[128,2048]{1,0:T(8,128)(2,1)S(1)}, bf16[128,2048]{1,0:T(8,128)(2,1)S(1)}, u32[]{:S(2)}, u32[]{:S(2)}) collective-permute-start(bf16[128,2048]{1,0:T(8,128)(2,1)S(1)} %get-tuple-element.92), channel_id=1, source_target_pairs={{0,9},{1,8},{2,11},{3,10},{4,13},{5,12},{6,15},{7,14}} | collective-permute-start | bytes 1572872 | tf_op jit(solution)/shard_map/ppermute | solution.py:302
  10.4 0.8 collective-permute-start.3
  11.2 30.9 %collective-permute-start.7 = (bf16[128,2048]{1,0:T(8,128)(2,1)S(1)}, bf16[128,2048]{1,0:T(8,128)(2,1)S(1)}, u32[]{:S(2)}, u32[]{:S(2)}) collective-permute-start(bf16[128,2048]{1,0:T(8,128)(2,1)S(1)} %get-tuple-element.106), channel_id=1, source_target_pairs={{8,26},{9,27},{10,28},{11,29},{12,30},{13,31},{14,24},{15,25}} | collective-permute-start | bytes 1572872 | tf_op jit(solution)/shard_map/ppermute | solution.py:302
  12.5 32.2 %collective-permute-start.6 = (bf16[128,2048]{1,0:T(8,128)(2,1)S(1)}, bf16[128,2048]{1,0:T(8,128)(2,1)S(1)}, u32[]{:S(2)}, u32[]{:S(2)}) collective-permute-start(bf16[128,2048]{1,0:T(8,128)(2,1)S(1)} %get-tuple-element.104), channel_id=1, source_target_pairs={{8,1},{9,0},{10,3},{11,2},{12,5},{13,4},{14,7},{15,6}} | collective-permute-start | bytes 1572872 | tf_op jit(solution)/shard_map/ppermute | solution.py:302
  13.2 31.5 %collective-permute-start.5 = (bf16[128,2048]{1,0:T(8,128)(2,1)S(1)}, bf16[128,2048]{1,0:T(8,128)(2,1)S(1)}, u32[]{:S(2)}, u32[]{:S(2)}) collective-permute-start(bf16[128,2048]{1,0:T(8,128)(2,1)S(1)} %get-tuple-element.104), channel_id=1, source_target_pairs={{8,0},{9,1},{10,2},{11,3},{12,4},{13,5},{14,6},{15,7}} | collective-permute-start | bytes 1572872 | tf_op jit(solution)/shard_map/ppermute | solution.py:302
  42.0 7.4 %collective-permute-start.9 = (bf16[128,2048]{1,0:T(8,128)(2,1)S(1)}, bf16[128,2048]{1,0:T(8,128)(2,1)S(1)}, u32[]{:S(2)}, u32[]{:S(2)}) collective-permute-start(bf16[128,2048]{1,0:T(8,128)(2,1)S(1)} %after.4), channel_id=1, source_target_pairs={{24,17},{25,16},{26,19},{27,18},{28,21},{29,20},{30,23},{31,22}} | collective-permute-start | bytes 1572872 | tf_op jit(solution)/shard_map/ppermute | solution.py:302
  43.4 6.1 %collective-permute-start.8 = (bf16[128,2048]{1,0:T(8,128)(2,1)S(1)}, bf16[128,2048]{1,0:T(8,128)(2,1)S(1)}, u32[]{:S(2)}, u32[]{:S(2)}) collective-permute-start(bf16[128,2048]{1,0:T(8,128)(2,1)S(1)} %after.4), channel_id=1, source_target_pairs={{24,16},{25,17},{26,18},{27,19},{28,20},{29,21},{30,22},{31,23}} | collective-permute-start | bytes 1572872 | tf_op jit(solution)/shard_map/ppermute | solution.py:302
  44.7 4.7 %collective-permute-start.10 = (bf16[128,2048]{1,0:T(8,128)(2,1)S(1)}, bf16[128,2048]{1,0:T(8,128)(2,1)S(1)}, u32[]{:S(2)}, u32[]{:S(2)}) collective-permute-start(bf16[128,2048]{1,0:T(8,128)(2,1)S(1)} %get-tuple-element.109), channel_id=1, source_target_pairs={{0,16},{1,17},{2,18},{3,19},{4,20},{5,21},{6,22},{7,23}} | collective-permute-start | bytes 1572872 | tf_op jit(solution)/shard_map/ppermute | solution.py:302
  49.7 15.9 %collective-permute-start.12 = (bf16[128,2048]{1,0:T(8,128)(2,1)S(1)}, bf16[128,2048]{1,0:T(8,128)(2,1)S(1)}, u32[]{:S(2)}, u32[]{:S(2)}) collective-permute-start(bf16[128,2048]{1,0:T(8,128)(2,1)S(1)} %get-tuple-element.123.share), channel_id=1, source_target_pairs={{16,31},{17,30},{18,25},{19,24},{20,27},{21,26},{22,29},{23,28}} | collective-permute-start | bytes 1572872 | tf_op jit(solution)/shard_map/ppermute | solution.py:302
  51.0 20.6 %collective-permute-start.11 = (bf16[128,2048]{1,0:T(8,128)(2,1)S(1)}, bf16[128,2048]{1,0:T(8,128)(2,1)S(1)}, u32[]{:S(2)}, u32[]{:S(2)}) collective-permute-start(bf16[128,2048]{1,0:T(8,128)(2,1)S(1)} %get-tuple-element.123.share), channel_id=1, source_target_pairs={{16,30},{17,31},{18,24},{19,25},{20,26},{21,27},{22,28},{23,29}} | collective-permute-start | bytes 1572872 | tf_op jit(solution)/shard_map/ppermute | solution.py:302
  52.4 20.3 %collective-permute-start.14 = (bf16[128,2048]{1,0:T(8,128)(2,1)S(1)}, bf16[128,2048]{1,0:T(8,128)(2,1)S(1)}, u32[]{:S(2)}, u32[]{:S(2)}) collective-permute-start(bf16[128,2048]{1,0:T(8,128)(2,1)S(1)} %get-tuple-element.125), channel_id=1, source_target_pairs={{16,25},{17,24},{18,27},{19,26},{20,29},{21,28},{22,31},{23,30}} | collective-permute-start | bytes 1572872 | tf_op jit(solution)/shard_map/ppermute | solution.py:302
  53.7 19.0 %collective-permute-start.13 = (bf16[128,2048]{1,0:T(8,128)(2,1)S(1)}, bf16[128,2048]{1,0:T(8,128)(2,1)S(1)}, u32[]{:S(2)}, u32[]{:S(2)}) collective-permute-start(bf16[128,2048]{1,0:T(8,128)(2,1)S(1)} %get-tuple-element.125), channel_id=1, source_target_pairs={{16,24},{17,25},{18,26},{19,27},{20,28},{21,29},{22,30},{23,31}} | collective-permute-start | bytes 1572872 | tf_op jit(solution)/shard_map/ppermute | solution.py:302
  55.0 21.3 %collective-permute-start.16 = (bf16[128,1024]{1,0:T(8,128)(2,1)S(1)}, bf16[128,1024]{1,0:T(8,128)(2,1)S(1)}, u32[]{:S(2)}, u32[]{:S(2)}) collective-permute-start(bf16[128,1024]{1,0:T(8,128)(2,1)S(1)} %after.5), channel_id=1, source_target_pairs={{8,2},{9,3},{10,4},{11,5},{12,6},{13,7},{14,0},{15,1},{16,17},{17,... | collective-permute-start | bytes 786440 | tf_op jit(solution)/shard_map/ppermute | solution.py:302
  74.9 6.5 %collective-permute-start.15 = (bf16[128,1024]{1,0:T(8,128)(2,1)S(1)}, bf16[128,1024]{1,0:T(8,128)(2,1)S(1)}, u32[]{:S(2)}, u32[]{:S(2)}) collective-permute-start(bf16[128,1024]{1,0:T(8,128)(2,1)S(1)} %get-tuple-element.136), channel_id=1, source_target_pairs={{24,19},{25,18},{26,21},{27,20},{28,23},{29,22},{30,17},{31,16}} | collective-permute-start | bytes 786440 | tf_op jit(solution)/shard_map/ppermute | solution.py:302
  77.5 6.2 %collective-permute-start.17 = (bf16[128,1024]{1,0:T(8,128)(2,1)S(1)}, bf16[128,1024]{1,0:T(8,128)(2,1)S(1)}, u32[]{:S(2)}, u32[]{:S(2)}) collective-permute-start(bf16[128,1024]{1,0:T(8,128)(2,1)S(1)} %get-tuple-element.142), channel_id=1, source_target_pairs={{24,17},{25,16},{26,19},{27,18},{28,21},{29,20},{30,23},{31,22}} | collective-permute-start | bytes 786440 | tf_op jit(solution)/shard_map/ppermute | solution.py:302
  78.8 4.9 %collective-permute-start.18 = (bf16[128,1024]{1,0:T(8,128)(2,1)S(1)}, bf16[128,1024]{1,0:T(8,128)(2,1)S(1)}, u32[]{:S(2)}, u32[]{:S(2)}) collective-permute-start(bf16[128,1024]{1,0:T(8,128)(2,1)S(1)} %get-tuple-element.144), channel_id=1, source_target_pairs={{24,18},{25,19},{26,20},{27,21},{28,22},{29,23},{30,16},{31,17}} | collective-permute-start | bytes 786440 | tf_op jit(solution)/shard_map/ppermute | solution.py:302
  80.1 3.6 %collective-permute-start.19 = (bf16[256,1024]{1,0:T(8,128)(2,1)S(1)}, bf16[256,1024]{1,0:T(8,128)(2,1)S(1)}, u32[]{:S(2)}, u32[]{:S(2)}) collective-permute-start(bf16[256,1024]{1,0:T(8,128)(2,1)S(1)} %get-tuple-element.149), channel_id=1, source_target_pairs={{8,0},{9,1},{10,2},{11,3},{12,4},{13,5},{14,6},{15,7},{16,8},{17,9... | collective-permute-start | bytes 1572872 | tf_op jit(solution)/shard_map/ppermute | solution.py:302
  83.7 5.3 %collective-permute-start.20 = (bf16[256,1024]{1,0:T(8,128)(2,1)S(1)}, bf16[256,1024]{1,0:T(8,128)(2,1)S(1)}, u32[]{:S(2)}, u32[]{:S(2)}) collective-permute-start(bf16[256,1024]{1,0:T(8,128)(2,1)S(1)} %get-tuple-element.150), channel_id=1, source_target_pairs={{16,24},{17,25},{18,26},{19,27},{20,28},{21,29},{22,30},{23,31}} | collective-permute-start | bytes 1572872 | tf_op jit(solution)/shard_map/ppermute | solution.py:302
  (3 other events, 3.9 us)

commit v5 on v4

--- a/solution.py
+++ b/solution.py
@@ -20,18 +20,16 @@
 MARK = jax.ShapeDtypeStruct((8, 128), jnp.float32)
 
 
-def project_kernel(section, chunk_order, n_parts, keep, first_row, mark, *refs):
-    parts, refs = refs[:n_parts], refs[n_parts:]
-    scale, weight, refs = refs[0], refs[1], refs[2 + 2 * (first_row > 0) :]
-    before, refs = (refs[0], refs[1:]) if keep == "hand on" else (None, refs)
-    x_ref, q_ref, k_ref, v_ref, refs = *refs[:4], refs[4:]
-    kept = refs[0] if keep else None
-    u_ref = refs[-1]
+def project_kernel(section, chunk_order, n_parts, n_filled, first_row, keep_row, mark, *refs):
+    parts, scale, weight = refs[:n_parts], refs[n_parts], refs[n_parts + 1]
+    x_ref, q_ref, k_ref, v_ref, *kept, _ = refs[n_parts + 2 + n_filled :]
     channels = q_ref.shape[1]
+    rows_here = len(chunk_order) * HALF
 
     @pl.when(lax.axis_index("pipe") == section)
     def _():
         mine = pl.ds(pl.multiple_of(lax.axis_index("head") * channels, channels), channels)
+        inverse = [None] * len(chunk_order)
         for source, target in enumerate(chunk_order):
             rows = pl.ds(source * HALF, HALF)
             put = pl.ds(target * HALF, HALF)
@@ -42,38 +40,37 @@
             x_ref[put, :] = x
             wide = x.astype(jnp.float32)
             mean_square = jnp.mean(wide * wide, axis=1, keepdims=True)
-            u_ref[put, :] = (wide * lax.rsqrt(mean_square + EPSILON)).astype(u_ref.dtype)
-        key = u_ref[:, mine]
-        here = slice(first_row, first_row + u_ref.shape[0])
+            inverse[target] = lax.rsqrt(mean_square + EPSILON)
+        inverse = jnp.concatenate(inverse, axis=0)
+        here = slice(first_row, first_row + rows_here)
+        values = jnp.dot(x_ref[...], weight[...], preferred_element_type=jnp.float32)
+        v_ref[here, :] = (values * inverse).astype(v_ref.dtype)
+        key = (x_ref[:, mine].astype(jnp.float32) * inverse).astype(k_ref.dtype)
         k_ref[here, :] = key
         q_ref[...] = (key.astype(jnp.float32) * scale[:, mine]).astype(q_ref.dtype)
-        v_ref[here, :] = jnp.dot(
-            u_ref[...], weight[...], preferred_element_type=jnp.float32
-        ).astype(v_ref.dtype)
-        if keep:
-            kept[...] = x_ref[:, mine]
-
-    if keep == "hand on":
-
-        @pl.when(lax.axis_index("pipe") != section)
-        def _():
-            kept[...] = before[...]
-
-
-def project(section, chunk_order, parts, mark, scale, weight, first_row, total_rows, filled, keep="", before=()):
+        for target in kept:
+            target[keep_row : keep_row + rows_here, :] = x_ref[:, mine]
+
+
+def project(section, chunk_order, parts, mark, scale, weight, first_row, total_rows, filled, kept=None, keep_rows=0):
     rows, width = parts[0].shape
     channels = weight.shape[1]
     shapes = [(rows, width), (rows, channels)] + [(total_rows, channels)] * 2
-    shapes += [(rows, channels)] * (1 if keep else 0)
-    arrays = [*parts, scale, weight, *filled, *before]
+    shapes += [(keep_rows, channels)] if keep_rows else []
+    arrays = [*parts, scale, weight, *filled] + ([] if kept is None else [kept])
     at = 1 + len(parts) + 2
-    return pl.pallas_call(
-        functools.partial(project_kernel, section, chunk_order, len(parts), keep, first_row),
+    aliases = {at: 2, at + 1: 3} if filled else {}
+    if kept is not None:
+        aliases[len(arrays)] = 4
+    keep_row = first_row if keep_rows > rows else 0
+    return pl.pallas_call(
+        functools.partial(
+            project_kernel, section, chunk_order, len(parts), len(arrays) - at + 1, first_row, keep_row
+        ),
         out_shape=tuple(jax.ShapeDtypeStruct(shape, jnp.bfloat16) for shape in shapes) + (MARK,),
         in_specs=[anywhere] + [vmem] * len(arrays),
         out_specs=(vmem,) * len(shapes) + (anywhere,),
-        input_output_aliases={at: 2, at + 1: 3} if filled else {},
-        scratch_shapes=[pltpu.VMEM((rows, width), jnp.bfloat16)],
+        input_output_aliases=aliases,
         compiler_params=pltpu.CompilerParams(vmem_limit_bytes=VMEM_LIMIT),
         cost_estimate=pl.CostEstimate(
             flops=2 * rows * width * channels, bytes_accessed=2 * width * channels, transcendentals=0
@@ -145,15 +142,10 @@
 
         @pl.when(lax.axis_index("pipe") != section)
         def _():
-            outs[1][...] = kept[0][...]
+            outs[1][...] = kept[0][: o_ref.shape[0], :]
 
     elif carry:
-        rows = o_ref.shape[0]
-        outs[0][rows:, :] = kept[1][...]
-
-        @pl.when(lax.axis_index("pipe") != section)
-        def _():
-            outs[0][:rows, :] = kept[0][...]
+        outs[0][o_ref.shape[0] :, :] = kept[0][...]
 
 
 def attend(section, pieces, blocks, mark, weight, split, kept=(), share=False):
@@ -213,7 +205,7 @@
     )(mark, *before, *terms)
 
 
-def finish_kernel(last, total, second, share, *refs):
+def finish_kernel(last, total, second, given, share, *refs):
     shared, out = refs[:-1], refs[-1]
     shape = (out.shape[0], HALF, out.shape[2])
     rows, channels = shared[0].shape
@@ -225,18 +217,6 @@
         out[:, first_half, :] = total[:rows, :].reshape(shape)
         out[:, second_half, :] = total[rows:, :].reshape(shape)
 
-    @pl.when(stage != last)
-    def _():
-        out[:, second_half, :] = second[rows:, :].reshape(shape)
-
-    @pl.when((stage < last - 1) & (stage % 2 == 0))
-    def _():
-        out[:, first_half, :] = shared[0][...].reshape(shape)
-
-    @pl.when((stage < last - 1) & (stage % 2 == 1))
-    def _():
-        out[:, first_half, :] = second[:rows, :].reshape(shape)
-
     @pl.when(stage == last - 1)
     def _():
         mine = pl.ds(pl.multiple_of(lax.axis_index("head") * channels, channels), channels)
@@ -244,10 +224,23 @@
         for term in shared:
             value = value + term[...].astype(jnp.float32)
         out[:, first_half, :] = value.astype(out.dtype).reshape(shape)
-
-
-def finish(last, row_count, total, second, share, shared):
-    arrays = [total, second, share, *shared]
+        out[:, second_half, :] = second[rows:, :].reshape(shape)
+
+    @pl.when(stage < last - 1)
+    def _():
+        out[:, second_half, :] = given[rows:, :].reshape(shape)
+
+        @pl.when(stage % 2 == 0)
+        def _():
+            out[:, first_half, :] = shared[0][...].reshape(shape)
+
+        @pl.when(stage % 2 == 1)
+        def _():
+            out[:, first_half, :] = given[:rows, :].reshape(shape)
+
+
+def finish(last, row_count, total, second, given, share, shared):
+    arrays = [total, second, given, share, *shared]
     return pl.pallas_call(
         functools.partial(finish_kernel, last),
         out_shape=jax.ShapeDtypeStruct((row_count, WIN, total.shape[1]), jnp.bfloat16),
@@ -268,7 +261,7 @@
     )()
 
 
-def after(arrays, *marks):
+def after(arrays, *marks, flops=0):
     shapes = tuple(jax.ShapeDtypeStruct(array.shape, array.dtype) for array in arrays)
     return pl.pallas_call(
         lambda *refs: None,
@@ -277,6 +270,7 @@
         out_specs=(anywhere,) * len(arrays),
         input_output_aliases={place: place for place in range(len(arrays))},
         compiler_params=pltpu.CompilerParams(vmem_limit_bytes=1024 * 1024),
+        cost_estimate=pl.CostEstimate(flops=flops, bytes_accessed=flops // 100, transcendentals=0),
         name="after",
     )(*arrays, *marks)
 
@@ -317,8 +311,7 @@
         filled = block[2:]
     halves = [[(block, half * piece, piece) for block in range(n_head)] for half in range(2)]
     straight = tuple(range(row_count * n_head))
-    kept = [None, None]
-    back = [(source, source - 1, 0, 0) for source in range(1, sections)]
+    kept = None
 
     for section in range(sections):
         shift = section % 2
@@ -327,16 +320,16 @@
         moved = []
         for half in range(2):
             share = section + 2 == sections and not half
-            carried = kept[:1] if share else kept if last and half else []
+            carried = [kept] if share or last and half else []
             if last and half:
-                (mark,) = after([mark], *early)
+                (mark,) = after([mark], given, *early)
             *part, mark = attend(section, halves[half], blocks, mark, out_rows, last, carried, share)
             if share:
                 own_share, *shared = part
             cross = 0 if half else shift if last else 1 if shift else -1
             if last and half:
                 terms = [send(part[turn], section, section - 1, 0, turn) for turn in range(1, n_head)]
-                terms += [send_all(part[0], back)]
+                terms += [send(part[0], section, section - 1)]
             elif last:
                 terms = [send(part[turn], section, section - 1, cross, turn) for turn in range(n_head)]
             elif shift and not half:
@@ -352,16 +345,19 @@
             total, mark = add(section - 1, moved[1], mark)
             moved[1] = [send(total, section - 1, section + 1)]
         if section + 2 == sections:
+            straight_back = [(source, source - 1, 0, 0) for source in range(1, section + 1)]
             across = [(source, source - 1, 1, 0) for source in range(1, section, 2)]
+            *shared, early_kept = after([*shared, kept], mark)
             early = [
                 send_all(block, ([] if turn else across) + [(section, section, 0, turn + 1)])
-                for turn, block in enumerate(after(shared, mark))
+                for turn, block in enumerate(shared)
             ]
+            given = send_all(early_kept, straight_back)
+            kept = None
         if not last:
             blocks, filled, rows = [], (), piece * n_head
             for half in range(2):
-                keep = "" if section + 2 == sections and not half else "hand on" if section else "start"
-                before = [kept[half]] if keep == "hand on" else []
+                keep_rows = 2 * rows if section + 2 < sections else half * rows
                 *block, mark = project(
                     section + 1,
                     straight,
@@ -372,20 +368,20 @@
                     half * rows,
                     2 * rows,
                     filled,
-                    keep,
-                    before,
+                    kept,
+                    keep_rows,
                 )
-                if keep:
-                    *block, kept[half] = block
+                if keep_rows:
+                    *block, kept = block
                 blocks.append(block)
                 filled = block[2:]
             halves = [[(0, 0, piece * n_head)], [(1, 0, piece * n_head)]]
-    *across, mark = after([*moved[0][1:], mark])
+    *across, mark = after([*moved[0][1:], mark], flops=4 * 10**9)
+    first, mark = add(sections - 2, [moved[0][0], *across], mark, 10**8)
     second, mark = add(sections - 2, moved[1][:-1], mark, 4 * 10**9)
-    first, mark = add(sections - 2, [moved[0][0], *across], mark, 4 * 10**9)
     total, mark = add(sections - 2, [second, moved[1][-1]], mark, 0, (first,))
     total = send(total, sections - 2, sections - 1)
-    return finish(sections - 1, row_count * n_head, total, moved[1][-1], own_share, early)[None]
+    return finish(sections - 1, row_count * n_head, total, moved[1][-1], given, own_share, early)[None]
 
 
 def solution(mesh):

time: 90.4 us -> 89.8 us (level)
  waiting for transfers between devices: 54.3 us -> 53.3 us
    ppermute x21 -> x22, waiting for transfers between devices: 54.3 us -> 53.3 us  [send_all(): return lax.ppermute(value, AXES, pairs)]
    ppermute x21 -> x22, starting transfers between devices: 22 us -> 22.6 us  [send_all(): return lax.ppermute(value, AXES, pairs)]
  transfers between devices with their start and end apart: 21 -> 22, of which waited for: 6 -> 7; matrix products, arithmetic and copies ran while one was open for 0% -> 0% of each run, Pallas kernels for 5% -> 5%
where the time goes in v5:
time: 89.8 us; the launch traced here: 89.2 us
  waiting for transfers between devices  53.3 us (59%)
  starting transfers between devices  22.6 us (25%)
  local copies, waits for them, and re-layouts  7.38 us (8%)
  Pallas kernels  5.51 us (6%)
    ppermute x22, waiting for transfers between devices, send_all(): return lax.ppermute(value, AXES, pairs)  53.3 us
    ppermute x22, starting transfers between devices, send_all(): return lax.ppermute(value, AXES, pairs)  22.6 us
    unnamed x12, local copies, waits for them, and re-layouts  7.38 us
    pallas_call x8, Pallas kernels, attend(): pl.pallas_call(functools.partial(attend_kernel, section, pieces, len(bloc...  2.65 us
    pallas_call x8, Pallas kernels, project(): pl.pallas_call(functools.partial(project_kernel, section, chunk_order, le...  2 us
  transfers between devices with their start and end apart: 22, of which 7 were waited for; matrix products, arithmetic and copies ran while one was open for 0% of the time, Pallas kernels for 5%

profile of v5, /device:TPU:5, one launch (start us, length us, event | category | flops | bytes accessed | tf_op | source)
XLA Modules:
  0.0 89.2 jit_solution(878687407334382654)
XLA Ops:
  0.7 2.2 %copy-done = bf16[1,2048,1024]{2,1,0:T(8,128)(2,1)S(1)} copy-done((bf16[1,2048,1024]{2,1,0:T(8,128)(2,1)S(1)}, bf16[1,2048,1024]{2,1,0:T(8,128)(2,1)}, u32[]{:S(2)}) %copy-start) | copy-done | bytes 4194328
  3.6 1.0 %copy-done.5 = bf16[4,32,2048]{2,1,0:T(8,128)(2,1)S(1)} copy-done((bf16[4,32,2048]{2,1,0:T(8,128)(2,1)S(1)}, bf16[4,32,2048]{2,1,0:T(8,128)(2,1)}, u32[]{:S(2)}) %copy-start.5) | copy-done | bytes 524312
  4.6 2.2 %copy-done.1 = bf16[1,2048,1024]{2,1,0:T(8,128)(2,1)S(1)} copy-done((bf16[1,2048,1024]{2,1,0:T(8,128)(2,1)S(1)}, bf16[1,2048,1024]{2,1,0:T(8,128)(2,1)}, u32[]{:S(2)}) %copy-start.1) | copy-done | bytes 4194328
  6.8 1.3 %copy-done.2 = bf16[1,1024,2048]{2,1,0:T(8,128)(2,1)S(1)} copy-done((bf16[1,1024,2048]{2,1,0:T(8,128)(2,1)S(1)}, bf16[1,1024,2048]{2,1,0:T(8,128)(2,1)}, u32[]{:S(2)}) %copy-start.2) | copy-done | bytes 4194328
  11.2 1.3 %collective-permute-start.7 = (bf16[128,2048]{1,0:T(8,128)(2,1)S(1)}, bf16[128,2048]{1,0:T(8,128)(2,1)S(1)}, u32[]{:S(2)}, u32[]{:S(2)}) collective-permute-start(bf16[128,2048]{1,0:T(8,128)(2,1)S(1)} %get-tuple-element.109), channel_id=1, source_target_pairs={{8,26},{9,27},{10,28},{11,29},{12,30},{13,31},{14,24},{15,25}} | collective-permute-start | bytes 1572872 | tf_op jit(solution)/shard_map/ppermute | solution.py:296
  13.9 27.9 %collective-permute-done.7.refs_0_ = bf16[128,2048]{1,0:T(8,128)(2,1)S(1)} collective-permute-done((bf16[128,2048]{1,0:T(8,128)(2,1)S(1)}, bf16[128,2048]{1,0:T(8,128)(2,1)S(1)}, u32[]{:S(2)}, u32[]{:S(2)}) %collective-permute-start.7) | collective-permute-done | bytes 524320 | tf_op jit(solution)/shard_map/ppermute | solution.py:296
  41.8 1.3 %collective-permute-start.9 = (bf16[128,2048]{1,0:T(8,128)(2,1)S(1)}, bf16[128,2048]{1,0:T(8,128)(2,1)S(1)}, u32[]{:S(2)}, u32[]{:S(2)}) collective-permute-start(bf16[128,2048]{1,0:T(8,128)(2,1)S(1)} %after.4), channel_id=1, source_target_pairs={{24,17},{25,16},{26,19},{27,18},{28,21},{29,20},{30,23},{31,22}} | collective-permute-start | bytes 1572872 | tf_op jit(solution)/shard_map/ppermute | solution.py:296
  43.1 1.3 %collective-permute-start.8 = (bf16[128,2048]{1,0:T(8,128)(2,1)S(1)}, bf16[128,2048]{1,0:T(8,128)(2,1)S(1)}, u32[]{:S(2)}, u32[]{:S(2)}) collective-permute-start(bf16[128,2048]{1,0:T(8,128)(2,1)S(1)} %after.4), channel_id=1, source_target_pairs={{24,16},{25,17},{26,18},{27,19},{28,20},{29,21},{30,22},{31,23}} | collective-permute-start | bytes 1572872 | tf_op jit(solution)/shard_map/ppermute | solution.py:296
  45.2 4.0 %collective-permute-done.9.refs_1_ = bf16[128,2048]{1,0:T(8,128)(2,1)S(1)} collective-permute-done((bf16[128,2048]{1,0:T(8,128)(2,1)S(1)}, bf16[128,2048]{1,0:T(8,128)(2,1)S(1)}, u32[]{:S(2)}, u32[]{:S(2)}) %collective-permute-start.9) | collective-permute-done | bytes 524320 | tf_op jit(solution)/shard_map/ppermute | solution.py:296
  49.3 1.3 %collective-permute-start.12 = (bf16[128,2048]{1,0:T(8,128)(2,1)S(1)}, bf16[128,2048]{1,0:T(8,128)(2,1)S(1)}, u32[]{:S(2)}, u32[]{:S(2)}) collective-permute-start(bf16[128,2048]{1,0:T(8,128)(2,1)S(1)} %get-tuple-element.126.share), channel_id=1, source_target_pairs={{16,31},{17,30},{18,25},{19,24},{20,27},{21,26},{22,29},{23,28}} | collective-permute-start | bytes 1572872 | tf_op jit(solution)/shard_map/ppermute | solution.py:296
  50.6 1.3 %collective-permute-start.11 = (bf16[128,2048]{1,0:T(8,128)(2,1)S(1)}, bf16[128,2048]{1,0:T(8,128)(2,1)S(1)}, u32[]{:S(2)}, u32[]{:S(2)}) collective-permute-start(bf16[128,2048]{1,0:T(8,128)(2,1)S(1)} %get-tuple-element.126.share), channel_id=1, source_target_pairs={{16,30},{17,31},{18,24},{19,25},{20,26},{21,27},{22,28},{23,29}} | collective-permute-start | bytes 1572872 | tf_op jit(solution)/shard_map/ppermute | solution.py:296
  52.1 1.3 %collective-permute-start.14 = (bf16[128,2048]{1,0:T(8,128)(2,1)S(1)}, bf16[128,2048]{1,0:T(8,128)(2,1)S(1)}, u32[]{:S(2)}, u32[]{:S(2)}) collective-permute-start(bf16[128,2048]{1,0:T(8,128)(2,1)S(1)} %get-tuple-element.128), channel_id=1, source_target_pairs={{16,25},{17,24},{18,27},{19,26},{20,29},{21,28},{22,31},{23,30}} | collective-permute-start | bytes 1572872 | tf_op jit(solution)/shard_map/ppermute | solution.py:296
  53.4 1.3 %collective-permute-start.13 = (bf16[128,2048]{1,0:T(8,128)(2,1)S(1)}, bf16[128,2048]{1,0:T(8,128)(2,1)S(1)}, u32[]{:S(2)}, u32[]{:S(2)}) collective-permute-start(bf16[128,2048]{1,0:T(8,128)(2,1)S(1)} %get-tuple-element.128), channel_id=1, source_target_pairs={{16,24},{17,25},{18,26},{19,27},{20,28},{21,29},{22,30},{23,31}} | collective-permute-start | bytes 1572872 | tf_op jit(solution)/shard_map/ppermute | solution.py:296
  55.4 9.8 %collective-permute-done.12.refs_1_ = bf16[128,2048]{1,0:T(8,128)(2,1)S(1)} collective-permute-done((bf16[128,2048]{1,0:T(8,128)(2,1)S(1)}, bf16[128,2048]{1,0:T(8,128)(2,1)S(1)}, u32[]{:S(2)}, u32[]{:S(2)}) %collective-permute-start.12) | collective-permute-done | bytes 524320 | tf_op jit(solution)/shard_map/ppermute | solution.py:296
  65.8 5.2 %collective-permute-done.11.refs_0_ = bf16[128,2048]{1,0:T(8,128)(2,1)S(1)} collective-permute-done((bf16[128,2048]{1,0:T(8,128)(2,1)S(1)}, bf16[128,2048]{1,0:T(8,128)(2,1)S(1)}, u32[]{:S(2)}, u32[]{:S(2)}) %collective-permute-start.11) | collective-permute-done | bytes 524320 | tf_op jit(solution)/shard_map/ppermute | solution.py:296
  73.0 1.2 %attend.14 = (bf16[128,1024]{1,0:T(8,128)(2,1)S(1)}, bf16[128,1024]{1,0:T(8,128)(2,1)S(1)}, f32[8,128]{1,0:T(8,128)S(1)}) custom-call(f32[8,128]{1,0:T(8,128)S(1)} %get-tuple-element.131.mark, bf16[256,1024]{1,0:T(8,128)(2,1)S(1)} %get-tuple-element.132.k, bf16[256,1024]{1,0:T(8,128)(2,1)S(1)} %get-tuple-element.133.v, ...), custom_call_target="tpu_custom_call" | custom-call | flops 671088640 | bytes 4194304 | tf_op jit(solution)/shard_map/attend/pallas_call | solution.py:165
  74.2 1.3 %collective-permute-start.15 = (bf16[128,1024]{1,0:T(8,128)(2,1)S(1)}, bf16[128,1024]{1,0:T(8,128)(2,1)S(1)}, u32[]{:S(2)}, u32[]{:S(2)}) collective-permute-start(bf16[128,1024]{1,0:T(8,128)(2,1)S(1)} %get-tuple-element.138), channel_id=1, source_target_pairs={{24,19},{25,18},{26,21},{27,20},{28,23},{29,22},{30,17},{31,16}} | collective-permute-start | bytes 786440 | tf_op jit(solution)/shard_map/ppermute | solution.py:296
  75.5 1.2 %attend.15 = (bf16[256,1024]{1,0:T(8,128)(2,1)S(1)}, bf16[128,1024]{1,0:T(8,128)(2,1)S(1)}, f32[8,128]{1,0:T(8,128)S(1)}) custom-call(f32[8,128]{1,0:T(8,128)S(1)} %after.6.mark, bf16[256,1024]{1,0:T(8,128)(2,1)S(1)} %get-tuple-element.132.k, bf16[256,1024]{1,0:T(8,128)(2,1)S(1)} %get-tuple-element.133.v, bf16[128,2048]{1,0:T(8,128)(2,1)S(1)} %get-tuple-element.134.refs_0_, ...), custom_call_target="tpu_custom_call" | custom-call | flops 671088640 | bytes 4194304 | tf_op jit(solution)/shard_map/attend/pallas_call | solution.py:165
  76.7 1.3 %collective-permute-start.19 = (bf16[128,1024]{1,0:T(8,128)(2,1)S(1)}, bf16[128,1024]{1,0:T(8,128)(2,1)S(1)}, u32[]{:S(2)}, u32[]{:S(2)}) collective-permute-start(bf16[128,1024]{1,0:T(8,128)(2,1)S(1)} %get-tuple-element.149), channel_id=1, source_target_pairs={{24,17},{25,16},{26,19},{27,18},{28,21},{29,20},{30,23},{31,22}} | collective-permute-start | bytes 786440 | tf_op jit(solution)/shard_map/ppermute | solution.py:296
  78.1 1.3 %collective-permute-start.18 = (bf16[128,1024]{1,0:T(8,128)(2,1)S(1)}, bf16[128,1024]{1,0:T(8,128)(2,1)S(1)}, u32[]{:S(2)}, u32[]{:S(2)}) collective-permute-start(bf16[128,1024]{1,0:T(8,128)(2,1)S(1)} %get-tuple-element.146), channel_id=1, source_target_pairs={{24,18},{25,19},{26,20},{27,21},{28,22},{29,23},{30,16},{31,17}} | collective-permute-start | bytes 786440 | tf_op jit(solution)/shard_map/ppermute | solution.py:296
  79.4 1.3 %collective-permute-start.20 = (bf16[256,1024]{1,0:T(8,128)(2,1)S(1)}, bf16[256,1024]{1,0:T(8,128)(2,1)S(1)}, u32[]{:S(2)}, u32[]{:S(2)}) collective-permute-start(bf16[256,1024]{1,0:T(8,128)(2,1)S(1)} %get-tuple-element.153), channel_id=1, source_target_pairs={{24,16},{25,17},{26,18},{27,19},{28,20},{29,21},{30,22},{31,23}} | collective-permute-start | bytes 1572872 | tf_op jit(solution)/shard_map/ppermute | solution.py:296
  80.7 1.9 %collective-permute-done.18.refs_0_ = bf16[128,1024]{1,0:T(8,128)(2,1)S(1)} collective-permute-done((bf16[128,1024]{1,0:T(8,128)(2,1)S(1)}, bf16[128,1024]{1,0:T(8,128)(2,1)S(1)}, u32[]{:S(2)}, u32[]{:S(2)}) %collective-permute-start.18) | collective-permute-done | bytes 262176 | tf_op jit(solution)/shard_map/ppermute | solution.py:296
  83.0 1.3 %collective-permute-start.21 = (bf16[256,1024]{1,0:T(8,128)(2,1)S(1)}, bf16[256,1024]{1,0:T(8,128)(2,1)S(1)}, u32[]{:S(2)}, u32[]{:S(2)}) collective-permute-start(bf16[256,1024]{1,0:T(8,128)(2,1)S(1)} %get-tuple-element.154), channel_id=1, source_target_pairs={{16,24},{17,25},{18,26},{19,27},{20,28},{21,29},{22,30},{23,31}} | collective-permute-start | bytes 1572872 | tf_op jit(solution)/shard_map/ppermute | solution.py:296
  84.3 4.1 %collective-permute-done.21.total = bf16[256,1024]{1,0:T(8,128)(2,1)S(1)} collective-permute-done((bf16[256,1024]{1,0:T(8,128)(2,1)S(1)}, bf16[256,1024]{1,0:T(8,128)(2,1)S(1)}, u32[]{:S(2)}, u32[]{:S(2)}) %collective-permute-start.21) | collective-permute-done | bytes 524320 | tf_op jit(solution)/shard_map/ppermute | solution.py:296
  (58 shorter events, 11.3 us)
Async XLA Ops:
  0.0 4.6 %collective-permute-start = (bf16[128,2048]{1,0:T(8,128)(2,1)}, bf16[128,2048]{1,0:T(8,128)(2,1)S(1)}, u32[]{:S(2)}, u32[]{:S(2)}) collective-permute-start(bf16[128,2048]{1,0:T(8,128)(2,1)} %bitcast.20), channel_id=1, source_target_pairs={{0,1},{1,0},{2,3},{3,2},{4,5},{5,4},{6,7},{7,6}} | collective-permute-start | bytes 1572872 | tf_op jit(solution)/shard_map/ppermute | solution.py:296
  4.6 3.5 %copy-start.2 = (bf16[1,1024,2048]{2,1,0:T(8,128)(2,1)S(1)}, bf16[1,1024,2048]{2,1,0:T(8,128)(2,1)}, u32[]{:S(2)}) copy-start(bf16[1,1024,2048]{2,1,0:T(8,128)(2,1)} %param.7) | copy-start | bytes 12582916
  8.1 3.0 %copy-start.4 = (f32[1,2048]{1,0:T(1,128)S(1)}, f32[1,2048]{1,0:T(1,128)}, u32[]{:S(2)}) copy-start(f32[1,2048]{1,0:T(1,128)} %refs_2_.9) | copy-start | bytes 24580
  8.1 3.0 %collective-permute-start.2 = (bf16[128,2048]{1,0:T(8,128)(2,1)S(1)}, bf16[128,2048]{1,0:T(8,128)(2,1)S(1)}, u32[]{:S(2)}, u32[]{:S(2)}) collective-permute-start(bf16[128,2048]{1,0:T(8,128)(2,1)S(1)} %get-tuple-element.92), channel_id=1, source_target_pairs={{0,15},{1,14},{2,9},{3,8},{4,11},{5,10},{6,13},{7,12}} | collective-permute-start | bytes 1572872 | tf_op jit(solution)/shard_map/ppermute | solution.py:296
  8.9 2.1 %collective-permute-start.1 = (bf16[128,2048]{1,0:T(8,128)(2,1)S(1)}, bf16[128,2048]{1,0:T(8,128)(2,1)S(1)}, u32[]{:S(2)}, u32[]{:S(2)}) collective-permute-start(bf16[128,2048]{1,0:T(8,128)(2,1)S(1)} %get-tuple-element.92), channel_id=1, source_target_pairs={{0,14},{1,15},{2,8},{3,9},{4,10},{5,11},{6,12},{7,13}} | collective-permute-start | bytes 1572872 | tf_op jit(solution)/shard_map/ppermute | solution.py:296
  9.7 1.5 %collective-permute-start.4 = (bf16[128,2048]{1,0:T(8,128)(2,1)S(1)}, bf16[128,2048]{1,0:T(8,128)(2,1)S(1)}, u32[]{:S(2)}, u32[]{:S(2)}) collective-permute-start(bf16[128,2048]{1,0:T(8,128)(2,1)S(1)} %get-tuple-element.94), channel_id=1, source_target_pairs={{0,9},{1,8},{2,11},{3,10},{4,13},{5,12},{6,15},{7,14}} | collective-permute-start | bytes 1572872 | tf_op jit(solution)/shard_map/ppermute | solution.py:296
  10.4 0.8 collective-permute-start.3
  11.2 30.6 %collective-permute-start.7 = (bf16[128,2048]{1,0:T(8,128)(2,1)S(1)}, bf16[128,2048]{1,0:T(8,128)(2,1)S(1)}, u32[]{:S(2)}, u32[]{:S(2)}) collective-permute-start(bf16[128,2048]{1,0:T(8,128)(2,1)S(1)} %get-tuple-element.109), channel_id=1, source_target_pairs={{8,26},{9,27},{10,28},{11,29},{12,30},{13,31},{14,24},{15,25}} | collective-permute-start | bytes 1572872 | tf_op jit(solution)/shard_map/ppermute | solution.py:296
  12.5 32.0 %collective-permute-start.6 = (bf16[128,2048]{1,0:T(8,128)(2,1)S(1)}, bf16[128,2048]{1,0:T(8,128)(2,1)S(1)}, u32[]{:S(2)}, u32[]{:S(2)}) collective-permute-start(bf16[128,2048]{1,0:T(8,128)(2,1)S(1)} %get-tuple-element.107), channel_id=1, source_target_pairs={{8,1},{9,0},{10,3},{11,2},{12,5},{13,4},{14,7},{15,6}} | collective-permute-start | bytes 1572872 | tf_op jit(solution)/shard_map/ppermute | solution.py:296
  13.2 31.3 %collective-permute-start.5 = (bf16[128,2048]{1,0:T(8,128)(2,1)S(1)}, bf16[128,2048]{1,0:T(8,128)(2,1)S(1)}, u32[]{:S(2)}, u32[]{:S(2)}) collective-permute-start(bf16[128,2048]{1,0:T(8,128)(2,1)S(1)} %get-tuple-element.107), channel_id=1, source_target_pairs={{8,0},{9,1},{10,2},{11,3},{12,4},{13,5},{14,6},{15,7}} | collective-permute-start | bytes 1572872 | tf_op jit(solution)/shard_map/ppermute | solution.py:296
  41.8 7.4 %collective-permute-start.9 = (bf16[128,2048]{1,0:T(8,128)(2,1)S(1)}, bf16[128,2048]{1,0:T(8,128)(2,1)S(1)}, u32[]{:S(2)}, u32[]{:S(2)}) collective-permute-start(bf16[128,2048]{1,0:T(8,128)(2,1)S(1)} %after.4), channel_id=1, source_target_pairs={{24,17},{25,16},{26,19},{27,18},{28,21},{29,20},{30,23},{31,22}} | collective-permute-start | bytes 1572872 | tf_op jit(solution)/shard_map/ppermute | solution.py:296
  43.1 6.1 %collective-permute-start.8 = (bf16[128,2048]{1,0:T(8,128)(2,1)S(1)}, bf16[128,2048]{1,0:T(8,128)(2,1)S(1)}, u32[]{:S(2)}, u32[]{:S(2)}) collective-permute-start(bf16[128,2048]{1,0:T(8,128)(2,1)S(1)} %after.4), channel_id=1, source_target_pairs={{24,16},{25,17},{26,18},{27,19},{28,20},{29,21},{30,22},{31,23}} | collective-permute-start | bytes 1572872 | tf_op jit(solution)/shard_map/ppermute | solution.py:296
  44.5 4.7 %collective-permute-start.10 = (bf16[128,2048]{1,0:T(8,128)(2,1)S(1)}, bf16[128,2048]{1,0:T(8,128)(2,1)S(1)}, u32[]{:S(2)}, u32[]{:S(2)}) collective-permute-start(bf16[128,2048]{1,0:T(8,128)(2,1)S(1)} %get-tuple-element.112), channel_id=1, source_target_pairs={{0,16},{1,17},{2,18},{3,19},{4,20},{5,21},{6,22},{7,23}} | collective-permute-start | bytes 1572872 | tf_op jit(solution)/shard_map/ppermute | solution.py:296
  49.3 15.9 %collective-permute-start.12 = (bf16[128,2048]{1,0:T(8,128)(2,1)S(1)}, bf16[128,2048]{1,0:T(8,128)(2,1)S(1)}, u32[]{:S(2)}, u32[]{:S(2)}) collective-permute-start(bf16[128,2048]{1,0:T(8,128)(2,1)S(1)} %get-tuple-element.126.share), channel_id=1, source_target_pairs={{16,31},{17,30},{18,25},{19,24},{20,27},{21,26},{22,29},{23,28}} | collective-permute-start | bytes 1572872 | tf_op jit(solution)/shard_map/ppermute | solution.py:296
  50.6 20.4 %collective-permute-start.11 = (bf16[128,2048]{1,0:T(8,128)(2,1)S(1)}, bf16[128,2048]{1,0:T(8,128)(2,1)S(1)}, u32[]{:S(2)}, u32[]{:S(2)}) collective-permute-start(bf16[128,2048]{1,0:T(8,128)(2,1)S(1)} %get-tuple-element.126.share), channel_id=1, source_target_pairs={{16,30},{17,31},{18,24},{19,25},{20,26},{21,27},{22,28},{23,29}} | collective-permute-start | bytes 1572872 | tf_op jit(solution)/shard_map/ppermute | solution.py:296
  52.1 19.9 %collective-permute-start.14 = (bf16[128,2048]{1,0:T(8,128)(2,1)S(1)}, bf16[128,2048]{1,0:T(8,128)(2,1)S(1)}, u32[]{:S(2)}, u32[]{:S(2)}) collective-permute-start(bf16[128,2048]{1,0:T(8,128)(2,1)S(1)} %get-tuple-element.128), channel_id=1, source_target_pairs={{16,25},{17,24},{18,27},{19,26},{20,29},{21,28},{22,31},{23,30}} | collective-permute-start | bytes 1572872 | tf_op jit(solution)/shard_map/ppermute | solution.py:296
  53.4 18.6 %collective-permute-start.13 = (bf16[128,2048]{1,0:T(8,128)(2,1)S(1)}, bf16[128,2048]{1,0:T(8,128)(2,1)S(1)}, u32[]{:S(2)}, u32[]{:S(2)}) collective-permute-start(bf16[128,2048]{1,0:T(8,128)(2,1)S(1)} %get-tuple-element.128), channel_id=1, source_target_pairs={{16,24},{17,25},{18,26},{19,27},{20,28},{21,29},{22,30},{23,31}} | collective-permute-start | bytes 1572872 | tf_op jit(solution)/shard_map/ppermute | solution.py:296
  54.7 20.8 %collective-permute-start.16 = (bf16[256,1024]{1,0:T(8,128)(2,1)S(1)}, bf16[256,1024]{1,0:T(8,128)(2,1)S(1)}, u32[]{:S(2)}, u32[]{:S(2)}) collective-permute-start(bf16[256,1024]{1,0:T(8,128)(2,1)S(1)} %get-tuple-element.141), channel_id=1, source_target_pairs={{8,0},{9,1},{10,2},{11,3},{12,4},{13,5},{14,6},{15,7},{16,8},{17,9... | collective-permute-start | bytes 1572872 | tf_op jit(solution)/shard_map/ppermute | solution.py:296
  65.1 10.4 %collective-permute-start.17 = (bf16[128,1024]{1,0:T(8,128)(2,1)S(1)}, bf16[128,1024]{1,0:T(8,128)(2,1)S(1)}, u32[]{:S(2)}, u32[]{:S(2)}) collective-permute-start(bf16[128,1024]{1,0:T(8,128)(2,1)S(1)} %get-tuple-element.142), channel_id=1, source_target_pairs={{8,2},{9,3},{10,4},{11,5},{12,6},{13,7},{14,0},{15,1},{16,17},{17,... | collective-permute-start | bytes 786440 | tf_op jit(solution)/shard_map/ppermute | solution.py:296
  74.2 6.5 %collective-permute-start.15 = (bf16[128,1024]{1,0:T(8,128)(2,1)S(1)}, bf16[128,1024]{1,0:T(8,128)(2,1)S(1)}, u32[]{:S(2)}, u32[]{:S(2)}) collective-permute-start(bf16[128,1024]{1,0:T(8,128)(2,1)S(1)} %get-tuple-element.138), channel_id=1, source_target_pairs={{24,19},{25,18},{26,21},{27,20},{28,23},{29,22},{30,17},{31,16}} | collective-permute-start | bytes 786440 | tf_op jit(solution)/shard_map/ppermute | solution.py:296
  76.7 6.3 %collective-permute-start.19 = (bf16[128,1024]{1,0:T(8,128)(2,1)S(1)}, bf16[128,1024]{1,0:T(8,128)(2,1)S(1)}, u32[]{:S(2)}, u32[]{:S(2)}) collective-permute-start(bf16[128,1024]{1,0:T(8,128)(2,1)S(1)} %get-tuple-element.149), channel_id=1, source_target_pairs={{24,17},{25,16},{26,19},{27,18},{28,21},{29,20},{30,23},{31,22}} | collective-permute-start | bytes 786440 | tf_op jit(solution)/shard_map/ppermute | solution.py:296
  78.1 4.6 %collective-permute-start.18 = (bf16[128,1024]{1,0:T(8,128)(2,1)S(1)}, bf16[128,1024]{1,0:T(8,128)(2,1)S(1)}, u32[]{:S(2)}, u32[]{:S(2)}) collective-permute-start(bf16[128,1024]{1,0:T(8,128)(2,1)S(1)} %get-tuple-element.146), channel_id=1, source_target_pairs={{24,18},{25,19},{26,20},{27,21},{28,22},{29,23},{30,16},{31,17}} | collective-permute-start | bytes 786440 | tf_op jit(solution)/shard_map/ppermute | solution.py:296
  79.4 3.6 %collective-permute-start.20 = (bf16[256,1024]{1,0:T(8,128)(2,1)S(1)}, bf16[256,1024]{1,0:T(8,128)(2,1)S(1)}, u32[]{:S(2)}, u32[]{:S(2)}) collective-permute-start(bf16[256,1024]{1,0:T(8,128)(2,1)S(1)} %get-tuple-element.153), channel_id=1, source_target_pairs={{24,16},{25,17},{26,18},{27,19},{28,20},{29,21},{30,22},{31,23}} | collective-permute-start | bytes 1572872 | tf_op jit(solution)/shard_map/ppermute | solution.py:296
  83.0 5.4 %collective-permute-start.21 = (bf16[256,1024]{1,0:T(8,128)(2,1)S(1)}, bf16[256,1024]{1,0:T(8,128)(2,1)S(1)}, u32[]{:S(2)}, u32[]{:S(2)}) collective-permute-start(bf16[256,1024]{1,0:T(8,128)(2,1)S(1)} %get-tuple-element.154), channel_id=1, source_target_pairs={{16,24},{17,25},{18,26},{19,27},{20,28},{21,29},{22,30},{23,31}} | collective-permute-start | bytes 1572872 | tf_op jit(solution)/shard_map/ppermute | solution.py:296
  (4 other events, 6.1 us)

commit v6 on v5

--- a/solution.py
+++ b/solution.py
@@ -20,9 +20,13 @@
 MARK = jax.ShapeDtypeStruct((8, 128), jnp.float32)
 
 
-def project_kernel(section, chunk_order, n_parts, n_filled, first_row, keep_row, mark, *refs):
-    parts, scale, weight = refs[:n_parts], refs[n_parts], refs[n_parts + 1]
-    x_ref, q_ref, k_ref, v_ref, *kept, _ = refs[n_parts + 2 + n_filled :]
+def project_kernel(section, chunk_order, counts, n_filled, first_row, keep_row, mark, *refs):
+    parts = []
+    for count in counts:
+        parts.append(refs[:count])
+        refs = refs[count:]
+    scale, weight = refs[:2]
+    x_ref, q_ref, k_ref, v_ref, *kept, _ = refs[2 + n_filled :]
     channels = q_ref.shape[1]
     rows_here = len(chunk_order) * HALF
 
@@ -33,9 +37,10 @@
         for source, target in enumerate(chunk_order):
             rows = pl.ds(source * HALF, HALF)
             put = pl.ds(target * HALF, HALF)
-            total = parts[0][rows, :].astype(jnp.float32)
-            for part in parts[1:]:
-                total = total + part[rows, :].astype(jnp.float32)
+            total = None
+            for part in parts:
+                term = join([columns[rows, :].astype(jnp.float32) for columns in part], 1)
+                total = term if total is None else total + term
             x = total.astype(x_ref.dtype)
             x_ref[put, :] = x
             wide = x.astype(jnp.float32)
@@ -53,19 +58,19 @@
 
 
 def project(section, chunk_order, parts, mark, scale, weight, first_row, total_rows, filled, kept=None, keep_rows=0):
-    rows, width = parts[0].shape
-    channels = weight.shape[1]
+    rows, (width, channels) = parts[0][0].shape[0], weight.shape
     shapes = [(rows, width), (rows, channels)] + [(total_rows, channels)] * 2
     shapes += [(keep_rows, channels)] if keep_rows else []
-    arrays = [*parts, scale, weight, *filled] + ([] if kept is None else [kept])
-    at = 1 + len(parts) + 2
+    counts = [len(part) for part in parts]
+    arrays = [block for part in parts for block in part] + [scale, weight, *filled] + ([] if kept is None else [kept])
+    at = 1 + sum(counts) + 2
     aliases = {at: 2, at + 1: 3} if filled else {}
     if kept is not None:
         aliases[len(arrays)] = 4
     keep_row = first_row if keep_rows > rows else 0
     return pl.pallas_call(
         functools.partial(
-            project_kernel, section, chunk_order, len(parts), len(arrays) - at + 1, first_row, keep_row
+            project_kernel, section, chunk_order, counts, len(arrays) - at + 1, first_row, keep_row
         ),
         out_shape=tuple(jax.ShapeDtypeStruct(shape, jnp.bfloat16) for shape in shapes) + (MARK,),
         in_specs=[anywhere] + [vmem] * len(arrays),
@@ -83,7 +88,7 @@
     return jnp.concatenate(values, axis=axis) if len(values) > 1 else values[0]
 
 
-def attend_kernel(section, pieces, n_blocks, split, carry, copies, mark, k, v, *refs):
+def attend_kernel(section, pieces, n_blocks, split, carry, copies, cut, mark, k, v, *refs):
     xs, qs, refs = refs[:n_blocks], refs[n_blocks : 2 * n_blocks], refs[2 * n_blocks :]
     weight, refs = refs[0], refs[1:]
     kept, refs = refs[:carry], refs[carry:]
@@ -121,6 +126,9 @@
             else:
                 out = outs[0]
                 lanes = put_lanes = slice(column, column + step)
+                if cut:
+                    part = column * 2 // width
+                    cut_out, cut_lanes = outs[len(outs) - 2 + part], slice(column - part * width // 2, column - part * width // 2 + step)
             g = jnp.dot(attended, weight[:, lanes], preferred_element_type=jnp.float32)
             at = 0
             for turn, (block, start, size) in enumerate(pieces):
@@ -131,7 +139,11 @@
                     rows = pl.ds(pl.multiple_of(place, size), size)
                 else:
                     rows = slice(0, size)
-                out[rows, put_lanes] = value.astype(out.dtype)
+                value = value.astype(out.dtype)
+                if len(outs) != 2 or not cut:
+                    out[rows, put_lanes] = value
+                if cut:
+                    cut_out[rows, cut_lanes] = value
                 at += size
         for turn in range(1, copies):
             block = lax.rem(lax.axis_index("head") + turn, n_head)
@@ -148,10 +160,10 @@
         outs[0][o_ref.shape[0] :, :] = kept[0][...]
 
 
-def attend(section, pieces, blocks, mark, weight, split, kept=(), share=False):
+def attend(section, pieces, blocks, filled, mark, weight, split, kept=(), share=False, cut=False, whole=True):
     rows = sum(size for _, _, size in pieces)
     channels, width = weight.shape
-    keys, values = blocks[-1][2:]
+    keys, values = filled
     n_head = width // channels
     if split:
         out_shape = tuple(
@@ -159,11 +171,12 @@
             for turn in range(n_head)
         )
     else:
-        out_shape = (jax.ShapeDtypeStruct((rows, width), jnp.bfloat16),)
+        out_shape = (jax.ShapeDtypeStruct((rows, width), jnp.bfloat16),) * (1 if whole else 0)
+        out_shape += (jax.ShapeDtypeStruct((rows, width // 2), jnp.bfloat16),) * (2 if cut else 0)
         out_shape += (jax.ShapeDtypeStruct((rows, channels), jnp.bfloat16),) * (n_head - 1 if share else 0)
     arrays = [keys, values] + [block[i] for i in range(2) for block in blocks] + [weight, *kept]
     return pl.pallas_call(
-        functools.partial(attend_kernel, section, pieces, len(blocks), split, len(kept), n_head if share else 0),
+        functools.partial(attend_kernel, section, pieces, len(blocks), split, len(kept), n_head if share else 0, cut),
         out_shape=out_shape + (MARK,),
         in_specs=[anywhere] + [vmem] * len(arrays),
         out_specs=(vmem,) * len(out_shape) + (anywhere,),
@@ -178,24 +191,26 @@
     )(mark, *arrays)
 
 
-def add_kernel(section, n_before, mark, *refs):
+def add_kernel(section, n_before, number, mark, *refs):
     @pl.when(lax.axis_index("pipe") == section)
     def _():
         before, terms, out = refs[:n_before], refs[n_before:-2], refs[-2]
         rows = out.shape[0] - sum(block.shape[0] for block in before)
-        total = terms[0][:rows, :].astype(jnp.float32)
-        for term in terms[1:]:
-            total = total + term[:rows, :].astype(jnp.float32)
+        width = out.shape[1]
+        lanes = [slice(0, width) if term.shape[1] == width else slice(number * width, (number + 1) * width) for term in terms]
+        total = terms[0][:rows, lanes[0]].astype(jnp.float32)
+        for term, columns in zip(terms[1:], lanes[1:]):
+            total = total + term[:rows, columns].astype(jnp.float32)
         for block in before:
             out[: block.shape[0], :] = block[...]
         out[out.shape[0] - rows :, :] = total.astype(out.dtype)
 
 
-def add(section, terms, mark, flops=0, before=()):
+def add(section, terms, mark, flops=0, before=(), number=0):
     rows, width = min(term.shape for term in terms)
     rows += sum(block.shape[0] for block in before)
     return pl.pallas_call(
-        functools.partial(add_kernel, section, len(before)),
+        functools.partial(add_kernel, section, len(before), number),
         out_shape=(jax.ShapeDtypeStruct((rows, width), terms[0].dtype), MARK),
         in_specs=[anywhere] + [vmem] * (len(before) + len(terms)),
         out_specs=(vmem, anywhere),
@@ -305,7 +320,7 @@
     blocks, filled = [], ()
     for turn, cells in enumerate(arrived):
         *block, mark = project(
-            0, natural, [cells], mark, score_scale, value_cols, turn * own.shape[0], n_head * own.shape[0], filled
+            0, natural, [[cells]], mark, score_scale, value_cols, turn * own.shape[0], n_head * own.shape[0], filled
         )
         blocks.append(block)
         filled = block[2:]
@@ -323,7 +338,11 @@
             carried = [kept] if share or last and half else []
             if last and half:
                 (mark,) = after([mark], given, *early)
-            *part, mark = attend(section, halves[half], blocks, mark, out_rows, last, carried, share)
+            cut = shift == 1 and half == 1 and not last
+            whole = not cut
+            *part, mark = attend(
+                section, halves[half], blocks, filled, mark, out_rows, last, carried, share, cut, whole
+            )
             if share:
                 own_share, *shared = part
             cross = 0 if half else shift if last else 1 if shift else -1
@@ -333,17 +352,22 @@
             elif last:
                 terms = [send(part[turn], section, section - 1, cross, turn) for turn in range(n_head)]
             elif shift and not half:
-                terms = [send(part[0], section, idle, cross)]
+                terms = [send(block, section, idle, cross) for block in part]
             elif shift:
-                terms = [send(part[0], section, section - 1, 0, turn) for turn in range(n_head)]
+                terms = [[send(block, section, section - 1, 0, turn) for turn in range(n_head)] for block in part]
             else:
-                terms = [send(part[0], section, section + 1, cross, turn) for turn in range(n_head)]
+                terms = [[send(part[0], section, section + 1, cross, turn)] for turn in range(n_head)]
             moved.append(terms)
         if shift and not last:
-            (one,) = after(moved[0], mark)
-            moved[0] = [send(one, idle, section + 1, 0, turn) for turn in range(n_head)]
-            total, mark = add(section - 1, moved[1], mark)
-            moved[1] = [send(total, section - 1, section + 1)]
+            arrived = [after([block], mark, flops=0)[0] for block in moved[0]]
+            moved[0] = [
+                [send(block, idle, section + 1, 0, turn) for block in arrived] for turn in range(n_head)
+            ]
+            sums = []
+            for number, terms in enumerate(moved[1]):
+                total, mark = add(section - 1, terms, mark, 0)
+                sums.append(send(total, section - 1, section + 1))
+            moved[1] = [sums]
         if section + 2 == sections:
             straight_back = [(source, source - 1, 0, 0) for source in range(1, section + 1)]
             across = [(source, source - 1, 1, 0) for source in range(1, section, 2)]
@@ -355,8 +379,8 @@
             given = send_all(early_kept, straight_back)
             kept = None
         if not last:
-            blocks, filled, rows = [], (), piece * n_head
-            for half in range(2):
+            blocks, filled, rows = [None, None], (), piece * n_head
+            for half in (1, 0) if shift else (0, 1):
                 keep_rows = 2 * rows if section + 2 < sections else half * rows
                 *block, mark = project(
                     section + 1,
@@ -373,7 +397,7 @@
                 )
                 if keep_rows:
                     *block, kept = block
-                blocks.append(block)
+                blocks[half] = block
                 filled = block[2:]
             halves = [[(0, 0, piece * n_head)], [(1, 0, piece * n_head)]]
     *across, mark = after([*moved[0][1:], mark], flops=4 * 10**9)

time: 89.8 us -> 88.7 us (0.988)
  waiting for transfers between devices: 53.3 us -> 50.1 us
  starting transfers between devices: 22.6 us -> 24.6 us
    ppermute x22 -> x25, waiting for transfers between devices: 53.3 us -> 50.1 us  [send_all(): return lax.ppermute(value, AXES, pairs)]
    ppermute x22 -> x25, starting transfers between devices: 22.6 us -> 24.6 us  [send_all(): return lax.ppermute(value, AXES, pairs)]
    pallas_call x12 -> x13, Pallas kernels: 2.02 us -> 2.02 us  [the longest x8 1.99 us: project(): pl.pallas_call(functools.partial(project_kernel, section, chunk_order, co...]
  transfers between devices with their start and end apart: 22 -> 25, of which waited for: 7 -> 7; matrix products, arithmetic and copies ran while one was open for 0% -> 0% of each run, Pallas kernels for 5% -> 5%
where the time goes in v6:
time: 88.7 us; the launch traced here: 88.1 us
  waiting for transfers between devices  50.1 us (56%)
  starting transfers between devices  24.6 us (28%)
  local copies, waits for them, and re-layouts  7.38 us (8%)
  Pallas kernels  5.53 us (6%)
    ppermute x25, waiting for transfers between devices, send_all(): return lax.ppermute(value, AXES, pairs)  50.1 us
    ppermute x25, starting transfers between devices, send_all(): return lax.ppermute(value, AXES, pairs)  24.6 us
    unnamed x12, local copies, waits for them, and re-layouts  7.38 us
    pallas_call x8, Pallas kernels, attend(): pl.pallas_call(functools.partial(attend_kernel, section, pieces, len(bloc...  2.66 us
    pallas_call x8, Pallas kernels, project(): pl.pallas_call(functools.partial(project_kernel, section, chunk_order, co...  1.99 us
  transfers between devices with their start and end apart: 25, of which 7 were waited for; matrix products, arithmetic and copies ran while one was open for 0% of the time, Pallas kernels for 5%

profile of v6, /device:TPU:5, one launch (start us, length us, event | category | flops | bytes accessed | tf_op | source)
XLA Modules:
  0.0 88.1 jit_solution(12661228893952979850)
XLA Ops:
  0.7 2.2 %copy-done = bf16[1,2048,1024]{2,1,0:T(8,128)(2,1)S(1)} copy-done((bf16[1,2048,1024]{2,1,0:T(8,128)(2,1)S(1)}, bf16[1,2048,1024]{2,1,0:T(8,128)(2,1)}, u32[]{:S(2)}) %copy-start) | copy-done | bytes 4194328
  3.6 1.0 %copy-done.5 = bf16[4,32,2048]{2,1,0:T(8,128)(2,1)S(1)} copy-done((bf16[4,32,2048]{2,1,0:T(8,128)(2,1)S(1)}, bf16[4,32,2048]{2,1,0:T(8,128)(2,1)}, u32[]{:S(2)}) %copy-start.5) | copy-done | bytes 524312
  4.6 2.2 %copy-done.1 = bf16[1,2048,1024]{2,1,0:T(8,128)(2,1)S(1)} copy-done((bf16[1,2048,1024]{2,1,0:T(8,128)(2,1)S(1)}, bf16[1,2048,1024]{2,1,0:T(8,128)(2,1)}, u32[]{:S(2)}) %copy-start.1) | copy-done | bytes 4194328
  6.8 1.3 %copy-done.2 = bf16[1,1024,2048]{2,1,0:T(8,128)(2,1)S(1)} copy-done((bf16[1,1024,2048]{2,1,0:T(8,128)(2,1)S(1)}, bf16[1,1024,2048]{2,1,0:T(8,128)(2,1)}, u32[]{:S(2)}) %copy-start.2) | copy-done | bytes 4194328
  11.2 1.3 %collective-permute-start.11 = (bf16[128,2048]{1,0:T(8,128)(2,1)S(1)}, bf16[128,2048]{1,0:T(8,128)(2,1)S(1)}, u32[]{:S(2)}, u32[]{:S(2)}) collective-permute-start(bf16[128,2048]{1,0:T(8,128)(2,1)S(1)} %get-tuple-element.118), channel_id=1, source_target_pairs={{8,26},{9,27},{10,28},{11,29},{12,30},{13,31},{14,24},{15,25}} | collective-permute-start | bytes 1572872 | tf_op jit(solution)/shard_map/ppermute | solution.py:311
  15.3 26.6 %collective-permute-done.11.refs_0_ = bf16[128,2048]{1,0:T(8,128)(2,1)S(1)} collective-permute-done((bf16[128,2048]{1,0:T(8,128)(2,1)S(1)}, bf16[128,2048]{1,0:T(8,128)(2,1)S(1)}, u32[]{:S(2)}, u32[]{:S(2)}) %collective-permute-start.11) | collective-permute-done | bytes 524320 | tf_op jit(solution)/shard_map/ppermute | solution.py:311
  41.8 1.3 %collective-permute-start.13 = (bf16[128,2048]{1,0:T(8,128)(2,1)S(1)}, bf16[128,2048]{1,0:T(8,128)(2,1)S(1)}, u32[]{:S(2)}, u32[]{:S(2)}) collective-permute-start(bf16[128,2048]{1,0:T(8,128)(2,1)S(1)} %after.4), channel_id=1, source_target_pairs={{24,17},{25,16},{26,19},{27,18},{28,21},{29,20},{30,23},{31,22}} | collective-permute-start | bytes 1572872 | tf_op jit(solution)/shard_map/ppermute | solution.py:311
  43.2 1.3 %collective-permute-start.12 = (bf16[128,2048]{1,0:T(8,128)(2,1)S(1)}, bf16[128,2048]{1,0:T(8,128)(2,1)S(1)}, u32[]{:S(2)}, u32[]{:S(2)}) collective-permute-start(bf16[128,2048]{1,0:T(8,128)(2,1)S(1)} %after.4), channel_id=1, source_target_pairs={{24,16},{25,17},{26,18},{27,19},{28,20},{29,21},{30,22},{31,23}} | collective-permute-start | bytes 1572872 | tf_op jit(solution)/shard_map/ppermute | solution.py:311
  46.0 3.2 %collective-permute-done.13.refs_1_ = bf16[128,2048]{1,0:T(8,128)(2,1)S(1)} collective-permute-done((bf16[128,2048]{1,0:T(8,128)(2,1)S(1)}, bf16[128,2048]{1,0:T(8,128)(2,1)S(1)}, u32[]{:S(2)}, u32[]{:S(2)}) %collective-permute-start.13) | collective-permute-done | bytes 524320 | tf_op jit(solution)/shard_map/ppermute | solution.py:311
  49.2 1.3 %collective-permute-start.15 = (bf16[128,2048]{1,0:T(8,128)(2,1)S(1)}, bf16[128,2048]{1,0:T(8,128)(2,1)S(1)}, u32[]{:S(2)}, u32[]{:S(2)}) collective-permute-start(bf16[128,2048]{1,0:T(8,128)(2,1)S(1)} %get-tuple-element.132.share), channel_id=1, source_target_pairs={{16,31},{17,30},{18,25},{19,24},{20,27},{21,26},{22,29},{23,28}} | collective-permute-start | bytes 1572872 | tf_op jit(solution)/shard_map/ppermute | solution.py:311
  50.5 1.3 %collective-permute-start.14 = (bf16[128,2048]{1,0:T(8,128)(2,1)S(1)}, bf16[128,2048]{1,0:T(8,128)(2,1)S(1)}, u32[]{:S(2)}, u32[]{:S(2)}) collective-permute-start(bf16[128,2048]{1,0:T(8,128)(2,1)S(1)} %get-tuple-element.132.share), channel_id=1, source_target_pairs={{16,30},{17,31},{18,24},{19,25},{20,26},{21,27},{22,28},{23,29}} | collective-permute-start | bytes 1572872 | tf_op jit(solution)/shard_map/ppermute | solution.py:311
  52.1 1.3 %collective-permute-start.17 = (bf16[128,2048]{1,0:T(8,128)(2,1)S(1)}, bf16[128,2048]{1,0:T(8,128)(2,1)S(1)}, u32[]{:S(2)}, u32[]{:S(2)}) collective-permute-start(bf16[128,2048]{1,0:T(8,128)(2,1)S(1)} %get-tuple-element.134), channel_id=1, source_target_pairs={{16,25},{17,24},{18,27},{19,26},{20,29},{21,28},{22,31},{23,30}} | collective-permute-start | bytes 1572872 | tf_op jit(solution)/shard_map/ppermute | solution.py:311
  53.4 1.3 %collective-permute-start.16 = (bf16[128,2048]{1,0:T(8,128)(2,1)S(1)}, bf16[128,2048]{1,0:T(8,128)(2,1)S(1)}, u32[]{:S(2)}, u32[]{:S(2)}) collective-permute-start(bf16[128,2048]{1,0:T(8,128)(2,1)S(1)} %get-tuple-element.134), channel_id=1, source_target_pairs={{16,24},{17,25},{18,26},{19,27},{20,28},{21,29},{22,30},{23,31}} | collective-permute-start | bytes 1572872 | tf_op jit(solution)/shard_map/ppermute | solution.py:311
  55.4 8.7 %collective-permute-done.15.refs_1_ = bf16[128,2048]{1,0:T(8,128)(2,1)S(1)} collective-permute-done((bf16[128,2048]{1,0:T(8,128)(2,1)S(1)}, bf16[128,2048]{1,0:T(8,128)(2,1)S(1)}, u32[]{:S(2)}, u32[]{:S(2)}) %collective-permute-start.15) | collective-permute-done | bytes 524320 | tf_op jit(solution)/shard_map/ppermute | solution.py:311
  64.7 5.2 %collective-permute-done.14.refs_0_ = bf16[128,2048]{1,0:T(8,128)(2,1)S(1)} collective-permute-done((bf16[128,2048]{1,0:T(8,128)(2,1)S(1)}, bf16[128,2048]{1,0:T(8,128)(2,1)S(1)}, u32[]{:S(2)}, u32[]{:S(2)}) %collective-permute-start.14) | collective-permute-done | bytes 524320 | tf_op jit(solution)/shard_map/ppermute | solution.py:311
  71.9 1.2 %attend.14 = (bf16[128,1024]{1,0:T(8,128)(2,1)S(1)}, bf16[128,1024]{1,0:T(8,128)(2,1)S(1)}, f32[8,128]{1,0:T(8,128)S(1)}) custom-call(f32[8,128]{1,0:T(8,128)S(1)} %get-tuple-element.137.mark, bf16[256,1024]{1,0:T(8,128)(2,1)S(1)} %get-tuple-element.138.k, bf16[256,1024]{1,0:T(8,128)(2,1)S(1)} %get-tuple-element.139.v, ...), custom_call_target="tpu_custom_call" | custom-call | flops 671088640 | bytes 4194304 | tf_op jit(solution)/shard_map/attend/pallas_call | solution.py:178
  73.1 1.3 %collective-permute-start.18 = (bf16[128,1024]{1,0:T(8,128)(2,1)S(1)}, bf16[128,1024]{1,0:T(8,128)(2,1)S(1)}, u32[]{:S(2)}, u32[]{:S(2)}) collective-permute-start(bf16[128,1024]{1,0:T(8,128)(2,1)S(1)} %get-tuple-element.144), channel_id=1, source_target_pairs={{24,19},{25,18},{26,21},{27,20},{28,23},{29,22},{30,17},{31,16}} | collective-permute-start | bytes 786440 | tf_op jit(solution)/shard_map/ppermute | solution.py:311
  74.4 1.2 %attend.15 = (bf16[256,1024]{1,0:T(8,128)(2,1)S(1)}, bf16[128,1024]{1,0:T(8,128)(2,1)S(1)}, f32[8,128]{1,0:T(8,128)S(1)}) custom-call(f32[8,128]{1,0:T(8,128)S(1)} %after.6.mark, bf16[256,1024]{1,0:T(8,128)(2,1)S(1)} %get-tuple-element.138.k, bf16[256,1024]{1,0:T(8,128)(2,1)S(1)} %get-tuple-element.139.v, bf16[128,2048]{1,0:T(8,128)(2,1)S(1)} %get-tuple-element.140.refs_0_, ...), custom_call_target="tpu_custom_call" | custom-call | flops 671088640 | bytes 4194304 | tf_op jit(solution)/shard_map/attend/pallas_call | solution.py:178
  75.6 1.3 %collective-permute-start.22 = (bf16[128,1024]{1,0:T(8,128)(2,1)S(1)}, bf16[128,1024]{1,0:T(8,128)(2,1)S(1)}, u32[]{:S(2)}, u32[]{:S(2)}) collective-permute-start(bf16[128,1024]{1,0:T(8,128)(2,1)S(1)} %get-tuple-element.155), channel_id=1, source_target_pairs={{24,17},{25,16},{26,19},{27,18},{28,21},{29,20},{30,23},{31,22}} | collective-permute-start | bytes 786440 | tf_op jit(solution)/shard_map/ppermute | solution.py:311
  76.9 1.3 %collective-permute-start.21 = (bf16[128,1024]{1,0:T(8,128)(2,1)S(1)}, bf16[128,1024]{1,0:T(8,128)(2,1)S(1)}, u32[]{:S(2)}, u32[]{:S(2)}) collective-permute-start(bf16[128,1024]{1,0:T(8,128)(2,1)S(1)} %get-tuple-element.152), channel_id=1, source_target_pairs={{24,18},{25,19},{26,20},{27,21},{28,22},{29,23},{30,16},{31,17}} | collective-permute-start | bytes 786440 | tf_op jit(solution)/shard_map/ppermute | solution.py:311
  78.2 1.3 %collective-permute-start.23 = (bf16[256,1024]{1,0:T(8,128)(2,1)S(1)}, bf16[256,1024]{1,0:T(8,128)(2,1)S(1)}, u32[]{:S(2)}, u32[]{:S(2)}) collective-permute-start(bf16[256,1024]{1,0:T(8,128)(2,1)S(1)} %get-tuple-element.159), channel_id=1, source_target_pairs={{24,16},{25,17},{26,18},{27,19},{28,20},{29,21},{30,22},{31,23}} | collective-permute-start | bytes 1572872 | tf_op jit(solution)/shard_map/ppermute | solution.py:311
  79.6 1.9 %collective-permute-done.21.refs_0_ = bf16[128,1024]{1,0:T(8,128)(2,1)S(1)} collective-permute-done((bf16[128,1024]{1,0:T(8,128)(2,1)S(1)}, bf16[128,1024]{1,0:T(8,128)(2,1)S(1)}, u32[]{:S(2)}, u32[]{:S(2)}) %collective-permute-start.21) | collective-permute-done | bytes 262176 | tf_op jit(solution)/shard_map/ppermute | solution.py:311
  81.9 1.3 %collective-permute-start.24 = (bf16[256,1024]{1,0:T(8,128)(2,1)S(1)}, bf16[256,1024]{1,0:T(8,128)(2,1)S(1)}, u32[]{:S(2)}, u32[]{:S(2)}) collective-permute-start(bf16[256,1024]{1,0:T(8,128)(2,1)S(1)} %get-tuple-element.160), channel_id=1, source_target_pairs={{16,24},{17,25},{18,26},{19,27},{20,28},{21,29},{22,30},{23,31}} | collective-permute-start | bytes 1572872 | tf_op jit(solution)/shard_map/ppermute | solution.py:311
  83.2 4.1 %collective-permute-done.24.total = bf16[256,1024]{1,0:T(8,128)(2,1)S(1)} collective-permute-done((bf16[256,1024]{1,0:T(8,128)(2,1)S(1)}, bf16[256,1024]{1,0:T(8,128)(2,1)S(1)}, u32[]{:S(2)}, u32[]{:S(2)}) %collective-permute-start.24) | collective-permute-done | bytes 524320 | tf_op jit(solution)/shard_map/ppermute | solution.py:311
  (65 shorter events, 13.2 us)
Async XLA Ops:
  0.0 4.6 %collective-permute-start = (bf16[128,2048]{1,0:T(8,128)(2,1)}, bf16[128,2048]{1,0:T(8,128)(2,1)S(1)}, u32[]{:S(2)}, u32[]{:S(2)}) collective-permute-start(bf16[128,2048]{1,0:T(8,128)(2,1)} %bitcast.20), channel_id=1, source_target_pairs={{0,1},{1,0},{2,3},{3,2},{4,5},{5,4},{6,7},{7,6}} | collective-permute-start | bytes 1572872 | tf_op jit(solution)/shard_map/ppermute | solution.py:311
  8.1 3.0 %collective-permute-start.2 = (bf16[128,2048]{1,0:T(8,128)(2,1)S(1)}, bf16[128,2048]{1,0:T(8,128)(2,1)S(1)}, u32[]{:S(2)}, u32[]{:S(2)}) collective-permute-start(bf16[128,2048]{1,0:T(8,128)(2,1)S(1)} %get-tuple-element.95), channel_id=1, source_target_pairs={{0,15},{1,14},{2,9},{3,8},{4,11},{5,10},{6,13},{7,12}} | collective-permute-start | bytes 1572872 | tf_op jit(solution)/shard_map/ppermute | solution.py:311
  8.9 2.1 %collective-permute-start.1 = (bf16[128,2048]{1,0:T(8,128)(2,1)S(1)}, bf16[128,2048]{1,0:T(8,128)(2,1)S(1)}, u32[]{:S(2)}, u32[]{:S(2)}) collective-permute-start(bf16[128,2048]{1,0:T(8,128)(2,1)S(1)} %get-tuple-element.95), channel_id=1, source_target_pairs={{0,14},{1,15},{2,8},{3,9},{4,10},{5,11},{6,12},{7,13}} | collective-permute-start | bytes 1572872 | tf_op jit(solution)/shard_map/ppermute | solution.py:311
  9.7 1.5 %collective-permute-start.4 = (bf16[128,2048]{1,0:T(8,128)(2,1)S(1)}, bf16[128,2048]{1,0:T(8,128)(2,1)S(1)}, u32[]{:S(2)}, u32[]{:S(2)}) collective-permute-start(bf16[128,2048]{1,0:T(8,128)(2,1)S(1)} %get-tuple-element.97), channel_id=1, source_target_pairs={{0,9},{1,8},{2,11},{3,10},{4,13},{5,12},{6,15},{7,14}} | collective-permute-start | bytes 1572872 | tf_op jit(solution)/shard_map/ppermute | solution.py:311
  10.4 0.8 collective-permute-start.3
  11.2 30.6 %collective-permute-start.11 = (bf16[128,2048]{1,0:T(8,128)(2,1)S(1)}, bf16[128,2048]{1,0:T(8,128)(2,1)S(1)}, u32[]{:S(2)}, u32[]{:S(2)}) collective-permute-start(bf16[128,2048]{1,0:T(8,128)(2,1)S(1)} %get-tuple-element.118), channel_id=1, source_target_pairs={{8,26},{9,27},{10,28},{11,29},{12,30},{13,31},{14,24},{15,25}} | collective-permute-start | bytes 1572872 | tf_op jit(solution)/shard_map/ppermute | solution.py:311
  12.5 30.6 %collective-permute-start.6 = (bf16[128,1024]{1,0:T(8,128)(2,1)S(1)}, bf16[128,1024]{1,0:T(8,128)(2,1)S(1)}, u32[]{:S(2)}, u32[]{:S(2)}) collective-permute-start(bf16[128,1024]{1,0:T(8,128)(2,1)S(1)} %get-tuple-element.110), channel_id=1, source_target_pairs={{8,1},{9,0},{10,3},{11,2},{12,5},{13,4},{14,7},{15,6}} | collective-permute-start | bytes 786440 | tf_op jit(solution)/shard_map/ppermute | solution.py:311
  13.2 31.3 %collective-permute-start.5 = (bf16[128,1024]{1,0:T(8,128)(2,1)S(1)}, bf16[128,1024]{1,0:T(8,128)(2,1)S(1)}, u32[]{:S(2)}, u32[]{:S(2)}) collective-permute-start(bf16[128,1024]{1,0:T(8,128)(2,1)S(1)} %get-tuple-element.110), channel_id=1, source_target_pairs={{8,0},{9,1},{10,2},{11,3},{12,4},{13,5},{14,6},{15,7}} | collective-permute-start | bytes 786440 | tf_op jit(solution)/shard_map/ppermute | solution.py:311
  13.9 31.3 %collective-permute-start.8 = (bf16[128,1024]{1,0:T(8,128)(2,1)S(1)}, bf16[128,1024]{1,0:T(8,128)(2,1)S(1)}, u32[]{:S(2)}, u32[]{:S(2)}) collective-permute-start(bf16[128,1024]{1,0:T(8,128)(2,1)S(1)} %get-tuple-element.112), channel_id=1, source_target_pairs={{8,1},{9,0},{10,3},{11,2},{12,5},{13,4},{14,7},{15,6}} | collective-permute-start | bytes 786440 | tf_op jit(solution)/shard_map/ppermute | solution.py:311
  14.6 30.6 %collective-permute-start.7 = (bf16[128,1024]{1,0:T(8,128)(2,1)S(1)}, bf16[128,1024]{1,0:T(8,128)(2,1)S(1)}, u32[]{:S(2)}, u32[]{:S(2)}) collective-permute-start(bf16[128,1024]{1,0:T(8,128)(2,1)S(1)} %get-tuple-element.112), channel_id=1, source_target_pairs={{8,0},{9,1},{10,2},{11,3},{12,4},{13,5},{14,6},{15,7}} | collective-permute-start | bytes 786440 | tf_op jit(solution)/shard_map/ppermute | solution.py:311
  41.8 7.4 %collective-permute-start.13 = (bf16[128,2048]{1,0:T(8,128)(2,1)S(1)}, bf16[128,2048]{1,0:T(8,128)(2,1)S(1)}, u32[]{:S(2)}, u32[]{:S(2)}) collective-permute-start(bf16[128,2048]{1,0:T(8,128)(2,1)S(1)} %after.4), channel_id=1, source_target_pairs={{24,17},{25,16},{26,19},{27,18},{28,21},{29,20},{30,23},{31,22}} | collective-permute-start | bytes 1572872 | tf_op jit(solution)/shard_map/ppermute | solution.py:311
  43.2 6.1 %collective-permute-start.12 = (bf16[128,2048]{1,0:T(8,128)(2,1)S(1)}, bf16[128,2048]{1,0:T(8,128)(2,1)S(1)}, u32[]{:S(2)}, u32[]{:S(2)}) collective-permute-start(bf16[128,2048]{1,0:T(8,128)(2,1)S(1)} %after.4), channel_id=1, source_target_pairs={{24,16},{25,17},{26,18},{27,19},{28,20},{29,21},{30,22},{31,23}} | collective-permute-start | bytes 1572872 | tf_op jit(solution)/shard_map/ppermute | solution.py:311
  44.5 1.4 %collective-permute-start.9 = (bf16[128,1024]{1,0:T(8,128)(2,1)S(1)}, bf16[128,1024]{1,0:T(8,128)(2,1)S(1)}, u32[]{:S(2)}, u32[]{:S(2)}) collective-permute-start(bf16[128,1024]{1,0:T(8,128)(2,1)S(1)} %get-tuple-element.114), channel_id=1, source_target_pairs={{0,16},{1,17},{2,18},{3,19},{4,20},{5,21},{6,22},{7,23}} | collective-permute-start | bytes 786440 | tf_op jit(solution)/shard_map/ppermute | solution.py:311
  49.2 14.8 %collective-permute-start.15 = (bf16[128,2048]{1,0:T(8,128)(2,1)S(1)}, bf16[128,2048]{1,0:T(8,128)(2,1)S(1)}, u32[]{:S(2)}, u32[]{:S(2)}) collective-permute-start(bf16[128,2048]{1,0:T(8,128)(2,1)S(1)} %get-tuple-element.132.share), channel_id=1, source_target_pairs={{16,31},{17,30},{18,25},{19,24},{20,27},{21,26},{22,29},{23,28}} | collective-permute-start | bytes 1572872 | tf_op jit(solution)/shard_map/ppermute | solution.py:311
  50.5 19.4 %collective-permute-start.14 = (bf16[128,2048]{1,0:T(8,128)(2,1)S(1)}, bf16[128,2048]{1,0:T(8,128)(2,1)S(1)}, u32[]{:S(2)}, u32[]{:S(2)}) collective-permute-start(bf16[128,2048]{1,0:T(8,128)(2,1)S(1)} %get-tuple-element.132.share), channel_id=1, source_target_pairs={{16,30},{17,31},{18,24},{19,25},{20,26},{21,27},{22,28},{23,29}} | collective-permute-start | bytes 1572872 | tf_op jit(solution)/shard_map/ppermute | solution.py:311
  52.1 18.8 %collective-permute-start.17 = (bf16[128,2048]{1,0:T(8,128)(2,1)S(1)}, bf16[128,2048]{1,0:T(8,128)(2,1)S(1)}, u32[]{:S(2)}, u32[]{:S(2)}) collective-permute-start(bf16[128,2048]{1,0:T(8,128)(2,1)S(1)} %get-tuple-element.134), channel_id=1, source_target_pairs={{16,25},{17,24},{18,27},{19,26},{20,29},{21,28},{22,31},{23,30}} | collective-permute-start | bytes 1572872 | tf_op jit(solution)/shard_map/ppermute | solution.py:311
  53.4 17.5 %collective-permute-start.16 = (bf16[128,2048]{1,0:T(8,128)(2,1)S(1)}, bf16[128,2048]{1,0:T(8,128)(2,1)S(1)}, u32[]{:S(2)}, u32[]{:S(2)}) collective-permute-start(bf16[128,2048]{1,0:T(8,128)(2,1)S(1)} %get-tuple-element.134), channel_id=1, source_target_pairs={{16,24},{17,25},{18,26},{19,27},{20,28},{21,29},{22,30},{23,31}} | collective-permute-start | bytes 1572872 | tf_op jit(solution)/shard_map/ppermute | solution.py:311
  54.7 19.7 %collective-permute-start.19 = (bf16[256,1024]{1,0:T(8,128)(2,1)S(1)}, bf16[256,1024]{1,0:T(8,128)(2,1)S(1)}, u32[]{:S(2)}, u32[]{:S(2)}) collective-permute-start(bf16[256,1024]{1,0:T(8,128)(2,1)S(1)} %get-tuple-element.147), channel_id=1, source_target_pairs={{8,0},{9,1},{10,2},{11,3},{12,4},{13,5},{14,6},{15,7},{16,8},{17,9... | collective-permute-start | bytes 1572872 | tf_op jit(solution)/shard_map/ppermute | solution.py:311
  64.0 10.4 %collective-permute-start.20 = (bf16[128,1024]{1,0:T(8,128)(2,1)S(1)}, bf16[128,1024]{1,0:T(8,128)(2,1)S(1)}, u32[]{:S(2)}, u32[]{:S(2)}) collective-permute-start(bf16[128,1024]{1,0:T(8,128)(2,1)S(1)} %get-tuple-element.148), channel_id=1, source_target_pairs={{8,2},{9,3},{10,4},{11,5},{12,6},{13,7},{14,0},{15,1},{16,17},{17,... | collective-permute-start | bytes 786440 | tf_op jit(solution)/shard_map/ppermute | solution.py:311
  73.1 6.5 %collective-permute-start.18 = (bf16[128,1024]{1,0:T(8,128)(2,1)S(1)}, bf16[128,1024]{1,0:T(8,128)(2,1)S(1)}, u32[]{:S(2)}, u32[]{:S(2)}) collective-permute-start(bf16[128,1024]{1,0:T(8,128)(2,1)S(1)} %get-tuple-element.144), channel_id=1, source_target_pairs={{24,19},{25,18},{26,21},{27,20},{28,23},{29,22},{30,17},{31,16}} | collective-permute-start | bytes 786440 | tf_op jit(solution)/shard_map/ppermute | solution.py:311
  75.6 6.3 %collective-permute-start.22 = (bf16[128,1024]{1,0:T(8,128)(2,1)S(1)}, bf16[128,1024]{1,0:T(8,128)(2,1)S(1)}, u32[]{:S(2)}, u32[]{:S(2)}) collective-permute-start(bf16[128,1024]{1,0:T(8,128)(2,1)S(1)} %get-tuple-element.155), channel_id=1, source_target_pairs={{24,17},{25,16},{26,19},{27,18},{28,21},{29,20},{30,23},{31,22}} | collective-permute-start | bytes 786440 | tf_op jit(solution)/shard_map/ppermute | solution.py:311
  76.9 4.6 %collective-permute-start.21 = (bf16[128,1024]{1,0:T(8,128)(2,1)S(1)}, bf16[128,1024]{1,0:T(8,128)(2,1)S(1)}, u32[]{:S(2)}, u32[]{:S(2)}) collective-permute-start(bf16[128,1024]{1,0:T(8,128)(2,1)S(1)} %get-tuple-element.152), channel_id=1, source_target_pairs={{24,18},{25,19},{26,20},{27,21},{28,22},{29,23},{30,16},{31,17}} | collective-permute-start | bytes 786440 | tf_op jit(solution)/shard_map/ppermute | solution.py:311
  78.2 3.6 %collective-permute-start.23 = (bf16[256,1024]{1,0:T(8,128)(2,1)S(1)}, bf16[256,1024]{1,0:T(8,128)(2,1)S(1)}, u32[]{:S(2)}, u32[]{:S(2)}) collective-permute-start(bf16[256,1024]{1,0:T(8,128)(2,1)S(1)} %get-tuple-element.159), channel_id=1, source_target_pairs={{24,16},{25,17},{26,18},{27,19},{28,20},{29,21},{30,22},{31,23}} | collective-permute-start | bytes 1572872 | tf_op jit(solution)/shard_map/ppermute | solution.py:311
  81.9 5.4 %collective-permute-start.24 = (bf16[256,1024]{1,0:T(8,128)(2,1)S(1)}, bf16[256,1024]{1,0:T(8,128)(2,1)S(1)}, u32[]{:S(2)}, u32[]{:S(2)}) collective-permute-start(bf16[256,1024]{1,0:T(8,128)(2,1)S(1)} %get-tuple-element.160), channel_id=1, source_target_pairs={{16,24},{17,25},{18,26},{19,27},{20,28},{21,29},{22,30},{23,31}} | collective-permute-start | bytes 1572872 | tf_op jit(solution)/shard_map/ppermute | solution.py:311
  (7 other events, 13.3 us)

commit v7 on v6

--- a/solution.py
+++ b/solution.py
@@ -400,8 +400,8 @@
                 blocks[half] = block
                 filled = block[2:]
             halves = [[(0, 0, piece * n_head)], [(1, 0, piece * n_head)]]
-    *across, mark = after([*moved[0][1:], mark], flops=4 * 10**9)
-    first, mark = add(sections - 2, [moved[0][0], *across], mark, 10**8)
+    *across, mark = after([*moved[0][1:], mark])
+    first, mark = add(sections - 2, [moved[0][0], *across], mark, 4 * 10**9)
     second, mark = add(sections - 2, moved[1][:-1], mark, 4 * 10**9)
     total, mark = add(sections - 2, [second, moved[1][-1]], mark, 0, (first,))
     total = send(total, sections - 2, sections - 1)

time: 88.7 us -> 87.7 us (0.989)
  waiting for transfers between devices: 50.1 us -> 49 us
    ppermute x25, waiting for transfers between devices: 50.1 us -> 49 us  [send_all(): return lax.ppermute(value, AXES, pairs)]
where the time goes in v7:
time: 87.7 us; the launch traced here: 87 us
  waiting for transfers between devices  49 us (56%)
  starting transfers between devices  24.6 us (28%)
  local copies, waits for them, and re-layouts  7.38 us (8%)
  Pallas kernels  5.53 us (6%)
    ppermute x25, waiting for transfers between devices, send_all(): return lax.ppermute(value, AXES, pairs)  49 us
    ppermute x25, starting transfers between devices, send_all(): return lax.ppermute(value, AXES, pairs)  24.6 us
    unnamed x12, local copies, waits for them, and re-layouts  7.38 us
    pallas_call x8, Pallas kernels, attend(): pl.pallas_call(functools.partial(attend_kernel, section, pieces, len(bloc...  2.66 us
    pallas_call x8, Pallas kernels, project(): pl.pallas_call(functools.partial(project_kernel, section, chunk_order, co...  1.99 us
  transfers between devices with their start and end apart: 25, of which 7 were waited for; matrix products, arithmetic and copies ran while one was open for 0% of the time, Pallas kernels for 5%

profile of v7, /device:TPU:5, one launch (start us, length us, event | category | flops | bytes accessed | tf_op | source)
XLA Modules:
  0.0 87.0 jit_solution(4595885699234460595)
XLA Ops:
  0.7 2.2 %copy-done = bf16[1,2048,1024]{2,1,0:T(8,128)(2,1)S(1)} copy-done((bf16[1,2048,1024]{2,1,0:T(8,128)(2,1)S(1)}, bf16[1,2048,1024]{2,1,0:T(8,128)(2,1)}, u32[]{:S(2)}) %copy-start) | copy-done | bytes 4194328
  3.6 1.0 %copy-done.5 = bf16[4,32,2048]{2,1,0:T(8,128)(2,1)S(1)} copy-done((bf16[4,32,2048]{2,1,0:T(8,128)(2,1)S(1)}, bf16[4,32,2048]{2,1,0:T(8,128)(2,1)}, u32[]{:S(2)}) %copy-start.5) | copy-done | bytes 524312
  4.6 2.2 %copy-done.1 = bf16[1,2048,1024]{2,1,0:T(8,128)(2,1)S(1)} copy-done((bf16[1,2048,1024]{2,1,0:T(8,128)(2,1)S(1)}, bf16[1,2048,1024]{2,1,0:T(8,128)(2,1)}, u32[]{:S(2)}) %copy-start.1) | copy-done | bytes 4194328
  6.8 1.3 %copy-done.2 = bf16[1,1024,2048]{2,1,0:T(8,128)(2,1)S(1)} copy-done((bf16[1,1024,2048]{2,1,0:T(8,128)(2,1)S(1)}, bf16[1,1024,2048]{2,1,0:T(8,128)(2,1)}, u32[]{:S(2)}) %copy-start.2) | copy-done | bytes 4194328
  11.2 1.3 %collective-permute-start.11 = (bf16[128,2048]{1,0:T(8,128)(2,1)S(1)}, bf16[128,2048]{1,0:T(8,128)(2,1)S(1)}, u32[]{:S(2)}, u32[]{:S(2)}) collective-permute-start(bf16[128,2048]{1,0:T(8,128)(2,1)S(1)} %get-tuple-element.118), channel_id=1, source_target_pairs={{8,26},{9,27},{10,28},{11,29},{12,30},{13,31},{14,24},{15,25}} | collective-permute-start | bytes 1572872 | tf_op jit(solution)/shard_map/ppermute | solution.py:311
  15.3 26.6 %collective-permute-done.11.refs_0_ = bf16[128,2048]{1,0:T(8,128)(2,1)S(1)} collective-permute-done((bf16[128,2048]{1,0:T(8,128)(2,1)S(1)}, bf16[128,2048]{1,0:T(8,128)(2,1)S(1)}, u32[]{:S(2)}, u32[]{:S(2)}) %collective-permute-start.11) | collective-permute-done | bytes 524320 | tf_op jit(solution)/shard_map/ppermute | solution.py:311
  41.8 1.3 %collective-permute-start.13 = (bf16[128,2048]{1,0:T(8,128)(2,1)S(1)}, bf16[128,2048]{1,0:T(8,128)(2,1)S(1)}, u32[]{:S(2)}, u32[]{:S(2)}) collective-permute-start(bf16[128,2048]{1,0:T(8,128)(2,1)S(1)} %after.4), channel_id=1, source_target_pairs={{24,17},{25,16},{26,19},{27,18},{28,21},{29,20},{30,23},{31,22}} | collective-permute-start | bytes 1572872 | tf_op jit(solution)/shard_map/ppermute | solution.py:311
  43.2 1.3 %collective-permute-start.12 = (bf16[128,2048]{1,0:T(8,128)(2,1)S(1)}, bf16[128,2048]{1,0:T(8,128)(2,1)S(1)}, u32[]{:S(2)}, u32[]{:S(2)}) collective-permute-start(bf16[128,2048]{1,0:T(8,128)(2,1)S(1)} %after.4), channel_id=1, source_target_pairs={{24,16},{25,17},{26,18},{27,19},{28,20},{29,21},{30,22},{31,23}} | collective-permute-start | bytes 1572872 | tf_op jit(solution)/shard_map/ppermute | solution.py:311
  46.0 3.2 %collective-permute-done.13.refs_1_ = bf16[128,2048]{1,0:T(8,128)(2,1)S(1)} collective-permute-done((bf16[128,2048]{1,0:T(8,128)(2,1)S(1)}, bf16[128,2048]{1,0:T(8,128)(2,1)S(1)}, u32[]{:S(2)}, u32[]{:S(2)}) %collective-permute-start.13) | collective-permute-done | bytes 524320 | tf_op jit(solution)/shard_map/ppermute | solution.py:311
  49.2 1.3 %collective-permute-start.15 = (bf16[128,2048]{1,0:T(8,128)(2,1)S(1)}, bf16[128,2048]{1,0:T(8,128)(2,1)S(1)}, u32[]{:S(2)}, u32[]{:S(2)}) collective-permute-start(bf16[128,2048]{1,0:T(8,128)(2,1)S(1)} %get-tuple-element.132.share), channel_id=1, source_target_pairs={{16,31},{17,30},{18,25},{19,24},{20,27},{21,26},{22,29},{23,28}} | collective-permute-start | bytes 1572872 | tf_op jit(solution)/shard_map/ppermute | solution.py:311
  50.5 1.3 %collective-permute-start.14 = (bf16[128,2048]{1,0:T(8,128)(2,1)S(1)}, bf16[128,2048]{1,0:T(8,128)(2,1)S(1)}, u32[]{:S(2)}, u32[]{:S(2)}) collective-permute-start(bf16[128,2048]{1,0:T(8,128)(2,1)S(1)} %get-tuple-element.132.share), channel_id=1, source_target_pairs={{16,30},{17,31},{18,24},{19,25},{20,26},{21,27},{22,28},{23,29}} | collective-permute-start | bytes 1572872 | tf_op jit(solution)/shard_map/ppermute | solution.py:311
  52.1 1.3 %collective-permute-start.17 = (bf16[128,2048]{1,0:T(8,128)(2,1)S(1)}, bf16[128,2048]{1,0:T(8,128)(2,1)S(1)}, u32[]{:S(2)}, u32[]{:S(2)}) collective-permute-start(bf16[128,2048]{1,0:T(8,128)(2,1)S(1)} %get-tuple-element.134), channel_id=1, source_target_pairs={{16,25},{17,24},{18,27},{19,26},{20,29},{21,28},{22,31},{23,30}} | collective-permute-start | bytes 1572872 | tf_op jit(solution)/shard_map/ppermute | solution.py:311
  53.4 1.3 %collective-permute-start.16 = (bf16[128,2048]{1,0:T(8,128)(2,1)S(1)}, bf16[128,2048]{1,0:T(8,128)(2,1)S(1)}, u32[]{:S(2)}, u32[]{:S(2)}) collective-permute-start(bf16[128,2048]{1,0:T(8,128)(2,1)S(1)} %get-tuple-element.134), channel_id=1, source_target_pairs={{16,24},{17,25},{18,26},{19,27},{20,28},{21,29},{22,30},{23,31}} | collective-permute-start | bytes 1572872 | tf_op jit(solution)/shard_map/ppermute | solution.py:311
  55.4 8.7 %collective-permute-done.15.refs_1_ = bf16[128,2048]{1,0:T(8,128)(2,1)S(1)} collective-permute-done((bf16[128,2048]{1,0:T(8,128)(2,1)S(1)}, bf16[128,2048]{1,0:T(8,128)(2,1)S(1)}, u32[]{:S(2)}, u32[]{:S(2)}) %collective-permute-start.15) | collective-permute-done | bytes 524320 | tf_op jit(solution)/shard_map/ppermute | solution.py:311
  64.7 5.2 %collective-permute-done.14.refs_0_ = bf16[128,2048]{1,0:T(8,128)(2,1)S(1)} collective-permute-done((bf16[128,2048]{1,0:T(8,128)(2,1)S(1)}, bf16[128,2048]{1,0:T(8,128)(2,1)S(1)}, u32[]{:S(2)}, u32[]{:S(2)}) %collective-permute-start.14) | collective-permute-done | bytes 524320 | tf_op jit(solution)/shard_map/ppermute | solution.py:311
  71.9 1.2 %attend.14 = (bf16[128,1024]{1,0:T(8,128)(2,1)S(1)}, bf16[128,1024]{1,0:T(8,128)(2,1)S(1)}, f32[8,128]{1,0:T(8,128)S(1)}) custom-call(f32[8,128]{1,0:T(8,128)S(1)} %get-tuple-element.137.mark, bf16[256,1024]{1,0:T(8,128)(2,1)S(1)} %get-tuple-element.138.k, bf16[256,1024]{1,0:T(8,128)(2,1)S(1)} %get-tuple-element.139.v, ...), custom_call_target="tpu_custom_call" | custom-call | flops 671088640 | bytes 4194304 | tf_op jit(solution)/shard_map/attend/pallas_call | solution.py:178
  73.1 1.3 %collective-permute-start.18 = (bf16[128,1024]{1,0:T(8,128)(2,1)S(1)}, bf16[128,1024]{1,0:T(8,128)(2,1)S(1)}, u32[]{:S(2)}, u32[]{:S(2)}) collective-permute-start(bf16[128,1024]{1,0:T(8,128)(2,1)S(1)} %get-tuple-element.144), channel_id=1, source_target_pairs={{24,19},{25,18},{26,21},{27,20},{28,23},{29,22},{30,17},{31,16}} | collective-permute-start | bytes 786440 | tf_op jit(solution)/shard_map/ppermute | solution.py:311
  74.4 1.3 %collective-permute-start.21 = (bf16[128,1024]{1,0:T(8,128)(2,1)S(1)}, bf16[128,1024]{1,0:T(8,128)(2,1)S(1)}, u32[]{:S(2)}, u32[]{:S(2)}) collective-permute-start(bf16[128,1024]{1,0:T(8,128)(2,1)S(1)} %get-tuple-element.152), channel_id=1, source_target_pairs={{24,18},{25,19},{26,20},{27,21},{28,22},{29,23},{30,16},{31,17}} | collective-permute-start | bytes 786440 | tf_op jit(solution)/shard_map/ppermute | solution.py:311
  75.7 1.2 %attend.15 = (bf16[256,1024]{1,0:T(8,128)(2,1)S(1)}, bf16[128,1024]{1,0:T(8,128)(2,1)S(1)}, f32[8,128]{1,0:T(8,128)S(1)}) custom-call(f32[8,128]{1,0:T(8,128)S(1)} %after.6.mark, bf16[256,1024]{1,0:T(8,128)(2,1)S(1)} %get-tuple-element.138.k, bf16[256,1024]{1,0:T(8,128)(2,1)S(1)} %get-tuple-element.139.v, bf16[128,2048]{1,0:T(8,128)(2,1)S(1)} %get-tuple-element.140.refs_0_, ...), custom_call_target="tpu_custom_call" | custom-call | flops 671088640 | bytes 4194304 | tf_op jit(solution)/shard_map/attend/pallas_call | solution.py:178
  76.9 1.3 %collective-permute-start.22 = (bf16[128,1024]{1,0:T(8,128)(2,1)S(1)}, bf16[128,1024]{1,0:T(8,128)(2,1)S(1)}, u32[]{:S(2)}, u32[]{:S(2)}) collective-permute-start(bf16[128,1024]{1,0:T(8,128)(2,1)S(1)} %get-tuple-element.155), channel_id=1, source_target_pairs={{24,17},{25,16},{26,19},{27,18},{28,21},{29,20},{30,23},{31,22}} | collective-permute-start | bytes 786440 | tf_op jit(solution)/shard_map/ppermute | solution.py:311
  78.2 1.3 %collective-permute-start.23 = (bf16[256,1024]{1,0:T(8,128)(2,1)S(1)}, bf16[256,1024]{1,0:T(8,128)(2,1)S(1)}, u32[]{:S(2)}, u32[]{:S(2)}) collective-permute-start(bf16[256,1024]{1,0:T(8,128)(2,1)S(1)} %get-tuple-element.159), channel_id=1, source_target_pairs={{24,16},{25,17},{26,18},{27,19},{28,20},{29,21},{30,22},{31,23}} | collective-permute-start | bytes 1572872 | tf_op jit(solution)/shard_map/ppermute | solution.py:311
  80.5 1.4 %collective-permute-done.22.refs_0_ = bf16[128,1024]{1,0:T(8,128)(2,1)S(1)} collective-permute-done((bf16[128,1024]{1,0:T(8,128)(2,1)S(1)}, bf16[128,1024]{1,0:T(8,128)(2,1)S(1)}, u32[]{:S(2)}, u32[]{:S(2)}) %collective-permute-start.22) | collective-permute-done | bytes 262176 | tf_op jit(solution)/shard_map/ppermute | solution.py:311
  81.9 1.3 %collective-permute-start.24 = (bf16[256,1024]{1,0:T(8,128)(2,1)S(1)}, bf16[256,1024]{1,0:T(8,128)(2,1)S(1)}, u32[]{:S(2)}, u32[]{:S(2)}) collective-permute-start(bf16[256,1024]{1,0:T(8,128)(2,1)S(1)} %get-tuple-element.160), channel_id=1, source_target_pairs={{16,24},{17,25},{18,26},{19,27},{20,28},{21,29},{22,30},{23,31}} | collective-permute-start | bytes 1572872 | tf_op jit(solution)/shard_map/ppermute | solution.py:311
  83.2 3.0 %collective-permute-done.24.total = bf16[256,1024]{1,0:T(8,128)(2,1)S(1)} collective-permute-done((bf16[256,1024]{1,0:T(8,128)(2,1)S(1)}, bf16[256,1024]{1,0:T(8,128)(2,1)S(1)}, u32[]{:S(2)}, u32[]{:S(2)}) %collective-permute-start.24) | collective-permute-done | bytes 524320 | tf_op jit(solution)/shard_map/ppermute | solution.py:311
  (65 shorter events, 13.8 us)
Async XLA Ops:
  0.0 4.6 %collective-permute-start = (bf16[128,2048]{1,0:T(8,128)(2,1)}, bf16[128,2048]{1,0:T(8,128)(2,1)S(1)}, u32[]{:S(2)}, u32[]{:S(2)}) collective-permute-start(bf16[128,2048]{1,0:T(8,128)(2,1)} %bitcast.20), channel_id=1, source_target_pairs={{0,1},{1,0},{2,3},{3,2},{4,5},{5,4},{6,7},{7,6}} | collective-permute-start | bytes 1572872 | tf_op jit(solution)/shard_map/ppermute | solution.py:311
  8.1 3.0 %collective-permute-start.2 = (bf16[128,2048]{1,0:T(8,128)(2,1)S(1)}, bf16[128,2048]{1,0:T(8,128)(2,1)S(1)}, u32[]{:S(2)}, u32[]{:S(2)}) collective-permute-start(bf16[128,2048]{1,0:T(8,128)(2,1)S(1)} %get-tuple-element.95), channel_id=1, source_target_pairs={{0,15},{1,14},{2,9},{3,8},{4,11},{5,10},{6,13},{7,12}} | collective-permute-start | bytes 1572872 | tf_op jit(solution)/shard_map/ppermute | solution.py:311
  8.9 2.1 %collective-permute-start.1 = (bf16[128,2048]{1,0:T(8,128)(2,1)S(1)}, bf16[128,2048]{1,0:T(8,128)(2,1)S(1)}, u32[]{:S(2)}, u32[]{:S(2)}) collective-permute-start(bf16[128,2048]{1,0:T(8,128)(2,1)S(1)} %get-tuple-element.95), channel_id=1, source_target_pairs={{0,14},{1,15},{2,8},{3,9},{4,10},{5,11},{6,12},{7,13}} | collective-permute-start | bytes 1572872 | tf_op jit(solution)/shard_map/ppermute | solution.py:311
  9.7 1.5 %collective-permute-start.4 = (bf16[128,2048]{1,0:T(8,128)(2,1)S(1)}, bf16[128,2048]{1,0:T(8,128)(2,1)S(1)}, u32[]{:S(2)}, u32[]{:S(2)}) collective-permute-start(bf16[128,2048]{1,0:T(8,128)(2,1)S(1)} %get-tuple-element.97), channel_id=1, source_target_pairs={{0,9},{1,8},{2,11},{3,10},{4,13},{5,12},{6,15},{7,14}} | collective-permute-start | bytes 1572872 | tf_op jit(solution)/shard_map/ppermute | solution.py:311
  10.4 0.8 collective-permute-start.3
  11.2 30.6 %collective-permute-start.11 = (bf16[128,2048]{1,0:T(8,128)(2,1)S(1)}, bf16[128,2048]{1,0:T(8,128)(2,1)S(1)}, u32[]{:S(2)}, u32[]{:S(2)}) collective-permute-start(bf16[128,2048]{1,0:T(8,128)(2,1)S(1)} %get-tuple-element.118), channel_id=1, source_target_pairs={{8,26},{9,27},{10,28},{11,29},{12,30},{13,31},{14,24},{15,25}} | collective-permute-start | bytes 1572872 | tf_op jit(solution)/shard_map/ppermute | solution.py:311
  12.5 30.6 %collective-permute-start.6 = (bf16[128,1024]{1,0:T(8,128)(2,1)S(1)}, bf16[128,1024]{1,0:T(8,128)(2,1)S(1)}, u32[]{:S(2)}, u32[]{:S(2)}) collective-permute-start(bf16[128,1024]{1,0:T(8,128)(2,1)S(1)} %get-tuple-element.110), channel_id=1, source_target_pairs={{8,1},{9,0},{10,3},{11,2},{12,5},{13,4},{14,7},{15,6}} | collective-permute-start | bytes 786440 | tf_op jit(solution)/shard_map/ppermute | solution.py:311
  13.2 31.3 %collective-permute-start.5 = (bf16[128,1024]{1,0:T(8,128)(2,1)S(1)}, bf16[128,1024]{1,0:T(8,128)(2,1)S(1)}, u32[]{:S(2)}, u32[]{:S(2)}) collective-permute-start(bf16[128,1024]{1,0:T(8,128)(2,1)S(1)} %get-tuple-element.110), channel_id=1, source_target_pairs={{8,0},{9,1},{10,2},{11,3},{12,4},{13,5},{14,6},{15,7}} | collective-permute-start | bytes 786440 | tf_op jit(solution)/shard_map/ppermute | solution.py:311
  13.9 31.3 %collective-permute-start.8 = (bf16[128,1024]{1,0:T(8,128)(2,1)S(1)}, bf16[128,1024]{1,0:T(8,128)(2,1)S(1)}, u32[]{:S(2)}, u32[]{:S(2)}) collective-permute-start(bf16[128,1024]{1,0:T(8,128)(2,1)S(1)} %get-tuple-element.112), channel_id=1, source_target_pairs={{8,1},{9,0},{10,3},{11,2},{12,5},{13,4},{14,7},{15,6}} | collective-permute-start | bytes 786440 | tf_op jit(solution)/shard_map/ppermute | solution.py:311
  14.6 30.6 %collective-permute-start.7 = (bf16[128,1024]{1,0:T(8,128)(2,1)S(1)}, bf16[128,1024]{1,0:T(8,128)(2,1)S(1)}, u32[]{:S(2)}, u32[]{:S(2)}) collective-permute-start(bf16[128,1024]{1,0:T(8,128)(2,1)S(1)} %get-tuple-element.112), channel_id=1, source_target_pairs={{8,0},{9,1},{10,2},{11,3},{12,4},{13,5},{14,6},{15,7}} | collective-permute-start | bytes 786440 | tf_op jit(solution)/shard_map/ppermute | solution.py:311
  41.8 7.4 %collective-permute-start.13 = (bf16[128,2048]{1,0:T(8,128)(2,1)S(1)}, bf16[128,2048]{1,0:T(8,128)(2,1)S(1)}, u32[]{:S(2)}, u32[]{:S(2)}) collective-permute-start(bf16[128,2048]{1,0:T(8,128)(2,1)S(1)} %after.4), channel_id=1, source_target_pairs={{24,17},{25,16},{26,19},{27,18},{28,21},{29,20},{30,23},{31,22}} | collective-permute-start | bytes 1572872 | tf_op jit(solution)/shard_map/ppermute | solution.py:311
  43.2 6.1 %collective-permute-start.12 = (bf16[128,2048]{1,0:T(8,128)(2,1)S(1)}, bf16[128,2048]{1,0:T(8,128)(2,1)S(1)}, u32[]{:S(2)}, u32[]{:S(2)}) collective-permute-start(bf16[128,2048]{1,0:T(8,128)(2,1)S(1)} %after.4), channel_id=1, source_target_pairs={{24,16},{25,17},{26,18},{27,19},{28,20},{29,21},{30,22},{31,23}} | collective-permute-start | bytes 1572872 | tf_op jit(solution)/shard_map/ppermute | solution.py:311
  44.5 1.4 %collective-permute-start.9 = (bf16[128,1024]{1,0:T(8,128)(2,1)S(1)}, bf16[128,1024]{1,0:T(8,128)(2,1)S(1)}, u32[]{:S(2)}, u32[]{:S(2)}) collective-permute-start(bf16[128,1024]{1,0:T(8,128)(2,1)S(1)} %get-tuple-element.114), channel_id=1, source_target_pairs={{0,16},{1,17},{2,18},{3,19},{4,20},{5,21},{6,22},{7,23}} | collective-permute-start | bytes 786440 | tf_op jit(solution)/shard_map/ppermute | solution.py:311
  49.2 14.8 %collective-permute-start.15 = (bf16[128,2048]{1,0:T(8,128)(2,1)S(1)}, bf16[128,2048]{1,0:T(8,128)(2,1)S(1)}, u32[]{:S(2)}, u32[]{:S(2)}) collective-permute-start(bf16[128,2048]{1,0:T(8,128)(2,1)S(1)} %get-tuple-element.132.share), channel_id=1, source_target_pairs={{16,31},{17,30},{18,25},{19,24},{20,27},{21,26},{22,29},{23,28}} | collective-permute-start | bytes 1572872 | tf_op jit(solution)/shard_map/ppermute | solution.py:311
  50.5 19.4 %collective-permute-start.14 = (bf16[128,2048]{1,0:T(8,128)(2,1)S(1)}, bf16[128,2048]{1,0:T(8,128)(2,1)S(1)}, u32[]{:S(2)}, u32[]{:S(2)}) collective-permute-start(bf16[128,2048]{1,0:T(8,128)(2,1)S(1)} %get-tuple-element.132.share), channel_id=1, source_target_pairs={{16,30},{17,31},{18,24},{19,25},{20,26},{21,27},{22,28},{23,29}} | collective-permute-start | bytes 1572872 | tf_op jit(solution)/shard_map/ppermute | solution.py:311
  52.1 18.8 %collective-permute-start.17 = (bf16[128,2048]{1,0:T(8,128)(2,1)S(1)}, bf16[128,2048]{1,0:T(8,128)(2,1)S(1)}, u32[]{:S(2)}, u32[]{:S(2)}) collective-permute-start(bf16[128,2048]{1,0:T(8,128)(2,1)S(1)} %get-tuple-element.134), channel_id=1, source_target_pairs={{16,25},{17,24},{18,27},{19,26},{20,29},{21,28},{22,31},{23,30}} | collective-permute-start | bytes 1572872 | tf_op jit(solution)/shard_map/ppermute | solution.py:311
  53.4 17.5 %collective-permute-start.16 = (bf16[128,2048]{1,0:T(8,128)(2,1)S(1)}, bf16[128,2048]{1,0:T(8,128)(2,1)S(1)}, u32[]{:S(2)}, u32[]{:S(2)}) collective-permute-start(bf16[128,2048]{1,0:T(8,128)(2,1)S(1)} %get-tuple-element.134), channel_id=1, source_target_pairs={{16,24},{17,25},{18,26},{19,27},{20,28},{21,29},{22,30},{23,31}} | collective-permute-start | bytes 1572872 | tf_op jit(solution)/shard_map/ppermute | solution.py:311
  54.7 21.1 %collective-permute-start.19 = (bf16[256,1024]{1,0:T(8,128)(2,1)S(1)}, bf16[256,1024]{1,0:T(8,128)(2,1)S(1)}, u32[]{:S(2)}, u32[]{:S(2)}) collective-permute-start(bf16[256,1024]{1,0:T(8,128)(2,1)S(1)} %get-tuple-element.147), channel_id=1, source_target_pairs={{8,0},{9,1},{10,2},{11,3},{12,4},{13,5},{14,6},{15,7},{16,8},{17,9... | collective-permute-start | bytes 1572872 | tf_op jit(solution)/shard_map/ppermute | solution.py:311
  64.0 11.7 %collective-permute-start.20 = (bf16[128,1024]{1,0:T(8,128)(2,1)S(1)}, bf16[128,1024]{1,0:T(8,128)(2,1)S(1)}, u32[]{:S(2)}, u32[]{:S(2)}) collective-permute-start(bf16[128,1024]{1,0:T(8,128)(2,1)S(1)} %get-tuple-element.148), channel_id=1, source_target_pairs={{8,2},{9,3},{10,4},{11,5},{12,6},{13,7},{14,0},{15,1},{16,17},{17,... | collective-permute-start | bytes 786440 | tf_op jit(solution)/shard_map/ppermute | solution.py:311
  73.1 6.5 %collective-permute-start.18 = (bf16[128,1024]{1,0:T(8,128)(2,1)S(1)}, bf16[128,1024]{1,0:T(8,128)(2,1)S(1)}, u32[]{:S(2)}, u32[]{:S(2)}) collective-permute-start(bf16[128,1024]{1,0:T(8,128)(2,1)S(1)} %get-tuple-element.144), channel_id=1, source_target_pairs={{24,19},{25,18},{26,21},{27,20},{28,23},{29,22},{30,17},{31,16}} | collective-permute-start | bytes 786440 | tf_op jit(solution)/shard_map/ppermute | solution.py:311
  74.4 6.1 %collective-permute-start.21 = (bf16[128,1024]{1,0:T(8,128)(2,1)S(1)}, bf16[128,1024]{1,0:T(8,128)(2,1)S(1)}, u32[]{:S(2)}, u32[]{:S(2)}) collective-permute-start(bf16[128,1024]{1,0:T(8,128)(2,1)S(1)} %get-tuple-element.152), channel_id=1, source_target_pairs={{24,18},{25,19},{26,20},{27,21},{28,22},{29,23},{30,16},{31,17}} | collective-permute-start | bytes 786440 | tf_op jit(solution)/shard_map/ppermute | solution.py:311
  76.9 4.9 %collective-permute-start.22 = (bf16[128,1024]{1,0:T(8,128)(2,1)S(1)}, bf16[128,1024]{1,0:T(8,128)(2,1)S(1)}, u32[]{:S(2)}, u32[]{:S(2)}) collective-permute-start(bf16[128,1024]{1,0:T(8,128)(2,1)S(1)} %get-tuple-element.155), channel_id=1, source_target_pairs={{24,17},{25,16},{26,19},{27,18},{28,21},{29,20},{30,23},{31,22}} | collective-permute-start | bytes 786440 | tf_op jit(solution)/shard_map/ppermute | solution.py:311
  78.2 3.6 %collective-permute-start.23 = (bf16[256,1024]{1,0:T(8,128)(2,1)S(1)}, bf16[256,1024]{1,0:T(8,128)(2,1)S(1)}, u32[]{:S(2)}, u32[]{:S(2)}) collective-permute-start(bf16[256,1024]{1,0:T(8,128)(2,1)S(1)} %get-tuple-element.159), channel_id=1, source_target_pairs={{24,16},{25,17},{26,18},{27,19},{28,20},{29,21},{30,22},{31,23}} | collective-permute-start | bytes 1572872 | tf_op jit(solution)/shard_map/ppermute | solution.py:311
  81.9 4.3 %collective-permute-start.24 = (bf16[256,1024]{1,0:T(8,128)(2,1)S(1)}, bf16[256,1024]{1,0:T(8,128)(2,1)S(1)}, u32[]{:S(2)}, u32[]{:S(2)}) collective-permute-start(bf16[256,1024]{1,0:T(8,128)(2,1)S(1)} %get-tuple-element.160), channel_id=1, source_target_pairs={{16,24},{17,25},{18,26},{19,27},{20,28},{21,29},{22,30},{23,31}} | collective-permute-start | bytes 1572872 | tf_op jit(solution)/shard_map/ppermute | solution.py:311
  (7 other events, 13.3 us)

commit v8 on v7

--- a/solution.py
+++ b/solution.py
@@ -365,7 +365,7 @@
             ]
             sums = []
             for number, terms in enumerate(moved[1]):
-                total, mark = add(section - 1, terms, mark, 0)
+                total, mark = add(section - 1, terms, mark, 4 * 10**9 if number else 0)
                 sums.append(send(total, section - 1, section + 1))
             moved[1] = [sums]
         if section + 2 == sections:

time: 87.7 us -> 87 us (level)
  no operation moved by 1% of the time
where the time goes in v8:
time: 87 us; the launch traced here: 86.4 us
  waiting for transfers between devices  48.4 us (56%)
  starting transfers between devices  24.6 us (28%)
  local copies, waits for them, and re-layouts  7.38 us (8%)
  Pallas kernels  5.5 us (6%)
    ppermute x25, waiting for transfers between devices, send_all(): return lax.ppermute(value, AXES, pairs)  48.4 us
    ppermute x25, starting transfers between devices, send_all(): return lax.ppermute(value, AXES, pairs)  24.6 us
    unnamed x12, local copies, waits for them, and re-layouts  7.38 us
    pallas_call x8, Pallas kernels, attend(): pl.pallas_call(functools.partial(attend_kernel, section, pieces, len(bloc...  2.64 us
    pallas_call x8, Pallas kernels, project(): pl.pallas_call(functools.partial(project_kernel, section, chunk_order, co...  1.99 us
  transfers between devices with their start and end apart: 25, of which 7 were waited for; matrix products, arithmetic and copies ran while one was open for 0% of the time, Pallas kernels for 5%

profile of v8, /device:TPU:5, one launch (start us, length us, event | category | flops | bytes accessed | tf_op | source)
XLA Modules:
  0.0 86.4 jit_solution(10582146187149505038)
XLA Ops:
  0.7 2.2 %copy-done = bf16[1,2048,1024]{2,1,0:T(8,128)(2,1)S(1)} copy-done((bf16[1,2048,1024]{2,1,0:T(8,128)(2,1)S(1)}, bf16[1,2048,1024]{2,1,0:T(8,128)(2,1)}, u32[]{:S(2)}) %copy-start) | copy-done | bytes 4194328
  3.6 1.0 %copy-done.5 = bf16[4,32,2048]{2,1,0:T(8,128)(2,1)S(1)} copy-done((bf16[4,32,2048]{2,1,0:T(8,128)(2,1)S(1)}, bf16[4,32,2048]{2,1,0:T(8,128)(2,1)}, u32[]{:S(2)}) %copy-start.5) | copy-done | bytes 524312
  4.6 2.2 %copy-done.1 = bf16[1,2048,1024]{2,1,0:T(8,128)(2,1)S(1)} copy-done((bf16[1,2048,1024]{2,1,0:T(8,128)(2,1)S(1)}, bf16[1,2048,1024]{2,1,0:T(8,128)(2,1)}, u32[]{:S(2)}) %copy-start.1) | copy-done | bytes 4194328
  6.8 1.3 %copy-done.2 = bf16[1,1024,2048]{2,1,0:T(8,128)(2,1)S(1)} copy-done((bf16[1,1024,2048]{2,1,0:T(8,128)(2,1)S(1)}, bf16[1,1024,2048]{2,1,0:T(8,128)(2,1)}, u32[]{:S(2)}) %copy-start.2) | copy-done | bytes 4194328
  11.2 1.3 %collective-permute-start.11 = (bf16[128,2048]{1,0:T(8,128)(2,1)S(1)}, bf16[128,2048]{1,0:T(8,128)(2,1)S(1)}, u32[]{:S(2)}, u32[]{:S(2)}) collective-permute-start(bf16[128,2048]{1,0:T(8,128)(2,1)S(1)} %get-tuple-element.118), channel_id=1, source_target_pairs={{8,26},{9,27},{10,28},{11,29},{12,30},{13,31},{14,24},{15,25}} | collective-permute-start | bytes 1572872 | tf_op jit(solution)/shard_map/ppermute | solution.py:311
  16.0 25.8 %collective-permute-done.11.refs_0_ = bf16[128,2048]{1,0:T(8,128)(2,1)S(1)} collective-permute-done((bf16[128,2048]{1,0:T(8,128)(2,1)S(1)}, bf16[128,2048]{1,0:T(8,128)(2,1)S(1)}, u32[]{:S(2)}, u32[]{:S(2)}) %collective-permute-start.11) | collective-permute-done | bytes 524320 | tf_op jit(solution)/shard_map/ppermute | solution.py:311
  41.8 1.3 %collective-permute-start.13 = (bf16[128,2048]{1,0:T(8,128)(2,1)S(1)}, bf16[128,2048]{1,0:T(8,128)(2,1)S(1)}, u32[]{:S(2)}, u32[]{:S(2)}) collective-permute-start(bf16[128,2048]{1,0:T(8,128)(2,1)S(1)} %after.4), channel_id=1, source_target_pairs={{24,17},{25,16},{26,19},{27,18},{28,21},{29,20},{30,23},{31,22}} | collective-permute-start | bytes 1572872 | tf_op jit(solution)/shard_map/ppermute | solution.py:311
  43.1 1.3 %collective-permute-start.12 = (bf16[128,2048]{1,0:T(8,128)(2,1)S(1)}, bf16[128,2048]{1,0:T(8,128)(2,1)S(1)}, u32[]{:S(2)}, u32[]{:S(2)}) collective-permute-start(bf16[128,2048]{1,0:T(8,128)(2,1)S(1)} %after.4), channel_id=1, source_target_pairs={{24,16},{25,17},{26,18},{27,19},{28,20},{29,21},{30,22},{31,23}} | collective-permute-start | bytes 1572872 | tf_op jit(solution)/shard_map/ppermute | solution.py:311
  45.3 4.0 %collective-permute-done.13.refs_1_ = bf16[128,2048]{1,0:T(8,128)(2,1)S(1)} collective-permute-done((bf16[128,2048]{1,0:T(8,128)(2,1)S(1)}, bf16[128,2048]{1,0:T(8,128)(2,1)S(1)}, u32[]{:S(2)}, u32[]{:S(2)}) %collective-permute-start.13) | collective-permute-done | bytes 524320 | tf_op jit(solution)/shard_map/ppermute | solution.py:311
  49.2 1.3 %collective-permute-start.15 = (bf16[128,2048]{1,0:T(8,128)(2,1)S(1)}, bf16[128,2048]{1,0:T(8,128)(2,1)S(1)}, u32[]{:S(2)}, u32[]{:S(2)}) collective-permute-start(bf16[128,2048]{1,0:T(8,128)(2,1)S(1)} %get-tuple-element.132.share), channel_id=1, source_target_pairs={{16,31},{17,30},{18,25},{19,24},{20,27},{21,26},{22,29},{23,28}} | collective-permute-start | bytes 1572872 | tf_op jit(solution)/shard_map/ppermute | solution.py:311
  50.5 1.3 %collective-permute-start.14 = (bf16[128,2048]{1,0:T(8,128)(2,1)S(1)}, bf16[128,2048]{1,0:T(8,128)(2,1)S(1)}, u32[]{:S(2)}, u32[]{:S(2)}) collective-permute-start(bf16[128,2048]{1,0:T(8,128)(2,1)S(1)} %get-tuple-element.132.share), channel_id=1, source_target_pairs={{16,30},{17,31},{18,24},{19,25},{20,26},{21,27},{22,28},{23,29}} | collective-permute-start | bytes 1572872 | tf_op jit(solution)/shard_map/ppermute | solution.py:311
  52.1 1.3 %collective-permute-start.17 = (bf16[128,2048]{1,0:T(8,128)(2,1)S(1)}, bf16[128,2048]{1,0:T(8,128)(2,1)S(1)}, u32[]{:S(2)}, u32[]{:S(2)}) collective-permute-start(bf16[128,2048]{1,0:T(8,128)(2,1)S(1)} %get-tuple-element.134), channel_id=1, source_target_pairs={{16,25},{17,24},{18,27},{19,26},{20,29},{21,28},{22,31},{23,30}} | collective-permute-start | bytes 1572872 | tf_op jit(solution)/shard_map/ppermute | solution.py:311
  53.4 1.3 %collective-permute-start.16 = (bf16[128,2048]{1,0:T(8,128)(2,1)S(1)}, bf16[128,2048]{1,0:T(8,128)(2,1)S(1)}, u32[]{:S(2)}, u32[]{:S(2)}) collective-permute-start(bf16[128,2048]{1,0:T(8,128)(2,1)S(1)} %get-tuple-element.134), channel_id=1, source_target_pairs={{16,24},{17,25},{18,26},{19,27},{20,28},{21,29},{22,30},{23,31}} | collective-permute-start | bytes 1572872 | tf_op jit(solution)/shard_map/ppermute | solution.py:311
  55.4 8.0 %collective-permute-done.15.refs_1_ = bf16[128,2048]{1,0:T(8,128)(2,1)S(1)} collective-permute-done((bf16[128,2048]{1,0:T(8,128)(2,1)S(1)}, bf16[128,2048]{1,0:T(8,128)(2,1)S(1)}, u32[]{:S(2)}, u32[]{:S(2)}) %collective-permute-start.15) | collective-permute-done | bytes 524320 | tf_op jit(solution)/shard_map/ppermute | solution.py:311
  64.0 5.2 %collective-permute-done.14.refs_0_ = bf16[128,2048]{1,0:T(8,128)(2,1)S(1)} collective-permute-done((bf16[128,2048]{1,0:T(8,128)(2,1)S(1)}, bf16[128,2048]{1,0:T(8,128)(2,1)S(1)}, u32[]{:S(2)}, u32[]{:S(2)}) %collective-permute-start.14) | collective-permute-done | bytes 524320 | tf_op jit(solution)/shard_map/ppermute | solution.py:311
  71.2 1.2 %attend.14 = (bf16[128,1024]{1,0:T(8,128)(2,1)S(1)}, bf16[128,1024]{1,0:T(8,128)(2,1)S(1)}, f32[8,128]{1,0:T(8,128)S(1)}) custom-call(f32[8,128]{1,0:T(8,128)S(1)} %get-tuple-element.137.mark, bf16[256,1024]{1,0:T(8,128)(2,1)S(1)} %get-tuple-element.138.k, bf16[256,1024]{1,0:T(8,128)(2,1)S(1)} %get-tuple-element.139.v, ...), custom_call_target="tpu_custom_call" | custom-call | flops 671088640 | bytes 4194304 | tf_op jit(solution)/shard_map/attend/pallas_call | solution.py:178
  72.4 1.3 %collective-permute-start.18 = (bf16[128,1024]{1,0:T(8,128)(2,1)S(1)}, bf16[128,1024]{1,0:T(8,128)(2,1)S(1)}, u32[]{:S(2)}, u32[]{:S(2)}) collective-permute-start(bf16[128,1024]{1,0:T(8,128)(2,1)S(1)} %get-tuple-element.144), channel_id=1, source_target_pairs={{24,19},{25,18},{26,21},{27,20},{28,23},{29,22},{30,17},{31,16}} | collective-permute-start | bytes 786440 | tf_op jit(solution)/shard_map/ppermute | solution.py:311
  73.7 1.3 %collective-permute-start.21 = (bf16[128,1024]{1,0:T(8,128)(2,1)S(1)}, bf16[128,1024]{1,0:T(8,128)(2,1)S(1)}, u32[]{:S(2)}, u32[]{:S(2)}) collective-permute-start(bf16[128,1024]{1,0:T(8,128)(2,1)S(1)} %get-tuple-element.152), channel_id=1, source_target_pairs={{24,18},{25,19},{26,20},{27,21},{28,22},{29,23},{30,16},{31,17}} | collective-permute-start | bytes 786440 | tf_op jit(solution)/shard_map/ppermute | solution.py:311
  75.1 1.2 %attend.15 = (bf16[256,1024]{1,0:T(8,128)(2,1)S(1)}, bf16[128,1024]{1,0:T(8,128)(2,1)S(1)}, f32[8,128]{1,0:T(8,128)S(1)}) custom-call(f32[8,128]{1,0:T(8,128)S(1)} %after.6.mark, bf16[256,1024]{1,0:T(8,128)(2,1)S(1)} %get-tuple-element.138.k, bf16[256,1024]{1,0:T(8,128)(2,1)S(1)} %get-tuple-element.139.v, bf16[128,2048]{1,0:T(8,128)(2,1)S(1)} %get-tuple-element.140.refs_0_, ...), custom_call_target="tpu_custom_call" | custom-call | flops 671088640 | bytes 4194304 | tf_op jit(solution)/shard_map/attend/pallas_call | solution.py:178
  76.3 1.3 %collective-permute-start.22 = (bf16[128,1024]{1,0:T(8,128)(2,1)S(1)}, bf16[128,1024]{1,0:T(8,128)(2,1)S(1)}, u32[]{:S(2)}, u32[]{:S(2)}) collective-permute-start(bf16[128,1024]{1,0:T(8,128)(2,1)S(1)} %get-tuple-element.155), channel_id=1, source_target_pairs={{24,17},{25,16},{26,19},{27,18},{28,21},{29,20},{30,23},{31,22}} | collective-permute-start | bytes 786440 | tf_op jit(solution)/shard_map/ppermute | solution.py:311
  77.6 1.3 %collective-permute-start.23 = (bf16[256,1024]{1,0:T(8,128)(2,1)S(1)}, bf16[256,1024]{1,0:T(8,128)(2,1)S(1)}, u32[]{:S(2)}, u32[]{:S(2)}) collective-permute-start(bf16[256,1024]{1,0:T(8,128)(2,1)S(1)} %get-tuple-element.159), channel_id=1, source_target_pairs={{24,16},{25,17},{26,18},{27,19},{28,20},{29,21},{30,22},{31,23}} | collective-permute-start | bytes 1572872 | tf_op jit(solution)/shard_map/ppermute | solution.py:311
  79.8 1.4 %collective-permute-done.22.refs_0_ = bf16[128,1024]{1,0:T(8,128)(2,1)S(1)} collective-permute-done((bf16[128,1024]{1,0:T(8,128)(2,1)S(1)}, bf16[128,1024]{1,0:T(8,128)(2,1)S(1)}, u32[]{:S(2)}, u32[]{:S(2)}) %collective-permute-start.22) | collective-permute-done | bytes 262176 | tf_op jit(solution)/shard_map/ppermute | solution.py:311
  81.2 1.3 %collective-permute-start.24 = (bf16[256,1024]{1,0:T(8,128)(2,1)S(1)}, bf16[256,1024]{1,0:T(8,128)(2,1)S(1)}, u32[]{:S(2)}, u32[]{:S(2)}) collective-permute-start(bf16[256,1024]{1,0:T(8,128)(2,1)S(1)} %get-tuple-element.160), channel_id=1, source_target_pairs={{16,24},{17,25},{18,26},{19,27},{20,28},{21,29},{22,30},{23,31}} | collective-permute-start | bytes 1572872 | tf_op jit(solution)/shard_map/ppermute | solution.py:311
  82.5 3.0 %collective-permute-done.24.total = bf16[256,1024]{1,0:T(8,128)(2,1)S(1)} collective-permute-done((bf16[256,1024]{1,0:T(8,128)(2,1)S(1)}, bf16[256,1024]{1,0:T(8,128)(2,1)S(1)}, u32[]{:S(2)}, u32[]{:S(2)}) %collective-permute-start.24) | collective-permute-done | bytes 524320 | tf_op jit(solution)/shard_map/ppermute | solution.py:311
  (65 shorter events, 13.8 us)
Async XLA Ops:
  0.0 4.6 %collective-permute-start = (bf16[128,2048]{1,0:T(8,128)(2,1)}, bf16[128,2048]{1,0:T(8,128)(2,1)S(1)}, u32[]{:S(2)}, u32[]{:S(2)}) collective-permute-start(bf16[128,2048]{1,0:T(8,128)(2,1)} %bitcast.20), channel_id=1, source_target_pairs={{0,1},{1,0},{2,3},{3,2},{4,5},{5,4},{6,7},{7,6}} | collective-permute-start | bytes 1572872 | tf_op jit(solution)/shard_map/ppermute | solution.py:311
  8.1 3.0 %collective-permute-start.2 = (bf16[128,2048]{1,0:T(8,128)(2,1)S(1)}, bf16[128,2048]{1,0:T(8,128)(2,1)S(1)}, u32[]{:S(2)}, u32[]{:S(2)}) collective-permute-start(bf16[128,2048]{1,0:T(8,128)(2,1)S(1)} %get-tuple-element.95), channel_id=1, source_target_pairs={{0,15},{1,14},{2,9},{3,8},{4,11},{5,10},{6,13},{7,12}} | collective-permute-start | bytes 1572872 | tf_op jit(solution)/shard_map/ppermute | solution.py:311
  8.9 2.1 %collective-permute-start.1 = (bf16[128,2048]{1,0:T(8,128)(2,1)S(1)}, bf16[128,2048]{1,0:T(8,128)(2,1)S(1)}, u32[]{:S(2)}, u32[]{:S(2)}) collective-permute-start(bf16[128,2048]{1,0:T(8,128)(2,1)S(1)} %get-tuple-element.95), channel_id=1, source_target_pairs={{0,14},{1,15},{2,8},{3,9},{4,10},{5,11},{6,12},{7,13}} | collective-permute-start | bytes 1572872 | tf_op jit(solution)/shard_map/ppermute | solution.py:311
  9.7 1.5 %collective-permute-start.4 = (bf16[128,2048]{1,0:T(8,128)(2,1)S(1)}, bf16[128,2048]{1,0:T(8,128)(2,1)S(1)}, u32[]{:S(2)}, u32[]{:S(2)}) collective-permute-start(bf16[128,2048]{1,0:T(8,128)(2,1)S(1)} %get-tuple-element.97), channel_id=1, source_target_pairs={{0,9},{1,8},{2,11},{3,10},{4,13},{5,12},{6,15},{7,14}} | collective-permute-start | bytes 1572872 | tf_op jit(solution)/shard_map/ppermute | solution.py:311
  10.4 0.8 collective-permute-start.3
  11.2 30.6 %collective-permute-start.11 = (bf16[128,2048]{1,0:T(8,128)(2,1)S(1)}, bf16[128,2048]{1,0:T(8,128)(2,1)S(1)}, u32[]{:S(2)}, u32[]{:S(2)}) collective-permute-start(bf16[128,2048]{1,0:T(8,128)(2,1)S(1)} %get-tuple-element.118), channel_id=1, source_target_pairs={{8,26},{9,27},{10,28},{11,29},{12,30},{13,31},{14,24},{15,25}} | collective-permute-start | bytes 1572872 | tf_op jit(solution)/shard_map/ppermute | solution.py:311
  12.5 2.7 %collective-permute-start.6 = (bf16[128,1024]{1,0:T(8,128)(2,1)S(1)}, bf16[128,1024]{1,0:T(8,128)(2,1)S(1)}, u32[]{:S(2)}, u32[]{:S(2)}) collective-permute-start(bf16[128,1024]{1,0:T(8,128)(2,1)S(1)} %get-tuple-element.110), channel_id=1, source_target_pairs={{8,1},{9,0},{10,3},{11,2},{12,5},{13,4},{14,7},{15,6}} | collective-permute-start | bytes 786440 | tf_op jit(solution)/shard_map/ppermute | solution.py:311
  13.2 2.1 %collective-permute-start.5 = (bf16[128,1024]{1,0:T(8,128)(2,1)S(1)}, bf16[128,1024]{1,0:T(8,128)(2,1)S(1)}, u32[]{:S(2)}, u32[]{:S(2)}) collective-permute-start(bf16[128,1024]{1,0:T(8,128)(2,1)S(1)} %get-tuple-element.110), channel_id=1, source_target_pairs={{8,0},{9,1},{10,2},{11,3},{12,4},{13,5},{14,6},{15,7}} | collective-permute-start | bytes 786440 | tf_op jit(solution)/shard_map/ppermute | solution.py:311
  13.9 30.6 %collective-permute-start.8 = (bf16[128,1024]{1,0:T(8,128)(2,1)S(1)}, bf16[128,1024]{1,0:T(8,128)(2,1)S(1)}, u32[]{:S(2)}, u32[]{:S(2)}) collective-permute-start(bf16[128,1024]{1,0:T(8,128)(2,1)S(1)} %get-tuple-element.112), channel_id=1, source_target_pairs={{8,1},{9,0},{10,3},{11,2},{12,5},{13,4},{14,7},{15,6}} | collective-permute-start | bytes 786440 | tf_op jit(solution)/shard_map/ppermute | solution.py:311
  14.6 29.9 %collective-permute-start.7 = (bf16[128,1024]{1,0:T(8,128)(2,1)S(1)}, bf16[128,1024]{1,0:T(8,128)(2,1)S(1)}, u32[]{:S(2)}, u32[]{:S(2)}) collective-permute-start(bf16[128,1024]{1,0:T(8,128)(2,1)S(1)} %get-tuple-element.112), channel_id=1, source_target_pairs={{8,0},{9,1},{10,2},{11,3},{12,4},{13,5},{14,6},{15,7}} | collective-permute-start | bytes 786440 | tf_op jit(solution)/shard_map/ppermute | solution.py:311
  15.3 29.9 %collective-permute-start.9 = (bf16[128,1024]{1,0:T(8,128)(2,1)S(1)}, bf16[128,1024]{1,0:T(8,128)(2,1)S(1)}, u32[]{:S(2)}, u32[]{:S(2)}) collective-permute-start(bf16[128,1024]{1,0:T(8,128)(2,1)S(1)} %get-tuple-element.114), channel_id=1, source_target_pairs={{0,16},{1,17},{2,18},{3,19},{4,20},{5,21},{6,22},{7,23}} | collective-permute-start | bytes 786440 | tf_op jit(solution)/shard_map/ppermute | solution.py:311
  41.8 7.4 %collective-permute-start.13 = (bf16[128,2048]{1,0:T(8,128)(2,1)S(1)}, bf16[128,2048]{1,0:T(8,128)(2,1)S(1)}, u32[]{:S(2)}, u32[]{:S(2)}) collective-permute-start(bf16[128,2048]{1,0:T(8,128)(2,1)S(1)} %after.4), channel_id=1, source_target_pairs={{24,17},{25,16},{26,19},{27,18},{28,21},{29,20},{30,23},{31,22}} | collective-permute-start | bytes 1572872 | tf_op jit(solution)/shard_map/ppermute | solution.py:311
  43.1 6.1 %collective-permute-start.12 = (bf16[128,2048]{1,0:T(8,128)(2,1)S(1)}, bf16[128,2048]{1,0:T(8,128)(2,1)S(1)}, u32[]{:S(2)}, u32[]{:S(2)}) collective-permute-start(bf16[128,2048]{1,0:T(8,128)(2,1)S(1)} %after.4), channel_id=1, source_target_pairs={{24,16},{25,17},{26,18},{27,19},{28,20},{29,21},{30,22},{31,23}} | collective-permute-start | bytes 1572872 | tf_op jit(solution)/shard_map/ppermute | solution.py:311
  49.2 14.1 %collective-permute-start.15 = (bf16[128,2048]{1,0:T(8,128)(2,1)S(1)}, bf16[128,2048]{1,0:T(8,128)(2,1)S(1)}, u32[]{:S(2)}, u32[]{:S(2)}) collective-permute-start(bf16[128,2048]{1,0:T(8,128)(2,1)S(1)} %get-tuple-element.132.share), channel_id=1, source_target_pairs={{16,31},{17,30},{18,25},{19,24},{20,27},{21,26},{22,29},{23,28}} | collective-permute-start | bytes 1572872 | tf_op jit(solution)/shard_map/ppermute | solution.py:311
  50.5 18.7 %collective-permute-start.14 = (bf16[128,2048]{1,0:T(8,128)(2,1)S(1)}, bf16[128,2048]{1,0:T(8,128)(2,1)S(1)}, u32[]{:S(2)}, u32[]{:S(2)}) collective-permute-start(bf16[128,2048]{1,0:T(8,128)(2,1)S(1)} %get-tuple-element.132.share), channel_id=1, source_target_pairs={{16,30},{17,31},{18,24},{19,25},{20,26},{21,27},{22,28},{23,29}} | collective-permute-start | bytes 1572872 | tf_op jit(solution)/shard_map/ppermute | solution.py:311
  52.1 18.1 %collective-permute-start.17 = (bf16[128,2048]{1,0:T(8,128)(2,1)S(1)}, bf16[128,2048]{1,0:T(8,128)(2,1)S(1)}, u32[]{:S(2)}, u32[]{:S(2)}) collective-permute-start(bf16[128,2048]{1,0:T(8,128)(2,1)S(1)} %get-tuple-element.134), channel_id=1, source_target_pairs={{16,25},{17,24},{18,27},{19,26},{20,29},{21,28},{22,31},{23,30}} | collective-permute-start | bytes 1572872 | tf_op jit(solution)/shard_map/ppermute | solution.py:311
  53.4 16.8 %collective-permute-start.16 = (bf16[128,2048]{1,0:T(8,128)(2,1)S(1)}, bf16[128,2048]{1,0:T(8,128)(2,1)S(1)}, u32[]{:S(2)}, u32[]{:S(2)}) collective-permute-start(bf16[128,2048]{1,0:T(8,128)(2,1)S(1)} %get-tuple-element.134), channel_id=1, source_target_pairs={{16,24},{17,25},{18,26},{19,27},{20,28},{21,29},{22,30},{23,31}} | collective-permute-start | bytes 1572872 | tf_op jit(solution)/shard_map/ppermute | solution.py:311
  54.7 20.4 %collective-permute-start.19 = (bf16[256,1024]{1,0:T(8,128)(2,1)S(1)}, bf16[256,1024]{1,0:T(8,128)(2,1)S(1)}, u32[]{:S(2)}, u32[]{:S(2)}) collective-permute-start(bf16[256,1024]{1,0:T(8,128)(2,1)S(1)} %get-tuple-element.147), channel_id=1, source_target_pairs={{8,0},{9,1},{10,2},{11,3},{12,4},{13,5},{14,6},{15,7},{16,8},{17,9... | collective-permute-start | bytes 1572872 | tf_op jit(solution)/shard_map/ppermute | solution.py:311
  63.4 11.7 %collective-permute-start.20 = (bf16[128,1024]{1,0:T(8,128)(2,1)S(1)}, bf16[128,1024]{1,0:T(8,128)(2,1)S(1)}, u32[]{:S(2)}, u32[]{:S(2)}) collective-permute-start(bf16[128,1024]{1,0:T(8,128)(2,1)S(1)} %get-tuple-element.148), channel_id=1, source_target_pairs={{8,2},{9,3},{10,4},{11,5},{12,6},{13,7},{14,0},{15,1},{16,17},{17,... | collective-permute-start | bytes 786440 | tf_op jit(solution)/shard_map/ppermute | solution.py:311
  72.4 6.5 %collective-permute-start.18 = (bf16[128,1024]{1,0:T(8,128)(2,1)S(1)}, bf16[128,1024]{1,0:T(8,128)(2,1)S(1)}, u32[]{:S(2)}, u32[]{:S(2)}) collective-permute-start(bf16[128,1024]{1,0:T(8,128)(2,1)S(1)} %get-tuple-element.144), channel_id=1, source_target_pairs={{24,19},{25,18},{26,21},{27,20},{28,23},{29,22},{30,17},{31,16}} | collective-permute-start | bytes 786440 | tf_op jit(solution)/shard_map/ppermute | solution.py:311
  73.7 6.1 %collective-permute-start.21 = (bf16[128,1024]{1,0:T(8,128)(2,1)S(1)}, bf16[128,1024]{1,0:T(8,128)(2,1)S(1)}, u32[]{:S(2)}, u32[]{:S(2)}) collective-permute-start(bf16[128,1024]{1,0:T(8,128)(2,1)S(1)} %get-tuple-element.152), channel_id=1, source_target_pairs={{24,18},{25,19},{26,20},{27,21},{28,22},{29,23},{30,16},{31,17}} | collective-permute-start | bytes 786440 | tf_op jit(solution)/shard_map/ppermute | solution.py:311
  76.3 5.0 %collective-permute-start.22 = (bf16[128,1024]{1,0:T(8,128)(2,1)S(1)}, bf16[128,1024]{1,0:T(8,128)(2,1)S(1)}, u32[]{:S(2)}, u32[]{:S(2)}) collective-permute-start(bf16[128,1024]{1,0:T(8,128)(2,1)S(1)} %get-tuple-element.155), channel_id=1, source_target_pairs={{24,17},{25,16},{26,19},{27,18},{28,21},{29,20},{30,23},{31,22}} | collective-permute-start | bytes 786440 | tf_op jit(solution)/shard_map/ppermute | solution.py:311
  77.6 3.7 %collective-permute-start.23 = (bf16[256,1024]{1,0:T(8,128)(2,1)S(1)}, bf16[256,1024]{1,0:T(8,128)(2,1)S(1)}, u32[]{:S(2)}, u32[]{:S(2)}) collective-permute-start(bf16[256,1024]{1,0:T(8,128)(2,1)S(1)} %get-tuple-element.159), channel_id=1, source_target_pairs={{24,16},{25,17},{26,18},{27,19},{28,20},{29,21},{30,22},{31,23}} | collective-permute-start | bytes 1572872 | tf_op jit(solution)/shard_map/ppermute | solution.py:311
  81.2 4.3 %collective-permute-start.24 = (bf16[256,1024]{1,0:T(8,128)(2,1)S(1)}, bf16[256,1024]{1,0:T(8,128)(2,1)S(1)}, u32[]{:S(2)}, u32[]{:S(2)}) collective-permute-start(bf16[256,1024]{1,0:T(8,128)(2,1)S(1)} %get-tuple-element.160), channel_id=1, source_target_pairs={{16,24},{17,25},{18,26},{19,27},{20,28},{21,29},{22,30},{23,31}} | collective-permute-start | bytes 1572872 | tf_op jit(solution)/shard_map/ppermute | solution.py:311
  (7 other events, 13.3 us)

commit v9 on v8

--- a/solution.py
+++ b/solution.py
@@ -109,7 +109,7 @@
                 q, k[:, lanes], (((1,), (1,)), ((), ())), preferred_element_type=jnp.float32
             )
             highest = jnp.max(scores, axis=1, keepdims=True)
-            weights.append(jnp.exp((scores - highest) * inv_root).astype(jnp.bfloat16))
+            weights.append(jnp.exp2((scores - highest) * (inv_root * math.log2(math.e))).astype(jnp.bfloat16))
         for lanes, weight_of_head in zip(heads, weights):
             values = jnp.concatenate([v[:, lanes], ones], axis=1)
             attended = jnp.dot(weight_of_head, values, preferred_element_type=jnp.float32)

time: 87 us -> 86.9 us (level)
  no operation moved by 1% of the time
where the time goes in v9:
time: 86.9 us; the launch traced here: 86.3 us
  waiting for transfers between devices  48.3 us (56%)
  starting transfers between devices  24.6 us (28%)
  local copies, waits for them, and re-layouts  7.38 us (8%)
  Pallas kernels  5.51 us (6%)
    ppermute x25, waiting for transfers between devices, send_all(): return lax.ppermute(value, AXES, pairs)  48.3 us
    ppermute x25, starting transfers between devices, send_all(): return lax.ppermute(value, AXES, pairs)  24.6 us
    unnamed x12, local copies, waits for them, and re-layouts  7.38 us
    pallas_call x8, Pallas kernels, attend(): pl.pallas_call(functools.partial(attend_kernel, section, pieces, len(bloc...  2.64 us
    pallas_call x8, Pallas kernels, project(): pl.pallas_call(functools.partial(project_kernel, section, chunk_order, co...  1.99 us
  transfers between devices with their start and end apart: 25, of which 7 were waited for; matrix products, arithmetic and copies ran while one was open for 0% of the time, Pallas kernels for 5%

profile of v9, /device:TPU:5, one launch (start us, length us, event | category | flops | bytes accessed | tf_op | source)
XLA Modules:
  0.0 86.3 jit_solution(123835068264315269)
XLA Ops:
  0.7 2.2 %copy-done = bf16[1,2048,1024]{2,1,0:T(8,128)(2,1)S(1)} copy-done((bf16[1,2048,1024]{2,1,0:T(8,128)(2,1)S(1)}, bf16[1,2048,1024]{2,1,0:T(8,128)(2,1)}, u32[]{:S(2)}) %copy-start) | copy-done | bytes 4194328
  3.6 1.0 %copy-done.5 = bf16[4,32,2048]{2,1,0:T(8,128)(2,1)S(1)} copy-done((bf16[4,32,2048]{2,1,0:T(8,128)(2,1)S(1)}, bf16[4,32,2048]{2,1,0:T(8,128)(2,1)}, u32[]{:S(2)}) %copy-start.5) | copy-done | bytes 524312
  4.6 2.2 %copy-done.1 = bf16[1,2048,1024]{2,1,0:T(8,128)(2,1)S(1)} copy-done((bf16[1,2048,1024]{2,1,0:T(8,128)(2,1)S(1)}, bf16[1,2048,1024]{2,1,0:T(8,128)(2,1)}, u32[]{:S(2)}) %copy-start.1) | copy-done | bytes 4194328
  6.8 1.3 %copy-done.2 = bf16[1,1024,2048]{2,1,0:T(8,128)(2,1)S(1)} copy-done((bf16[1,1024,2048]{2,1,0:T(8,128)(2,1)S(1)}, bf16[1,1024,2048]{2,1,0:T(8,128)(2,1)}, u32[]{:S(2)}) %copy-start.2) | copy-done | bytes 4194328
  11.2 1.3 %collective-permute-start.11 = (bf16[128,2048]{1,0:T(8,128)(2,1)S(1)}, bf16[128,2048]{1,0:T(8,128)(2,1)S(1)}, u32[]{:S(2)}, u32[]{:S(2)}) collective-permute-start(bf16[128,2048]{1,0:T(8,128)(2,1)S(1)} %get-tuple-element.118), channel_id=1, source_target_pairs={{8,26},{9,27},{10,28},{11,29},{12,30},{13,31},{14,24},{15,25}} | collective-permute-start | bytes 1572872 | tf_op jit(solution)/shard_map/ppermute | solution.py:311
  16.0 25.8 %collective-permute-done.11.refs_0_ = bf16[128,2048]{1,0:T(8,128)(2,1)S(1)} collective-permute-done((bf16[128,2048]{1,0:T(8,128)(2,1)S(1)}, bf16[128,2048]{1,0:T(8,128)(2,1)S(1)}, u32[]{:S(2)}, u32[]{:S(2)}) %collective-permute-start.11) | collective-permute-done | bytes 524320 | tf_op jit(solution)/shard_map/ppermute | solution.py:311
  41.8 1.3 %collective-permute-start.13 = (bf16[128,2048]{1,0:T(8,128)(2,1)S(1)}, bf16[128,2048]{1,0:T(8,128)(2,1)S(1)}, u32[]{:S(2)}, u32[]{:S(2)}) collective-permute-start(bf16[128,2048]{1,0:T(8,128)(2,1)S(1)} %after.4), channel_id=1, source_target_pairs={{24,17},{25,16},{26,19},{27,18},{28,21},{29,20},{30,23},{31,22}} | collective-permute-start | bytes 1572872 | tf_op jit(solution)/shard_map/ppermute | solution.py:311
  43.1 1.3 %collective-permute-start.12 = (bf16[128,2048]{1,0:T(8,128)(2,1)S(1)}, bf16[128,2048]{1,0:T(8,128)(2,1)S(1)}, u32[]{:S(2)}, u32[]{:S(2)}) collective-permute-start(bf16[128,2048]{1,0:T(8,128)(2,1)S(1)} %after.4), channel_id=1, source_target_pairs={{24,16},{25,17},{26,18},{27,19},{28,20},{29,21},{30,22},{31,23}} | collective-permute-start | bytes 1572872 | tf_op jit(solution)/shard_map/ppermute | solution.py:311
  45.2 4.0 %collective-permute-done.13.refs_1_ = bf16[128,2048]{1,0:T(8,128)(2,1)S(1)} collective-permute-done((bf16[128,2048]{1,0:T(8,128)(2,1)S(1)}, bf16[128,2048]{1,0:T(8,128)(2,1)S(1)}, u32[]{:S(2)}, u32[]{:S(2)}) %collective-permute-start.13) | collective-permute-done | bytes 524320 | tf_op jit(solution)/shard_map/ppermute | solution.py:311
  49.2 1.3 %collective-permute-start.15 = (bf16[128,2048]{1,0:T(8,128)(2,1)S(1)}, bf16[128,2048]{1,0:T(8,128)(2,1)S(1)}, u32[]{:S(2)}, u32[]{:S(2)}) collective-permute-start(bf16[128,2048]{1,0:T(8,128)(2,1)S(1)} %get-tuple-element.132.share), channel_id=1, source_target_pairs={{16,31},{17,30},{18,25},{19,24},{20,27},{21,26},{22,29},{23,28}} | collective-permute-start | bytes 1572872 | tf_op jit(solution)/shard_map/ppermute | solution.py:311
  50.5 1.3 %collective-permute-start.14 = (bf16[128,2048]{1,0:T(8,128)(2,1)S(1)}, bf16[128,2048]{1,0:T(8,128)(2,1)S(1)}, u32[]{:S(2)}, u32[]{:S(2)}) collective-permute-start(bf16[128,2048]{1,0:T(8,128)(2,1)S(1)} %get-tuple-element.132.share), channel_id=1, source_target_pairs={{16,30},{17,31},{18,24},{19,25},{20,26},{21,27},{22,28},{23,29}} | collective-permute-start | bytes 1572872 | tf_op jit(solution)/shard_map/ppermute | solution.py:311
  52.0 1.3 %collective-permute-start.17 = (bf16[128,2048]{1,0:T(8,128)(2,1)S(1)}, bf16[128,2048]{1,0:T(8,128)(2,1)S(1)}, u32[]{:S(2)}, u32[]{:S(2)}) collective-permute-start(bf16[128,2048]{1,0:T(8,128)(2,1)S(1)} %get-tuple-element.134), channel_id=1, source_target_pairs={{16,25},{17,24},{18,27},{19,26},{20,29},{21,28},{22,31},{23,30}} | collective-permute-start | bytes 1572872 | tf_op jit(solution)/shard_map/ppermute | solution.py:311
  53.3 1.3 %collective-permute-start.16 = (bf16[128,2048]{1,0:T(8,128)(2,1)S(1)}, bf16[128,2048]{1,0:T(8,128)(2,1)S(1)}, u32[]{:S(2)}, u32[]{:S(2)}) collective-permute-start(bf16[128,2048]{1,0:T(8,128)(2,1)S(1)} %get-tuple-element.134), channel_id=1, source_target_pairs={{16,24},{17,25},{18,26},{19,27},{20,28},{21,29},{22,30},{23,31}} | collective-permute-start | bytes 1572872 | tf_op jit(solution)/shard_map/ppermute | solution.py:311
  55.3 8.0 %collective-permute-done.15.refs_1_ = bf16[128,2048]{1,0:T(8,128)(2,1)S(1)} collective-permute-done((bf16[128,2048]{1,0:T(8,128)(2,1)S(1)}, bf16[128,2048]{1,0:T(8,128)(2,1)S(1)}, u32[]{:S(2)}, u32[]{:S(2)}) %collective-permute-start.15) | collective-permute-done | bytes 524320 | tf_op jit(solution)/shard_map/ppermute | solution.py:311
  64.0 5.2 %collective-permute-done.14.refs_0_ = bf16[128,2048]{1,0:T(8,128)(2,1)S(1)} collective-permute-done((bf16[128,2048]{1,0:T(8,128)(2,1)S(1)}, bf16[128,2048]{1,0:T(8,128)(2,1)S(1)}, u32[]{:S(2)}, u32[]{:S(2)}) %collective-permute-start.14) | collective-permute-done | bytes 524320 | tf_op jit(solution)/shard_map/ppermute | solution.py:311
  71.1 1.2 %attend.14 = (bf16[128,1024]{1,0:T(8,128)(2,1)S(1)}, bf16[128,1024]{1,0:T(8,128)(2,1)S(1)}, f32[8,128]{1,0:T(8,128)S(1)}) custom-call(f32[8,128]{1,0:T(8,128)S(1)} %get-tuple-element.137.mark, bf16[256,1024]{1,0:T(8,128)(2,1)S(1)} %get-tuple-element.138.k, bf16[256,1024]{1,0:T(8,128)(2,1)S(1)} %get-tuple-element.139.v, ...), custom_call_target="tpu_custom_call" | custom-call | flops 671088640 | bytes 4194304 | tf_op jit(solution)/shard_map/attend/pallas_call | solution.py:178
  72.3 1.3 %collective-permute-start.18 = (bf16[128,1024]{1,0:T(8,128)(2,1)S(1)}, bf16[128,1024]{1,0:T(8,128)(2,1)S(1)}, u32[]{:S(2)}, u32[]{:S(2)}) collective-permute-start(bf16[128,1024]{1,0:T(8,128)(2,1)S(1)} %get-tuple-element.144), channel_id=1, source_target_pairs={{24,19},{25,18},{26,21},{27,20},{28,23},{29,22},{30,17},{31,16}} | collective-permute-start | bytes 786440 | tf_op jit(solution)/shard_map/ppermute | solution.py:311
  73.7 1.3 %collective-permute-start.21 = (bf16[128,1024]{1,0:T(8,128)(2,1)S(1)}, bf16[128,1024]{1,0:T(8,128)(2,1)S(1)}, u32[]{:S(2)}, u32[]{:S(2)}) collective-permute-start(bf16[128,1024]{1,0:T(8,128)(2,1)S(1)} %get-tuple-element.152), channel_id=1, source_target_pairs={{24,18},{25,19},{26,20},{27,21},{28,22},{29,23},{30,16},{31,17}} | collective-permute-start | bytes 786440 | tf_op jit(solution)/shard_map/ppermute | solution.py:311
  75.0 1.2 %attend.15 = (bf16[256,1024]{1,0:T(8,128)(2,1)S(1)}, bf16[128,1024]{1,0:T(8,128)(2,1)S(1)}, f32[8,128]{1,0:T(8,128)S(1)}) custom-call(f32[8,128]{1,0:T(8,128)S(1)} %after.6.mark, bf16[256,1024]{1,0:T(8,128)(2,1)S(1)} %get-tuple-element.138.k, bf16[256,1024]{1,0:T(8,128)(2,1)S(1)} %get-tuple-element.139.v, bf16[128,2048]{1,0:T(8,128)(2,1)S(1)} %get-tuple-element.140.refs_0_, ...), custom_call_target="tpu_custom_call" | custom-call | flops 671088640 | bytes 4194304 | tf_op jit(solution)/shard_map/attend/pallas_call | solution.py:178
  76.2 1.3 %collective-permute-start.22 = (bf16[128,1024]{1,0:T(8,128)(2,1)S(1)}, bf16[128,1024]{1,0:T(8,128)(2,1)S(1)}, u32[]{:S(2)}, u32[]{:S(2)}) collective-permute-start(bf16[128,1024]{1,0:T(8,128)(2,1)S(1)} %get-tuple-element.155), channel_id=1, source_target_pairs={{24,17},{25,16},{26,19},{27,18},{28,21},{29,20},{30,23},{31,22}} | collective-permute-start | bytes 786440 | tf_op jit(solution)/shard_map/ppermute | solution.py:311
  77.5 1.3 %collective-permute-start.23 = (bf16[256,1024]{1,0:T(8,128)(2,1)S(1)}, bf16[256,1024]{1,0:T(8,128)(2,1)S(1)}, u32[]{:S(2)}, u32[]{:S(2)}) collective-permute-start(bf16[256,1024]{1,0:T(8,128)(2,1)S(1)} %get-tuple-element.159), channel_id=1, source_target_pairs={{24,16},{25,17},{26,18},{27,19},{28,20},{29,21},{30,22},{31,23}} | collective-permute-start | bytes 1572872 | tf_op jit(solution)/shard_map/ppermute | solution.py:311
  79.7 1.4 %collective-permute-done.22.refs_0_ = bf16[128,1024]{1,0:T(8,128)(2,1)S(1)} collective-permute-done((bf16[128,1024]{1,0:T(8,128)(2,1)S(1)}, bf16[128,1024]{1,0:T(8,128)(2,1)S(1)}, u32[]{:S(2)}, u32[]{:S(2)}) %collective-permute-start.22) | collective-permute-done | bytes 262176 | tf_op jit(solution)/shard_map/ppermute | solution.py:311
  81.1 1.3 %collective-permute-start.24 = (bf16[256,1024]{1,0:T(8,128)(2,1)S(1)}, bf16[256,1024]{1,0:T(8,128)(2,1)S(1)}, u32[]{:S(2)}, u32[]{:S(2)}) collective-permute-start(bf16[256,1024]{1,0:T(8,128)(2,1)S(1)} %get-tuple-element.160), channel_id=1, source_target_pairs={{16,24},{17,25},{18,26},{19,27},{20,28},{21,29},{22,30},{23,31}} | collective-permute-start | bytes 1572872 | tf_op jit(solution)/shard_map/ppermute | solution.py:311
  82.4 3.0 %collective-permute-done.24.total = bf16[256,1024]{1,0:T(8,128)(2,1)S(1)} collective-permute-done((bf16[256,1024]{1,0:T(8,128)(2,1)S(1)}, bf16[256,1024]{1,0:T(8,128)(2,1)S(1)}, u32[]{:S(2)}, u32[]{:S(2)}) %collective-permute-start.24) | collective-permute-done | bytes 524320 | tf_op jit(solution)/shard_map/ppermute | solution.py:311
  (65 shorter events, 13.8 us)
Async XLA Ops:
  0.0 4.6 %collective-permute-start = (bf16[128,2048]{1,0:T(8,128)(2,1)}, bf16[128,2048]{1,0:T(8,128)(2,1)S(1)}, u32[]{:S(2)}, u32[]{:S(2)}) collective-permute-start(bf16[128,2048]{1,0:T(8,128)(2,1)} %bitcast.20), channel_id=1, source_target_pairs={{0,1},{1,0},{2,3},{3,2},{4,5},{5,4},{6,7},{7,6}} | collective-permute-start | bytes 1572872 | tf_op jit(solution)/shard_map/ppermute | solution.py:311
  8.1 3.0 %collective-permute-start.2 = (bf16[128,2048]{1,0:T(8,128)(2,1)S(1)}, bf16[128,2048]{1,0:T(8,128)(2,1)S(1)}, u32[]{:S(2)}, u32[]{:S(2)}) collective-permute-start(bf16[128,2048]{1,0:T(8,128)(2,1)S(1)} %get-tuple-element.95), channel_id=1, source_target_pairs={{0,15},{1,14},{2,9},{3,8},{4,11},{5,10},{6,13},{7,12}} | collective-permute-start | bytes 1572872 | tf_op jit(solution)/shard_map/ppermute | solution.py:311
  8.9 2.1 %collective-permute-start.1 = (bf16[128,2048]{1,0:T(8,128)(2,1)S(1)}, bf16[128,2048]{1,0:T(8,128)(2,1)S(1)}, u32[]{:S(2)}, u32[]{:S(2)}) collective-permute-start(bf16[128,2048]{1,0:T(8,128)(2,1)S(1)} %get-tuple-element.95), channel_id=1, source_target_pairs={{0,14},{1,15},{2,8},{3,9},{4,10},{5,11},{6,12},{7,13}} | collective-permute-start | bytes 1572872 | tf_op jit(solution)/shard_map/ppermute | solution.py:311
  9.7 1.5 %collective-permute-start.4 = (bf16[128,2048]{1,0:T(8,128)(2,1)S(1)}, bf16[128,2048]{1,0:T(8,128)(2,1)S(1)}, u32[]{:S(2)}, u32[]{:S(2)}) collective-permute-start(bf16[128,2048]{1,0:T(8,128)(2,1)S(1)} %get-tuple-element.97), channel_id=1, source_target_pairs={{0,9},{1,8},{2,11},{3,10},{4,13},{5,12},{6,15},{7,14}} | collective-permute-start | bytes 1572872 | tf_op jit(solution)/shard_map/ppermute | solution.py:311
  10.4 0.8 collective-permute-start.3
  11.2 30.6 %collective-permute-start.11 = (bf16[128,2048]{1,0:T(8,128)(2,1)S(1)}, bf16[128,2048]{1,0:T(8,128)(2,1)S(1)}, u32[]{:S(2)}, u32[]{:S(2)}) collective-permute-start(bf16[128,2048]{1,0:T(8,128)(2,1)S(1)} %get-tuple-element.118), channel_id=1, source_target_pairs={{8,26},{9,27},{10,28},{11,29},{12,30},{13,31},{14,24},{15,25}} | collective-permute-start | bytes 1572872 | tf_op jit(solution)/shard_map/ppermute | solution.py:311
  12.5 2.7 %collective-permute-start.6 = (bf16[128,1024]{1,0:T(8,128)(2,1)S(1)}, bf16[128,1024]{1,0:T(8,128)(2,1)S(1)}, u32[]{:S(2)}, u32[]{:S(2)}) collective-permute-start(bf16[128,1024]{1,0:T(8,128)(2,1)S(1)} %get-tuple-element.110), channel_id=1, source_target_pairs={{8,1},{9,0},{10,3},{11,2},{12,5},{13,4},{14,7},{15,6}} | collective-permute-start | bytes 786440 | tf_op jit(solution)/shard_map/ppermute | solution.py:311
  13.2 2.1 %collective-permute-start.5 = (bf16[128,1024]{1,0:T(8,128)(2,1)S(1)}, bf16[128,1024]{1,0:T(8,128)(2,1)S(1)}, u32[]{:S(2)}, u32[]{:S(2)}) collective-permute-start(bf16[128,1024]{1,0:T(8,128)(2,1)S(1)} %get-tuple-element.110), channel_id=1, source_target_pairs={{8,0},{9,1},{10,2},{11,3},{12,4},{13,5},{14,6},{15,7}} | collective-permute-start | bytes 786440 | tf_op jit(solution)/shard_map/ppermute | solution.py:311
  13.9 30.6 %collective-permute-start.8 = (bf16[128,1024]{1,0:T(8,128)(2,1)S(1)}, bf16[128,1024]{1,0:T(8,128)(2,1)S(1)}, u32[]{:S(2)}, u32[]{:S(2)}) collective-permute-start(bf16[128,1024]{1,0:T(8,128)(2,1)S(1)} %get-tuple-element.112), channel_id=1, source_target_pairs={{8,1},{9,0},{10,3},{11,2},{12,5},{13,4},{14,7},{15,6}} | collective-permute-start | bytes 786440 | tf_op jit(solution)/shard_map/ppermute | solution.py:311
  14.6 29.9 %collective-permute-start.7 = (bf16[128,1024]{1,0:T(8,128)(2,1)S(1)}, bf16[128,1024]{1,0:T(8,128)(2,1)S(1)}, u32[]{:S(2)}, u32[]{:S(2)}) collective-permute-start(bf16[128,1024]{1,0:T(8,128)(2,1)S(1)} %get-tuple-element.112), channel_id=1, source_target_pairs={{8,0},{9,1},{10,2},{11,3},{12,4},{13,5},{14,6},{15,7}} | collective-permute-start | bytes 786440 | tf_op jit(solution)/shard_map/ppermute | solution.py:311
  15.3 29.9 %collective-permute-start.9 = (bf16[128,1024]{1,0:T(8,128)(2,1)S(1)}, bf16[128,1024]{1,0:T(8,128)(2,1)S(1)}, u32[]{:S(2)}, u32[]{:S(2)}) collective-permute-start(bf16[128,1024]{1,0:T(8,128)(2,1)S(1)} %get-tuple-element.114), channel_id=1, source_target_pairs={{0,16},{1,17},{2,18},{3,19},{4,20},{5,21},{6,22},{7,23}} | collective-permute-start | bytes 786440 | tf_op jit(solution)/shard_map/ppermute | solution.py:311
  41.8 7.4 %collective-permute-start.13 = (bf16[128,2048]{1,0:T(8,128)(2,1)S(1)}, bf16[128,2048]{1,0:T(8,128)(2,1)S(1)}, u32[]{:S(2)}, u32[]{:S(2)}) collective-permute-start(bf16[128,2048]{1,0:T(8,128)(2,1)S(1)} %after.4), channel_id=1, source_target_pairs={{24,17},{25,16},{26,19},{27,18},{28,21},{29,20},{30,23},{31,22}} | collective-permute-start | bytes 1572872 | tf_op jit(solution)/shard_map/ppermute | solution.py:311
  43.1 6.1 %collective-permute-start.12 = (bf16[128,2048]{1,0:T(8,128)(2,1)S(1)}, bf16[128,2048]{1,0:T(8,128)(2,1)S(1)}, u32[]{:S(2)}, u32[]{:S(2)}) collective-permute-start(bf16[128,2048]{1,0:T(8,128)(2,1)S(1)} %after.4), channel_id=1, source_target_pairs={{24,16},{25,17},{26,18},{27,19},{28,20},{29,21},{30,22},{31,23}} | collective-permute-start | bytes 1572872 | tf_op jit(solution)/shard_map/ppermute | solution.py:311
  49.2 14.1 %collective-permute-start.15 = (bf16[128,2048]{1,0:T(8,128)(2,1)S(1)}, bf16[128,2048]{1,0:T(8,128)(2,1)S(1)}, u32[]{:S(2)}, u32[]{:S(2)}) collective-permute-start(bf16[128,2048]{1,0:T(8,128)(2,1)S(1)} %get-tuple-element.132.share), channel_id=1, source_target_pairs={{16,31},{17,30},{18,25},{19,24},{20,27},{21,26},{22,29},{23,28}} | collective-permute-start | bytes 1572872 | tf_op jit(solution)/shard_map/ppermute | solution.py:311
  50.5 18.7 %collective-permute-start.14 = (bf16[128,2048]{1,0:T(8,128)(2,1)S(1)}, bf16[128,2048]{1,0:T(8,128)(2,1)S(1)}, u32[]{:S(2)}, u32[]{:S(2)}) collective-permute-start(bf16[128,2048]{1,0:T(8,128)(2,1)S(1)} %get-tuple-element.132.share), channel_id=1, source_target_pairs={{16,30},{17,31},{18,24},{19,25},{20,26},{21,27},{22,28},{23,29}} | collective-permute-start | bytes 1572872 | tf_op jit(solution)/shard_map/ppermute | solution.py:311
  52.0 18.1 %collective-permute-start.17 = (bf16[128,2048]{1,0:T(8,128)(2,1)S(1)}, bf16[128,2048]{1,0:T(8,128)(2,1)S(1)}, u32[]{:S(2)}, u32[]{:S(2)}) collective-permute-start(bf16[128,2048]{1,0:T(8,128)(2,1)S(1)} %get-tuple-element.134), channel_id=1, source_target_pairs={{16,25},{17,24},{18,27},{19,26},{20,29},{21,28},{22,31},{23,30}} | collective-permute-start | bytes 1572872 | tf_op jit(solution)/shard_map/ppermute | solution.py:311
  53.3 16.8 %collective-permute-start.16 = (bf16[128,2048]{1,0:T(8,128)(2,1)S(1)}, bf16[128,2048]{1,0:T(8,128)(2,1)S(1)}, u32[]{:S(2)}, u32[]{:S(2)}) collective-permute-start(bf16[128,2048]{1,0:T(8,128)(2,1)S(1)} %get-tuple-element.134), channel_id=1, source_target_pairs={{16,24},{17,25},{18,26},{19,27},{20,28},{21,29},{22,30},{23,31}} | collective-permute-start | bytes 1572872 | tf_op jit(solution)/shard_map/ppermute | solution.py:311
  54.6 20.4 %collective-permute-start.19 = (bf16[256,1024]{1,0:T(8,128)(2,1)S(1)}, bf16[256,1024]{1,0:T(8,128)(2,1)S(1)}, u32[]{:S(2)}, u32[]{:S(2)}) collective-permute-start(bf16[256,1024]{1,0:T(8,128)(2,1)S(1)} %get-tuple-element.147), channel_id=1, source_target_pairs={{8,0},{9,1},{10,2},{11,3},{12,4},{13,5},{14,6},{15,7},{16,8},{17,9... | collective-permute-start | bytes 1572872 | tf_op jit(solution)/shard_map/ppermute | solution.py:311
  63.3 11.7 %collective-permute-start.20 = (bf16[128,1024]{1,0:T(8,128)(2,1)S(1)}, bf16[128,1024]{1,0:T(8,128)(2,1)S(1)}, u32[]{:S(2)}, u32[]{:S(2)}) collective-permute-start(bf16[128,1024]{1,0:T(8,128)(2,1)S(1)} %get-tuple-element.148), channel_id=1, source_target_pairs={{8,2},{9,3},{10,4},{11,5},{12,6},{13,7},{14,0},{15,1},{16,17},{17,... | collective-permute-start | bytes 786440 | tf_op jit(solution)/shard_map/ppermute | solution.py:311
  72.3 6.5 %collective-permute-start.18 = (bf16[128,1024]{1,0:T(8,128)(2,1)S(1)}, bf16[128,1024]{1,0:T(8,128)(2,1)S(1)}, u32[]{:S(2)}, u32[]{:S(2)}) collective-permute-start(bf16[128,1024]{1,0:T(8,128)(2,1)S(1)} %get-tuple-element.144), channel_id=1, source_target_pairs={{24,19},{25,18},{26,21},{27,20},{28,23},{29,22},{30,17},{31,16}} | collective-permute-start | bytes 786440 | tf_op jit(solution)/shard_map/ppermute | solution.py:311
  73.7 6.1 %collective-permute-start.21 = (bf16[128,1024]{1,0:T(8,128)(2,1)S(1)}, bf16[128,1024]{1,0:T(8,128)(2,1)S(1)}, u32[]{:S(2)}, u32[]{:S(2)}) collective-permute-start(bf16[128,1024]{1,0:T(8,128)(2,1)S(1)} %get-tuple-element.152), channel_id=1, source_target_pairs={{24,18},{25,19},{26,20},{27,21},{28,22},{29,23},{30,16},{31,17}} | collective-permute-start | bytes 786440 | tf_op jit(solution)/shard_map/ppermute | solution.py:311
  76.2 5.0 %collective-permute-start.22 = (bf16[128,1024]{1,0:T(8,128)(2,1)S(1)}, bf16[128,1024]{1,0:T(8,128)(2,1)S(1)}, u32[]{:S(2)}, u32[]{:S(2)}) collective-permute-start(bf16[128,1024]{1,0:T(8,128)(2,1)S(1)} %get-tuple-element.155), channel_id=1, source_target_pairs={{24,17},{25,16},{26,19},{27,18},{28,21},{29,20},{30,23},{31,22}} | collective-permute-start | bytes 786440 | tf_op jit(solution)/shard_map/ppermute | solution.py:311
  77.5 3.6 %collective-permute-start.23 = (bf16[256,1024]{1,0:T(8,128)(2,1)S(1)}, bf16[256,1024]{1,0:T(8,128)(2,1)S(1)}, u32[]{:S(2)}, u32[]{:S(2)}) collective-permute-start(bf16[256,1024]{1,0:T(8,128)(2,1)S(1)} %get-tuple-element.159), channel_id=1, source_target_pairs={{24,16},{25,17},{26,18},{27,19},{28,20},{29,21},{30,22},{31,23}} | collective-permute-start | bytes 1572872 | tf_op jit(solution)/shard_map/ppermute | solution.py:311
  81.1 4.3 %collective-permute-start.24 = (bf16[256,1024]{1,0:T(8,128)(2,1)S(1)}, bf16[256,1024]{1,0:T(8,128)(2,1)S(1)}, u32[]{:S(2)}, u32[]{:S(2)}) collective-permute-start(bf16[256,1024]{1,0:T(8,128)(2,1)S(1)} %get-tuple-element.160), channel_id=1, source_target_pairs={{16,24},{17,25},{18,26},{19,27},{20,28},{21,29},{22,30},{23,31}} | collective-permute-start | bytes 1572872 | tf_op jit(solution)/shard_map/ppermute | solution.py:311
  (7 other events, 13.3 us)
